TPU v7x, 256 devices: a whole 4x4x8 slice. The times are simulated.
256 devices in a mesh: section: 8 (over z), expert: 16 (over y, x), dp: 2 (over core).
Axes of the slice: x: 4, y: 4, z: 8, core: 2. Of those that a mesh axis runs over, the one named last changes fastest.
Arguments:
- stream_up: bfloat16 [8, 2048, 3584], P('section', 'expert', 'dp'), may hold values from -6 to 6
- routes_up: int32 [8, 1, 2048, 1], P('section', None, 'expert'), may hold values from 0 to 3; in each aligned block of 128 rows (0 to 127, 128 to 255, ..., all dimensions but the last counted through in order) at most 40 rows name the same one
- cotangent_down: bfloat16 [8, 2048, 3584], P('section', 'expert', 'dp'), may hold values from -6 to 6
- saved_down: bfloat16 [8, 1, 2048, 3584], P('section', None, 'expert', 'dp'), may hold values from -6 to 6
- routes_down: int32 [8, 1, 2048, 1], P('section', None, 'expert'), may hold values from 0 to 3; in each aligned block of 128 rows (0 to 127, 128 to 255, ..., all dimensions but the last counted through in order) at most 40 rows name the same one
- weight_up: bfloat16 [8, 16, 3584, 256], P('section', 'expert', 'dp'), may hold values from -0.09375 to 0.09375
- weight_down: bfloat16 [8, 16, 256, 3584], P('section', 'expert', None, 'dp'), may hold values from -0.1875 to 0.1875
Outputs:
- stream_out: bfloat16 [8, 2048, 3584], P('section', 'expert', 'dp')
- grad_out: bfloat16 [8, 2048, 3584], P('section', 'expert', 'dp')
Inputs may be any that keep to these rules, and one draw needn't show every extreme that they name: `routes_up`: in each aligned block of 128 tokens (the rows of one device) no expert is named by more than 40 tokens, a bound that some block reaches. `routes_down`: in each aligned block of 128 tokens (the rows of one device) no expert is named by more than 40 tokens, a bound that some block reaches.
All inputs are finite; a program needn't handle non-finite values.
Results may differ from a plain program's by a relative error of at most 0.014.
Values may be sent and summed in bfloat16 or wider, within the bound.
No kernel may reach another device: no remote copies, remote signals or barrier semaphores. Data moves between devices by JAX's collectives and lax.ppermute only.
A program may use at most 64 MiB of HBM per device.

v0:
```python
import jax
import jax.numpy as jnp
from jax import lax
from jax.sharding import PartitionSpec as P


def shifted(block, axis, distance):
    devices = range(lax.axis_size(axis))
    route = [((i - distance) % len(devices), i) for i in devices]
    return lax.ppermute(block, axis, route)


def silu_grad(values):
    sigma = jax.nn.sigmoid(values)
    return sigma * (1.0 + values * (1.0 - sigma))


def build_table(expert_ids, experts, capacity):
    onehot = (expert_ids[:, None] == jnp.arange(experts, dtype=jnp.int32)[None, :]).astype(
        jnp.int32
    )
    before = jnp.cumsum(onehot, axis=0) - onehot
    position = jnp.sum(before * onehot, axis=1)
    slot_index = expert_ids * capacity + position
    return (slot_index[None, :] == jnp.arange(experts * capacity, dtype=jnp.int32)[:, None]).astype(
        jnp.bfloat16
    )


def spread_rows(dispatch_table, row_data, experts, split_count, capacity):
    packed = jnp.dot(dispatch_table, row_data, preferred_element_type=jnp.float32).astype(
        jnp.bfloat16
    )
    features = row_data.shape[1]
    packed = packed.reshape(experts, 1, capacity, features)
    copies = jnp.broadcast_to(packed, (experts, split_count, capacity, features))
    return copies.reshape(experts * split_count, capacity, features)


def fold_blocks(returned, experts, split_count, capacity):
    features = returned.shape[2]
    summed = jnp.sum(
        returned.reshape(experts, split_count, capacity, features).astype(jnp.float32), axis=1
    )
    return summed.reshape(experts * capacity, features)


def collect_rows(dispatch_table, summed):
    return lax.dot_general(
        dispatch_table.astype(jnp.float32),
        summed,
        (((0,), (0,)), ((), ())),
        precision=lax.Precision.HIGHEST,
        preferred_element_type=jnp.float32,
    )


def per_device(
    stream_up, routes_up, cotangent_down, saved_down, routes_down, weight_up, weight_down
):
    devices_all = lax.axis_size("expert")
    split_count = min(4, devices_all)
    experts = devices_all // split_count
    row_count = stream_up.shape[1]
    features = stream_up.shape[2]
    capacity = min(row_count, 5 * row_count // (4 * experts))
    up_matrix = weight_up[0, 0]
    down_matrix = weight_down[0, 0]
    forward_rows = stream_up[0]
    cotangent = cotangent_down[0]
    table_up = build_table(routes_up[0, 0, :, 0], experts, capacity)
    table_down = build_table(routes_down[0, 0, :, 0], experts, capacity)
    send_forward = spread_rows(table_up, forward_rows, experts, split_count, capacity)
    send_saved = spread_rows(table_down, saved_down[0, 0], experts, split_count, capacity)
    send_grad = spread_rows(table_down, cotangent, experts, split_count, capacity)
    recv_forward = lax.all_to_all(send_forward, "expert", split_axis=0, concat_axis=0, tiled=True)
    recv_saved = lax.all_to_all(send_saved, "expert", split_axis=0, concat_axis=0, tiled=True)
    recv_grad = lax.all_to_all(send_grad, "expert", split_axis=0, concat_axis=0, tiled=True)
    recv_forward = recv_forward.reshape(devices_all * capacity, features)
    recv_saved = recv_saved.reshape(devices_all * capacity, features)
    recv_grad = recv_grad.reshape(devices_all * capacity, features)
    hidden_forward = jnp.dot(recv_forward, up_matrix, preferred_element_type=jnp.float32)
    hidden_saved = jnp.dot(recv_saved, up_matrix, preferred_element_type=jnp.float32)
    hidden_grad_in = lax.dot_general(
        recv_grad, down_matrix, (((1,), (1,)), ((), ())), preferred_element_type=jnp.float32
    )
    hidden_forward, hidden_saved, hidden_grad_in = (
        lax.psum(hidden_forward.astype(jnp.bfloat16), "dp").astype(jnp.float32),
        lax.psum(hidden_saved.astype(jnp.bfloat16), "dp").astype(jnp.float32),
        lax.psum(hidden_grad_in.astype(jnp.bfloat16), "dp").astype(jnp.float32),
    )
    activated = jax.nn.silu(hidden_forward).astype(jnp.bfloat16)
    hidden_grad = (hidden_grad_in * silu_grad(hidden_saved)).astype(jnp.bfloat16)
    expert_out = jnp.dot(activated, down_matrix, preferred_element_type=jnp.float32).astype(
        jnp.bfloat16
    )
    input_grad = lax.dot_general(
        hidden_grad, up_matrix, (((1,), (1,)), ((), ())), preferred_element_type=jnp.float32
    ).astype(jnp.bfloat16)
    back_forward = lax.all_to_all(
        expert_out.reshape(devices_all, capacity, features),
        "expert",
        split_axis=0,
        concat_axis=0,
        tiled=True,
    )
    back_grad = lax.all_to_all(
        input_grad.reshape(devices_all, capacity, features),
        "expert",
        split_axis=0,
        concat_axis=0,
        tiled=True,
    )
    summed_forward = fold_blocks(back_forward, experts, split_count, capacity)
    summed_grad = fold_blocks(back_grad, experts, split_count, capacity)
    forward_new = (
        forward_rows.astype(jnp.float32) + collect_rows(table_up, summed_forward)
    ).astype(jnp.bfloat16)
    cotangent_new = (cotangent.astype(jnp.float32) + collect_rows(table_down, summed_grad)).astype(
        jnp.bfloat16
    )
    forward_rows = shifted(forward_new, "section", 1)
    cotangent = shifted(cotangent_new, "section", -1)
    return (forward_rows[None], cotangent[None])


def solution(mesh):
    return jax.shard_map(
        per_device,
        mesh=mesh,
        in_specs=(
            P("section", "expert", "dp"),
            P("section", None, "expert", None),
            P("section", "expert", "dp"),
            P("section", None, "expert", "dp"),
            P("section", None, "expert", None),
            P("section", "expert", "dp", None),
            P("section", "expert", None, "dp"),
        ),
        out_specs=(P("section", "expert", "dp"), P("section", "expert", "dp")),
        check_vma=False,
    )
```

profile of v0, /device:TPU:1, one launch (start us, length us, event | category | flops | bytes accessed | tf_op | source)
XLA Modules:
  0.0 271.9 jit_solution(10854802495317052271)
XLA Ops:
  7.2 0.0 copy-start
  7.2 0.8 fusion.25
  8.0 0.2 reduce_window_sum.18
  8.2 0.8 select_reduce_fusion
  9.0 0.7 multiply_add_fusion
  9.7 1.3 convolution_convert_fusion.2
  11.0 1.5 broadcast_in_dim.39
  12.5 0.0 copy-start.4
  12.5 7.7 %all-to-all-start.3 = ((bf16[16,40,1792]{2,1,0:T(8,128)(2,1)}), bf16[16,40,1792]{2,1,0:T(8,128)(2,1)S(1)}, u32[]{:S(2)}, u32[]{:S(2)}) async-start(bf16[16,40,1792]{2,1,0:T(8,128)(2,1)} %bitcast.18), calls=%async_computation.3 | async-start | bytes 4587520 | tf_op jit(solution)/shard_map/all_to_all | solution.py:77
  20.3 0.0 copy-done.4
  20.3 0.1 fusion.26
  20.4 0.2 reduce_window_sum.17
  20.5 0.2 select_reduce_fusion.1
  20.7 2.2 convolution_convert_fusion.4
  22.9 31.1 %all-to-all-done.3 = bf16[16,40,1792]{2,1,0:T(8,128)(2,1)S(1)} async-done(((bf16[16,40,1792]{2,1,0:T(8,128)(2,1)}), bf16[16,40,1792]{2,1,0:T(8,128)(2,1)S(1)}, u32[]{:S(2)}, u32[]{:S(2)}) %all-to-all-start.3) | async-done | bytes 2293792 | tf_op jit(solution)/shard_map/all_to_all | solution.py:77
  53.9 2.6 broadcast_in_dim.34
  56.5 4.4 %all-to-all-start = ((bf16[16,40,1792]{2,1,0:T(8,128)(2,1)}), bf16[16,40,1792]{2,1,0:T(8,128)(2,1)}, u32[]{:S(2)}, u32[]{:S(2)}) async-start(bf16[16,40,1792]{2,1,0:T(8,128)(2,1)} %bitcast.3), calls=%async_computation | async-start | bytes 4587520 | tf_op jit(solution)/shard_map/all_to_all | solution.py:76
  60.9 2.1 convolution_convert_fusion.3
  63.1 28.6 %all-to-all-done = bf16[16,40,1792]{2,1,0:T(8,128)(2,1)} async-done(((bf16[16,40,1792]{2,1,0:T(8,128)(2,1)}), bf16[16,40,1792]{2,1,0:T(8,128)(2,1)}, u32[]{:S(2)}, u32[]{:S(2)}) %all-to-all-start) | async-done | bytes 2293792 | tf_op jit(solution)/shard_map/all_to_all | solution.py:76
  91.7 2.6 broadcast_in_dim.37
  94.4 5.8 %all-to-all-start.2 = ((bf16[16,40,1792]{2,1,0:T(8,128)(2,1)}), bf16[16,40,1792]{2,1,0:T(8,128)(2,1)}, u32[]{:S(2)}, u32[]{:S(2)}) async-start(bf16[16,40,1792]{2,1,0:T(8,128)(2,1)} %bitcast.14), calls=%async_computation.2 | async-start | bytes 4587520 | tf_op jit(solution)/shard_map/all_to_all | solution.py:78
  100.1 0.0 all-reduce.3.cloned.1.call-start
  100.2 0.0 copy-done
  100.2 1.5 convolution_convert_fusion.5
  101.7 0.0 copy-start.5
  101.7 3.2 %convolution_convert_fusion.7 = bf16[640,256]{1,0:T(8,128)(2,1)} fusion(bf16[640,1792]{1,0:T(8,128)(2,1)} %bitcast.4, bf16[1,1,1792,256]{3,2,1,0:T(8,128)(2,1)S(1)} %copy-done), kind=kOutput, calls=%fused_computation.13 | convolution fusion | flops 587366400 | bytes 3538944 | tf_op jit(solution)/shard_map/dot_general | solution.py:82
  104.9 25.4 %all-to-all-done.2 = bf16[16,40,1792]{2,1,0:T(8,128)(2,1)} async-done(((bf16[16,40,1792]{2,1,0:T(8,128)(2,1)}), bf16[16,40,1792]{2,1,0:T(8,128)(2,1)}, u32[]{:S(2)}, u32[]{:S(2)}) %all-to-all-start.2) | async-done | bytes 2293792 | tf_op jit(solution)/shard_map/all_to_all | solution.py:78
  130.3 0.0 copy-done.5
  130.3 3.2 %convolution_convert_fusion.6 = bf16[640,256]{1,0:T(8,128)(2,1)} fusion(bf16[640,1792]{1,0:T(8,128)(2,1)} %bitcast.15, bf16[1,1,256,1792]{3,2,1,0:T(8,128)(2,1)S(1)} %copy-done.5), kind=kOutput, calls=%fused_computation.12 | convolution fusion | flops 587366400 | bytes 3538944 | tf_op jit(solution)/shard_map/dot_general | solution.py:84
  133.5 0.0 all-reduce.3.cloned.1.call-update
  133.5 33.6 %all-reduce.3.cloned.1.call-done = (bf16[640,256]{1,0:T(8,128)(2,1)}, bf16[640,256]{1,0:T(8,128)(2,1)}, bf16[640,256]{1,0:T(8,128)(2,1)}) async-done(((bf16[640,256]{1,0:T(8,128)(2,1)}, bf16[640,256]{1,0:T(8,128)(2,1)}, bf16[640,256]{1,0:T(8,128)(2,1)}), (bf16[640,256]{1,0:T(8,128)(2,1)}, bf16[640,256]{1,0:T(8,128)(2,1)}, bf16[640,256]{1,0:T(8,128)(2,1)})) %all-reduce.3.cloned.1.call-update) | async-done | bytes 983056 | tf_op jit(solution)/shard_map/psum | solution.py:88
  167.1 3.4 %convolution_convert_fusion = bf16[640,1792]{1,0:T(8,128)(2,1)} fusion(bf16[1,1,1792,256]{3,2,1,0:T(8,128)(2,1)S(1)} %copy-done, bf16[640,256]{1,0:T(8,128)(2,1)} %get-tuple-element.3, bf16[640,256]{1,0:T(8,128)(2,1)} %get-tuple-element.4), kind=kOutput, calls=%fused_computation.2 | convolution fusion | flops 590151680 | bytes 3866624 | tf_op jit(solution)/shard_map/dot_general | solution.py:97
  170.5 6.3 %all-to-all-start.4 = ((bf16[16,40,1792]{2,1,0:T(8,128)(2,1)}), bf16[16,40,1792]{2,1,0:T(8,128)(2,1)S(1)}, u32[]{:S(2)}, u32[]{:S(2)}) async-start(bf16[16,40,1792]{2,1,0:T(8,128)(2,1)} %bitcast.57), calls=%async_computation.4 | async-start | bytes 4587520 | tf_op jit(solution)/shard_map/all_to_all | solution.py:107
  176.7 3.5 %convolution_convert_fusion.1 = bf16[640,1792]{1,0:T(8,128)(2,1)} fusion(bf16[1,1,256,1792]{3,2,1,0:T(8,128)(2,1)} %param.13, bf16[640,256]{1,0:T(8,128)(2,1)} %get-tuple-element.2), kind=kOutput, calls=%fused_computation.3 | convolution fusion | flops 589332480 | bytes 3538944 | tf_op jit(solution)/shard_map/dot_general | solution.py:94
  180.3 31.9 %all-to-all-done.4 = bf16[16,40,1792]{2,1,0:T(8,128)(2,1)S(1)} async-done(((bf16[16,40,1792]{2,1,0:T(8,128)(2,1)}), bf16[16,40,1792]{2,1,0:T(8,128)(2,1)S(1)}, u32[]{:S(2)}, u32[]{:S(2)}) %all-to-all-start.4) | async-done | bytes 2293792 | tf_op jit(solution)/shard_map/all_to_all | solution.py:107
  212.2 0.0 copy-start.1
  212.2 1.4 copy-done.1
  213.5 3.7 %all-to-all-start.1 = ((bf16[16,40,1792]{2,1,0:T(8,128)(2,1)}), bf16[16,40,1792]{2,1,0:T(8,128)(2,1)S(1)}, u32[]{:S(2)}, u32[]{:S(2)}) async-start(bf16[16,40,1792]{2,1,0:T(8,128)(2,1)} %bitcast.56), calls=%async_computation.1 | async-start | bytes 4587520 | tf_op jit(solution)/shard_map/all_to_all | solution.py:100
  217.3 0.0 copy-start.2
  217.3 2.2 convert_reduce_fusion
  219.5 0.0 copy-done.2
  219.5 1.5 fusion.1
  220.9 3.0 %collective-permute-start.1 = (bf16[128,1792]{1,0:T(8,128)(2,1)}, bf16[128,1792]{1,0:T(8,128)(2,1)}, u32[]{:S(2)}, u32[]{:S(2)}) collective-permute-start(bf16[128,1792]{1,0:T(8,128)(2,1)} %fusion.1), channel_id=1, source_target_pairs={{32,0},{64,32},{96,64},{128,96},{160,128},{192,160},{224,192},{0,2... | collective-permute-start | bytes 1376264 | tf_op jit(solution)/shard_map/ppermute | solution.py:10
  224.0 25.4 %all-to-all-done.1 = bf16[16,40,1792]{2,1,0:T(8,128)(2,1)S(1)} async-done(((bf16[16,40,1792]{2,1,0:T(8,128)(2,1)}), bf16[16,40,1792]{2,1,0:T(8,128)(2,1)S(1)}, u32[]{:S(2)}, u32[]{:S(2)}) %all-to-all-start.1) | async-done | bytes 2293792 | tf_op jit(solution)/shard_map/all_to_all | solution.py:100
  249.4 0.0 copy-start.3
  249.4 0.3 convert_reduce_fusion.1
  249.7 0.7 copy-done.3
  250.4 0.7 fusion
  251.1 1.4 collective-permute-start
  252.4 0.0 collective-permute-done.1
  252.4 10.0 %collective-permute-done = bf16[128,1792]{1,0:T(8,128)(2,1)S(1)} collective-permute-done((bf16[128,1792]{1,0:T(8,128)(2,1)S(1)}, bf16[128,1792]{1,0:T(8,128)(2,1)S(1)}, u32[]{:S(2)}, u32[]{:S(2)}) %collective-permute-start) | collective-permute-done | bytes 458784 | tf_op jit(solution)/shard_map/ppermute | solution.py:10
  262.5 0.8 copy.14
  263.2 1.8 copy.15
  (1 shorter events, 0.0 us)
Async XLA Ops:
  7.2 93.0 %copy-start = (bf16[1,1,1792,256]{3,2,1,0:T(8,128)(2,1)S(1)}, bf16[1,1,1792,256]{3,2,1,0:T(8,128)(2,1)}, u32[]{:S(2)}) copy-start(bf16[1,1,1792,256]{3,2,1,0:T(8,128)(2,1)} %param.12) | copy-start | bytes 2752516
  12.5 7.7 %copy-start.4 = (s32[1,1,128,1]{2,3,1,0:T(1,128)S(1)}, s32[1,1,128,1]{2,3,1,0:T(1,128)}, u32[]{:S(2)}) copy-start(s32[1,1,128,1]{2,3,1,0:T(1,128)} %param.8) | copy-start | bytes 1540
  12.5 41.4 %all-to-all-start.3 = ((bf16[16,40,1792]{2,1,0:T(8,128)(2,1)}), bf16[16,40,1792]{2,1,0:T(8,128)(2,1)S(1)}, u32[]{:S(2)}, u32[]{:S(2)}) async-start(bf16[16,40,1792]{2,1,0:T(8,128)(2,1)} %bitcast.18), calls=%async_computation.3 | async-start | bytes 4587520 | tf_op jit(solution)/shard_map/all_to_all | solution.py:77
  56.5 35.2 %all-to-all-start = ((bf16[16,40,1792]{2,1,0:T(8,128)(2,1)}), bf16[16,40,1792]{2,1,0:T(8,128)(2,1)}, u32[]{:S(2)}, u32[]{:S(2)}) async-start(bf16[16,40,1792]{2,1,0:T(8,128)(2,1)} %bitcast.3), calls=%async_computation | async-start | bytes 4587520 | tf_op jit(solution)/shard_map/all_to_all | solution.py:76
  94.4 35.9 %all-to-all-start.2 = ((bf16[16,40,1792]{2,1,0:T(8,128)(2,1)}), bf16[16,40,1792]{2,1,0:T(8,128)(2,1)}, u32[]{:S(2)}, u32[]{:S(2)}) async-start(bf16[16,40,1792]{2,1,0:T(8,128)(2,1)} %bitcast.14), calls=%async_computation.2 | async-start | bytes 4587520 | tf_op jit(solution)/shard_map/all_to_all | solution.py:78
  100.1 67.0 %all-reduce.3.cloned.1.call-start = ((), (), s32[]{:S(2)}) async-start(), calls=%async_computation.5 | async-start | bytes 1966080 | tf_op jit(solution)/shard_map/psum | solution.py:88
  101.7 28.6 %copy-start.5 = (bf16[1,1,256,1792]{3,2,1,0:T(8,128)(2,1)S(1)}, bf16[1,1,256,1792]{3,2,1,0:T(8,128)(2,1)}, u32[]{:S(2)}) copy-start(bf16[1,1,256,1792]{3,2,1,0:T(8,128)(2,1)} %param.13) | copy-start | bytes 2752516
  170.5 41.7 %all-to-all-start.4 = ((bf16[16,40,1792]{2,1,0:T(8,128)(2,1)}), bf16[16,40,1792]{2,1,0:T(8,128)(2,1)S(1)}, u32[]{:S(2)}, u32[]{:S(2)}) async-start(bf16[16,40,1792]{2,1,0:T(8,128)(2,1)} %bitcast.57), calls=%async_computation.4 | async-start | bytes 4587520 | tf_op jit(solution)/shard_map/all_to_all | solution.py:107
  212.2 1.4 copy-start.1
  213.5 35.8 %all-to-all-start.1 = ((bf16[16,40,1792]{2,1,0:T(8,128)(2,1)}), bf16[16,40,1792]{2,1,0:T(8,128)(2,1)S(1)}, u32[]{:S(2)}, u32[]{:S(2)}) async-start(bf16[16,40,1792]{2,1,0:T(8,128)(2,1)} %bitcast.56), calls=%async_computation.1 | async-start | bytes 4587520 | tf_op jit(solution)/shard_map/all_to_all | solution.py:100
  217.3 2.2 copy-start.2
  220.9 31.5 %collective-permute-start.1 = (bf16[128,1792]{1,0:T(8,128)(2,1)}, bf16[128,1792]{1,0:T(8,128)(2,1)}, u32[]{:S(2)}, u32[]{:S(2)}) collective-permute-start(bf16[128,1792]{1,0:T(8,128)(2,1)} %fusion.1), channel_id=1, source_target_pairs={{32,0},{64,32},{96,64},{128,96},{160,128},{192,160},{224,192},{0,2... | collective-permute-start | bytes 1376264 | tf_op jit(solution)/shard_map/ppermute | solution.py:10
  249.4 1.0 copy-start.3
  251.1 11.4 %collective-permute-start = (bf16[128,1792]{1,0:T(8,128)(2,1)S(1)}, bf16[128,1792]{1,0:T(8,128)(2,1)S(1)}, u32[]{:S(2)}, u32[]{:S(2)}) collective-permute-start(bf16[128,1792]{1,0:T(8,128)(2,1)S(1)} %fusion), channel_id=1, source_target_pairs={{224,0},{0,32},{32,64},{64,96},{96,128},{128,160},{160,192},{192,2... | collective-permute-start | bytes 1376264 | tf_op jit(solution)/shard_map/ppermute | solution.py:10
Sparse Core Ops, SparseCore 0:
  133.6 33.4 all-reduce.2
where the time goes:
time: 273 us; the launch traced here: 272 us
  waiting for transfers between devices  186 us (68%)
  starting transfers between devices  32.3 us (12%)
  matrix products  22.6 us (8%)
  between operations  14.2 us (5%)
  local copies, waits for them, and re-layouts  11.4 us (4%)
  other arithmetic  5.42 us (2%)
    psum x1, waiting for transfers between devices, per_device(): lax.psum(hidden_forward.astype(jnp.bfloat16), 'dp').astype(jnp.float32)  33.6 us
    all_to_all x1, waiting for transfers between devices, per_device(): lax.all_to_all(input_grad.reshape(devices_all, capacity, features), 'expe...  31.9 us
    all_to_all x1, waiting for transfers between devices, per_device(): lax.all_to_all(send_saved, 'expert', split_axis=0, concat_axis=0, tiled=T...  31.1 us
    all_to_all x1, waiting for transfers between devices, per_device(): lax.all_to_all(send_forward, 'expert', split_axis=0, concat_axis=0, tiled...  28.6 us
    all_to_all x1, waiting for transfers between devices, per_device(): lax.all_to_all(send_grad, 'expert', split_axis=0, concat_axis=0, tiled=True)  25.4 us
    all_to_all x1, waiting for transfers between devices, per_device(): lax.all_to_all(expert_out.reshape(devices_all, capacity, features), 'expe...  25.4 us
    ppermute x2, waiting for transfers between devices, shifted(): return lax.ppermute(block, axis, route)  10 us
    all_to_all x1, starting transfers between devices, per_device(): lax.all_to_all(send_saved, 'expert', split_axis=0, concat_axis=0, tiled=T...  7.72 us
  transfers between devices with their start and end apart: 8, of which 7 were waited for; matrix products, arithmetic and copies ran while one was open for 6% of the time, Pallas kernels for 0%

commit v1 on v0

v1 whole, which is shorter than its diff:
```python
import functools

import jax
import jax.numpy as jnp
from jax import lax
from jax.experimental import pallas as pl
from jax.experimental.pallas import tpu as pltpu
from jax.sharding import PartitionSpec as P

NX = 4
NY = 4
NZ = 8
CAP = 40
ROWS = 128
BF = jnp.bfloat16
F32 = jnp.float32
VM = pl.BlockSpec(memory_space=pltpu.VMEM)
SM = pl.BlockSpec(memory_space=pltpu.SMEM)
LIMIT = 24 * 1024 * 1024


def move_x(v, d):
    return lax.ppermute(
        v, "expert", [(y * NX + x, y * NX + (x + d) % NX) for y in range(NY) for x in range(NX)]
    )


def move_y(v, d):
    return lax.ppermute(
        v, "expert", [(y * NX + x, (y + d) % NY * NX + x) for y in range(NY) for x in range(NX)]
    )


def move_z(v, d):
    return lax.ppermute(v, "section", [(z, (z + d) % NZ) for z in range(NZ)])


def move_zy(v, dz, dy):
    n = NX * NY
    pairs = [
        (z * n + y * NX + x, (z + dz) % NZ * n + (y + dy) % NY * NX + x)
        for z in range(NZ)
        for y in range(NY)
        for x in range(NX)
    ]
    return lax.ppermute(v, ("section", "expert"), pairs)


def swap(v):
    return lax.ppermute(v, "dp", [(0, 1), (1, 0)])


def call(kernel, outs, flops, nbytes, in_specs, *args):
    return pl.pallas_call(
        kernel,
        out_shape=outs,
        in_specs=in_specs,
        out_specs=jax.tree.map(lambda _: VM, outs),
        compiler_params=pltpu.CompilerParams(vmem_limit_bytes=LIMIT),
        cost_estimate=pl.CostEstimate(flops=flops, bytes_accessed=nbytes, transcendentals=0),
    )(*args)


def sds(shape, dtype=BF):
    return jax.ShapeDtypeStruct(shape, dtype)


def nn(a, b):
    return jnp.dot(a, b, preferred_element_type=F32)


def nt(a, b):
    return lax.dot_general(a, b, (((1,), (1,)), ((), ())), preferred_element_type=F32)


def tn(a, b):
    return lax.dot_general(a, b, (((0,), (0,)), ((), ())), preferred_element_type=F32)


def slot_table(ids, y):
    n = ids.shape[1]
    rel = jnp.bitwise_and(ids - y + NY, NY - 1)
    onehot = (lax.broadcasted_iota(jnp.int32, (8, n), 0) == rel).astype(F32)
    earlier = lax.broadcasted_iota(jnp.int32, (n, n), 0) < lax.broadcasted_iota(
        jnp.int32, (n, n), 1
    )
    before = nn(onehot.astype(BF), earlier.astype(F32).astype(BF))
    rank = jnp.sum(before * onehot, axis=0, keepdims=True).astype(jnp.int32)
    slot = rel * CAP + rank
    table = lax.broadcasted_iota(jnp.int32, (NY * CAP, n), 0) == slot
    return table.astype(F32).astype(BF)


def columns(width, step=256):
    return [slice(c, c + step) for c in range(0, width, step)]


def dispatch_kernel(y_ref, up_ref, down_ref, fwd_ref, saved_ref, grad_ref, *outs):
    y = y_ref[0]
    table_up = slot_table(up_ref[...], y)
    table_down = slot_table(down_ref[...], y)
    for c in columns(fwd_ref.shape[1]):
        f = nn(table_up, fwd_ref[:, c])
        s = nn(table_down, saved_ref[:, c])
        g = nn(table_down, grad_ref[:, c])
        pad = jnp.zeros((ROWS - 3 * CAP, f.shape[1]), F32)
        for rel in range(NY):
            r = slice(rel * CAP, (rel + 1) * CAP)
            outs[rel][:, c] = jnp.concatenate([f[r], s[r], g[r], pad], axis=0).astype(BF)


def up_kernel(r0, r1, r2, r3, *refs):
    *weights, out = refs
    rows = jnp.concatenate([r[0 : 2 * CAP, :] for r in (r0, r1, r2, r3)], axis=0)
    for i, w in enumerate(weights):
        out[:, i * 256 : (i + 1) * 256] = nn(rows, w[...]).astype(BF)


def up_halves_kernel(r0, r1, r2, r3, wa, wb, out):
    rows = jnp.concatenate([r[0 : 2 * CAP, :] for r in (r0, r1, r2, r3)], axis=0)
    half = wa.shape[0]
    out[...] = (nn(rows[:, :half], wa[...]) + nn(rows[:, half:], wb[...])).astype(BF)


def down_kernel(r0, r1, r2, r3, *refs):
    *weights, out = refs
    rows = jnp.concatenate([r[2 * CAP : ROWS, :] for r in (r0, r1, r2, r3)], axis=0)
    at = 0
    for w in weights:
        n = w.shape[0]
        out[:, at : at + n] = nt(rows, w[...]).astype(BF)
        at += n


def pick(v, start, stride):
    return jnp.concatenate(
        [v[i * stride + start : i * stride + start + CAP, :] for i in range(NY)], axis=0
    )


def added(a_ref, b_ref):
    return a_ref[...].astype(F32) + b_ref[...].astype(F32)


def activate(pu):
    v = pick(pu, 0, 2 * CAP)
    return (v * jax.nn.sigmoid(v)).astype(BF)


def grad_hidden(pu, pv):
    v = pick(pu, CAP, 2 * CAP)
    g = pick(pv, 0, ROWS - 2 * CAP)
    q = jax.nn.sigmoid(v)
    return (g * (q * (1.0 + v * (1.0 - q)))).astype(BF)


def mid_kernel(pu, qu, pv, qv, u0, u1, u2, v0, v1, v2, acc_f, acc_b):
    su = added(pu, qu)
    act = activate(su)
    hid = grad_hidden(su, added(pv, qv))
    for c in columns(acc_f.shape[1]):
        acc_f[:, c] = sum(
            nn(act[:, i * 256 : (i + 1) * 256], v[:, c]) for i, v in enumerate((v0, v1, v2))
        )
        acc_b[:, c] = sum(
            nt(hid[:, i * 256 : (i + 1) * 256], u[c, :]) for i, u in enumerate((u0, u1, u2))
        )


def last_f_kernel(pu, qu, va, vb, acc, *outs):
    act = activate(added(pu, qu))
    half = va.shape[0]
    for c in columns(acc.shape[1]):
        t = acc[:, c] + nn(act[:, :half], va[:, c]) + nn(act[:, half:], vb[:, c])
        for i in range(NY):
            outs[i][:, c] = t[i * CAP : (i + 1) * CAP].astype(BF)


def last_b_kernel(pu, qu, pv, qv, ua, ub, acc, *outs):
    hid = grad_hidden(added(pu, qu), added(pv, qv))
    half = ua.shape[0]
    for u, base in ((ua, 0), (ub, half)):
        for c in columns(half, 128):
            o = slice(base + c.start, base + c.stop)
            t = acc[:, o] + nt(hid, u[c, :])
            for i in range(NY):
                outs[i][:, o] = t[i * CAP : (i + 1) * CAP].astype(BF)


def combine_kernel(y_ref, ids_ref, rows_ref, f0, f1, f2, f3, out):
    table = slot_table(ids_ref[...], y_ref[0])
    for c in columns(rows_ref.shape[1]):
        got = jnp.concatenate([f[:, c].astype(F32) for f in (f0, f1, f2, f3)], axis=0).astype(BF)
        out[:, c] = (rows_ref[:, c].astype(F32) + tn(table, got)).astype(BF)


def per_device(
    stream_up, routes_up, cotangent_down, saved_down, routes_down, weight_up, weight_down
):
    u_own = weight_up[0, 0]
    v_own = weight_down[0, 0]
    fwd = stream_up[0]
    cot = cotangent_down[0]
    saved = saved_down[0, 0]
    n, width = fwd.shape
    hp = u_own.shape[1]
    ids_up = routes_up.reshape(1, n)
    ids_down = routes_down.reshape(1, n)
    y = (lax.axis_index("expert") // NX).reshape(1)

    u_l, u_r = move_x(u_own, 1), move_x(u_own, -1)
    v_l, v_r = move_x(v_own, 1), move_x(v_own, -1)

    sent = call(
        dispatch_kernel,
        [sds((ROWS, width))] * NY,
        6 * 160 * 128 * width,
        7 * 128 * width * 2,
        [SM] + [VM] * 5,
        y,
        ids_up,
        ids_down,
        fwd,
        saved,
        cot,
    )
    rows = [sent[0]] + [move_y(sent[d], d) for d in range(1, NY)]

    fwd_next, ids_up_next = move_z(fwd, 1), move_z(ids_up, 1)
    cot_next, ids_down_next = move_z(cot, -1), move_z(ids_down, -1)

    u_a, u_b = move_x(u_l[: width // 2], 1), move_x(u_r[width // 2 :], -1)
    v_a, v_b = move_x(v_l[: hp // 2], 1), move_x(v_r[hp // 2 :], -1)

    mm = 2 * 320 * width * hp
    pu = call(
        up_kernel, sds((2 * CAP * NY, 3 * hp)), 3 * mm, 4 << 20, [VM] * 7, *rows, u_own, u_l, u_r
    )
    qu = swap(pu)
    pv = call(
        down_kernel,
        sds(((ROWS - 2 * CAP) * NY, 3 * hp)),
        2 * mm,
        4 << 20,
        [VM] * 7,
        *rows,
        v_own,
        v_l,
        v_r,
    )
    qv = swap(pv)
    acc_f, acc_b = call(
        mid_kernel,
        [sds((NY * CAP, width), F32)] * 2,
        3 * mm,
        8 << 20,
        [VM] * 10,
        pu,
        qu,
        pv,
        qv,
        u_own,
        u_l,
        u_r,
        v_own,
        v_l,
        v_r,
    )
    pu2 = call(up_halves_kernel, sds((2 * CAP * NY, hp)), mm, 2 << 20, [VM] * 6, *rows, u_a, u_b)
    qu2 = swap(pu2)
    pv2 = call(
        down_kernel,
        sds(((ROWS - 2 * CAP) * NY, hp)),
        mm // 2,
        2 << 20,
        [VM] * 6,
        *rows,
        v_a,
        v_b,
    )
    qv2 = swap(pv2)
    outs = [sds((CAP, width))] * NY
    res_f = call(
        last_f_kernel, outs, mm // 2, 2 << 20, [VM] * 5, pu2, qu2, v_a, v_b, acc_f
    )
    res_b = call(
        last_b_kernel, outs, mm // 2, 2 << 20, [VM] * 7, pu2, qu2, pv2, qv2, u_a, u_b, acc_b
    )
    got_f = [move_zy(r, 1, -d) for d, r in enumerate(res_f)]
    got_b = [move_zy(r, -1, -d) for d, r in enumerate(res_b)]
    final = functools.partial(
        call,
        combine_kernel,
        sds((n, width)),
        2 * 160 * 128 * width,
        2 << 20,
        [SM] + [VM] * 6,
        y,
    )
    out_f = final(ids_up_next, fwd_next, *got_f)
    out_b = final(ids_down_next, cot_next, *got_b)
    return (out_f[None], out_b[None])


def solution(mesh):
    return jax.shard_map(
        per_device,
        mesh=mesh,
        in_specs=(
            P("section", "expert", "dp"),
            P("section", None, "expert", None),
            P("section", "expert", "dp"),
            P("section", None, "expert", "dp"),
            P("section", None, "expert", None),
            P("section", "expert", "dp", None),
            P("section", "expert", None, "dp"),
        ),
        out_specs=(P("section", "expert", "dp"), P("section", "expert", "dp")),
        check_vma=False,
    )
```

time: 273 us -> 107 us (0.39)
  waiting for transfers between devices: 186 us -> 33.8 us
  starting transfers between devices: 32.3 us -> 55.5 us
  matrix products: 22.6 us -> 0 us
  between operations: 14.2 us -> 0.85 us
  Pallas kernels: 0 us -> 11.1 us
  local copies, waits for them, and re-layouts: 11.4 us -> 5.54 us
  other arithmetic: 5.42 us -> 0 us
    all_to_all x5 -> x0, waiting for transfers between devices: 142 us -> none  [the longest x1 31.9 us: per_device(): lax.all_to_all(input_grad.reshape(devices_all, capacity, features), 'expe...]
    ppermute x2 -> x27, starting transfers between devices: 4.38 us -> 55.5 us  [the longest x8 15 us: move_zy(): return lax.ppermute(v, ('section', 'expert'), pairs)]
    psum x1 -> x0, waiting for transfers between devices: 33.6 us -> none  [per_device(): lax.psum(hidden_forward.astype(jnp.bfloat16), 'dp').astype(jnp.float32)]
    all_to_all x5 -> x0, starting transfers between devices: 27.9 us -> none  [the longest x1 7.72 us: per_device(): lax.all_to_all(send_saved, 'expert', split_axis=0, concat_axis=0, tiled=T...]
    ppermute x2 -> x27, waiting for transfers between devices: 10 us -> 33.8 us  [the longest x8 22.4 us: move_x(): lax.ppermute(v, 'expert', [(y * NX + x, y * NX + (x + d) % NX) for y in r...]
    dot_general x10 -> x0, matrix products: 22.6 us -> none  [the longest x3 5.61 us: spread_rows(): jnp.dot(dispatch_table, row_data, preferred_element_type=jnp.float32)]
    pallas_call x0 -> x10, Pallas kernels: none -> 11.1 us  [call(): pl.pallas_call(kernel, out_shape=outs, in_specs=in_specs, out_specs=jax.t...]
    broadcast_in_dim x3 -> x0, local copies, waits for them, and re-layouts: 6.75 us -> none  [spread_rows(): jnp.broadcast_to(packed, (experts, split_count, capacity, features))]
  transfers between devices with their start and end apart: 8 -> 27, of which waited for: 7 -> 7; matrix products, arithmetic and copies ran while one was open for 6% -> 1% of each run, Pallas kernels for 0% -> 9%
where the time goes in v1:
time: 107 us
  starting transfers between devices  55.5 us (52%)
  waiting for transfers between devices  33.8 us (32%)
  Pallas kernels  11.1 us (10%)
  local copies, waits for them, and re-layouts  5.54 us (5%)
    ppermute x8, waiting for transfers between devices, move_x(): lax.ppermute(v, 'expert', [(y * NX + x, y * NX + (x + d) % NX) for y in r...  22.4 us
    ppermute x8, starting transfers between devices, move_zy(): return lax.ppermute(v, ('section', 'expert'), pairs)  15 us
    ppermute x8, starting transfers between devices, move_x(): lax.ppermute(v, 'expert', [(y * NX + x, y * NX + (x + d) % NX) for y in r...  12.5 us
    pallas_call x10, Pallas kernels, call(): pl.pallas_call(kernel, out_shape=outs, in_specs=in_specs, out_specs=jax.t...  11.1 us
    ppermute x4, starting transfers between devices, move_z(): return lax.ppermute(v, 'section', [(z, (z + d) % NZ) for z in range(NZ)])  11.1 us
    ppermute x8, waiting for transfers between devices, move_zy(): return lax.ppermute(v, ('section', 'expert'), pairs)  10.3 us
    ppermute x4, starting transfers between devices, swap(): return lax.ppermute(v, 'dp', [(0, 1), (1, 0)])  9.49 us
    ppermute x3, starting transfers between devices, move_y(): lax.ppermute(v, 'expert', [(y * NX + x, (y + d) % NY * NX + x) for y in r...  7.33 us
  transfers between devices with their start and end apart: 27, of which 7 were waited for; matrix products, arithmetic and copies ran while one was open for 1% of the time, Pallas kernels for 9%

profile of v1, /device:TPU:1, one launch (start us, length us, event | category | flops | bytes accessed | tf_op | source)
XLA Modules:
  0.0 106.8 jit_solution(773042263695549755)
XLA Ops:
  0.6 2.1 %collective-permute-start.5 = (bf16[1792,256]{1,0:T(8,128)(2,1)}, bf16[1792,256]{1,0:T(8,128)(2,1)S(1)}, u32[]{:S(2)}, u32[]{:S(2)}) collective-permute-start(bf16[1792,256]{1,0:T(8,128)(2,1)} %bitcast.10), channel_id=1, source_target_pairs={{0,2},{2,4},{4,6},{6,0},{8,10},{10,12},{12,14},{14,8},{16,18},{18,... | collective-permute-start | bytes 2752520 | tf_op jit(solution)/shard_map/ppermute | solution.py:23
  2.7 1.4 %collective-permute-start.7 = (bf16[1792,256]{1,0:T(8,128)(2,1)}, bf16[1792,256]{1,0:T(8,128)(2,1)S(1)}, u32[]{:S(2)}, u32[]{:S(2)}) collective-permute-start(bf16[1792,256]{1,0:T(8,128)(2,1)} %bitcast.11), channel_id=1, source_target_pairs={{0,6},{2,0},{4,2},{6,4},{8,14},{10,8},{12,10},{14,12},{16,22},{18,... | collective-permute-start | bytes 2752520 | tf_op jit(solution)/shard_map/ppermute | solution.py:23
  4.1 0.1 collective-permute-start.10
  4.2 2.6 %collective-permute-start.12 = (bf16[256,1792]{1,0:T(8,128)(2,1)}, bf16[256,1792]{1,0:T(8,128)(2,1)}, u32[]{:S(2)}, u32[]{:S(2)}) collective-permute-start(bf16[256,1792]{1,0:T(8,128)(2,1)} %bitcast.15), channel_id=1, source_target_pairs={{0,6},{2,0},{4,2},{6,4},{8,14},{10,8},{12,10},{14,12},{16,22},{18,... | collective-permute-start | bytes 2752520 | tf_op jit(solution)/shard_map/ppermute | solution.py:23
  6.8 1.0 copy-done.2
  7.8 1.0 copy-done.3
  8.8 1.0 copy-done.5
  9.8 0.7 copy-done.7
  10.5 0.7 copy-done.9
  11.2 0.7 shard_map.86
  11.9 1.5 %collective-permute-start.2 = (bf16[128,1792]{1,0:T(8,128)(2,1)S(1)}, bf16[128,1792]{1,0:T(8,128)(2,1)S(1)}, u32[]{:S(2)}, u32[]{:S(2)}) collective-permute-start(bf16[128,1792]{1,0:T(8,128)(2,1)S(1)} %get-tuple-element.17), channel_id=1, source_target_pairs={{0,8},{2,10},{4,12},{6,14},{8,16},{10,18},{12,20},{14,22},{16,24},... | collective-permute-start | bytes 1376264 | tf_op jit(solution)/shard_map/ppermute | solution.py:29
  13.4 8.6 %collective-permute-done.5.refs_1_.u1 = bf16[1792,256]{1,0:T(8,128)(2,1)S(1)} collective-permute-done((bf16[1792,256]{1,0:T(8,128)(2,1)}, bf16[1792,256]{1,0:T(8,128)(2,1)S(1)}, u32[]{:S(2)}, u32[]{:S(2)}) %collective-permute-start.5) | collective-permute-done | bytes 917536 | tf_op jit(solution)/shard_map/ppermute | solution.py:23
  22.0 5.1 %collective-permute-start.3 = (bf16[128,1792]{1,0:T(8,128)(2,1)S(1)}, bf16[128,1792]{1,0:T(8,128)(2,1)S(1)}, u32[]{:S(2)}, u32[]{:S(2)}) collective-permute-start(bf16[128,1792]{1,0:T(8,128)(2,1)S(1)} %get-tuple-element.18), channel_id=1, source_target_pairs={{0,16},{2,18},{4,20},{6,22},{8,24},{10,26},{12,28},{14,30},{16,0},... | collective-permute-start | bytes 1376264 | tf_op jit(solution)/shard_map/ppermute | solution.py:29
  27.1 0.8 collective-permute-start.4
  27.9 13.8 %collective-permute-done.10.refs_1_.v1 = bf16[256,1792]{1,0:T(8,128)(2,1)S(1)} collective-permute-done((bf16[256,1792]{1,0:T(8,128)(2,1)}, bf16[256,1792]{1,0:T(8,128)(2,1)S(1)}, u32[]{:S(2)}, u32[]{:S(2)}) %collective-permute-start.10) | collective-permute-done | bytes 917536 | tf_op jit(solution)/shard_map/ppermute | solution.py:23
  41.7 2.0 %collective-permute-start.6 = (bf16[896,256]{1,0:T(8,128)(2,1)S(1)}, bf16[896,256]{1,0:T(8,128)(2,1)S(1)}, u32[]{:S(2)}, u32[]{:S(2)}) collective-permute-start(bf16[896,256]{1,0:T(8,128)(2,1)S(1)} %slice.16), channel_id=1, source_target_pairs={{0,2},{2,4},{4,6},{6,0},{8,10},{10,12},{12,14},{14,8},{16,18},{18,... | collective-permute-start | bytes 1376264 | tf_op jit(solution)/shard_map/ppermute | solution.py:23
  43.7 0.0 copy-start
  43.7 0.0 collective-permute-done.12.refs_2_.v2
  43.7 1.6 %collective-permute-start.8 = (bf16[896,256]{1,0:T(8,128)(2,1)S(1)}, bf16[896,256]{1,0:T(8,128)(2,1)S(1)}, u32[]{:S(2)}, u32[]{:S(2)}) collective-permute-start(bf16[896,256]{1,0:T(8,128)(2,1)S(1)} %slice.17), channel_id=1, source_target_pairs={{0,6},{2,0},{4,2},{6,4},{8,14},{10,8},{12,10},{14,12},{16,22},{18,... | collective-permute-start | bytes 1376264 | tf_op jit(solution)/shard_map/ppermute | solution.py:23
  45.4 1.1 slice.19
  46.4 0.0 collective-permute-done.2.r1
  46.4 0.1 collective-permute-start.11
  46.6 2.6 %collective-permute-start.13 = (bf16[128,1792]{1,0:T(8,128)(2,1)S(1)}, bf16[128,1792]{1,0:T(8,128)(2,1)S(1)}, u32[]{:S(2)}, u32[]{:S(2)}) collective-permute-start(bf16[128,1792]{1,0:T(8,128)(2,1)S(1)} %slice.19), channel_id=1, source_target_pairs={{0,6},{2,0},{4,2},{6,4},{8,14},{10,8},{12,10},{14,12},{16,22},{18,... | collective-permute-start | bytes 1376264 | tf_op jit(solution)/shard_map/ppermute | solution.py:23
  49.2 1.1 shard_map.88.pu
  50.3 3.9 %collective-permute-start.14 = (bf16[320,768]{1,0:T(8,128)(2,1)S(1)}, bf16[320,768]{1,0:T(8,128)(2,1)S(1)}, u32[]{:S(2)}, u32[]{:S(2)}) collective-permute-start(bf16[320,768]{1,0:T(8,128)(2,1)S(1)} %shard_map.88.pu), channel_id=1, source_target_pairs={{0,1},{1,0},{2,3},{3,2},{4,5},{5,4},{6,7},{7,6},{8,9},{9,8},{10,11... | collective-permute-start | bytes 1474568 | tf_op jit(solution)/shard_map/ppermute | solution.py:50
  54.2 6.9 %collective-permute-start.21 = (bf16[128,1792]{1,0:T(8,128)(2,1)S(1)}, bf16[128,1792]{1,0:T(8,128)(2,1)S(1)}, u32[]{:S(2)}, u32[]{:S(2)}) collective-permute-start(bf16[128,1792]{1,0:T(8,128)(2,1)S(1)} %bitcast.20), channel_id=1, source_target_pairs={{0,224},{32,0},{64,32},{96,64},{128,96},{160,128},{192,160},{224,1... | collective-permute-start | bytes 1376264 | tf_op jit(solution)/shard_map/ppermute | solution.py:35
  61.1 2.2 %shard_map.89.pv = bf16[192,768]{1,0:T(8,128)(2,1)S(1)} custom-call(bf16[128,1792]{1,0:T(8,128)(2,1)S(1)} %get-tuple-element.16.r0, bf16[128,1792]{1,0:T(8,128)(2,1)S(1)} %collective-permute-done.2.r1, bf16[128,1792]{1,0:T(8,128)(2,1)S(1)} %collective-permute-done.3.r2, bf16[128,1792]{1,0:T(8,128)(2,1)S(1)} %collective-permute-done.4.r3, ...), custom_call_target="tpu_custom_call" | custom-call | flops 587202560 | bytes 4194304 | tf_op jit(solution)/shard_map/pallas_call | solution.py:54
  63.3 0.0 copy-start.6
  63.3 0.0 collective-permute-done.8.wb.ub
  63.4 5.1 %collective-permute-start.15 = (bf16[192,768]{1,0:T(8,128)(2,1)S(1)}, bf16[192,768]{1,0:T(8,128)(2,1)S(1)}, u32[]{:S(2)}, u32[]{:S(2)}) collective-permute-start(bf16[192,768]{1,0:T(8,128)(2,1)S(1)} %shard_map.89.pv), channel_id=1, source_target_pairs={{0,1},{1,0},{2,3},{3,2},{4,5},{5,4},{6,7},{7,6},{8,9},{9,8},{10,11... | collective-permute-start | bytes 884744 | tf_op jit(solution)/shard_map/ppermute | solution.py:50
  68.4 0.5 shard_map.87.pu
  68.9 0.0 copy-start.8
  69.0 0.1 collective-permute-start.9
  69.1 0.0 collective-permute-done.13.vb.refs_1_
  69.1 0.4 collective-permute-start.1
  69.5 0.5 shard_map.93.pv
  70.0 0.0 copy-start.10
  70.0 0.0 collective-permute-done.15.qv
  70.0 0.4 collective-permute-start.22
  70.5 0.0 collective-permute-done.14.qu
  70.5 3.7 %collective-permute-start.20 = (s32[1,128]{1,0:T(1,128)S(1)}, s32[1,128]{1,0:T(1,128)S(1)}, u32[]{:S(2)}, u32[]{:S(2)}) collective-permute-start(s32[1,128]{1,0:T(1,128)S(1)} %bitcast.24), channel_id=1, source_target_pairs={{0,224},{32,0},{64,32},{96,64},{128,96},{160,128},{192,160},{224,1... | collective-permute-start | bytes 1544 | tf_op jit(solution)/shard_map/ppermute | solution.py:35
  74.1 2.7 %shard_map.90 = (f32[160,1792]{1,0:T(8,128)S(1)}, f32[160,1792]{1,0:T(8,128)S(1)}) custom-call(bf16[320,768]{1,0:T(8,128)(2,1)S(1)} %shard_map.88.pu, bf16[320,768]{1,0:T(8,128)(2,1)S(1)} %collective-permute-done.14.qu, bf16[192,768]{1,0:T(8,128)(2,1)S(1)} %shard_map.89.pv, bf16[192,768]{1,0:T(8,128)(2,1)S(1)} %collective-permute-done.15.qv, ...), custom_call_target="tpu_custom_call" | custom-call | flops 880803840 | bytes 8388608 | tf_op jit(solution)/shard_map/pallas_call | solution.py:54
  76.9 0.0 collective-permute-done.22.qv
  76.9 0.1 collective-permute-start
  77.0 0.0 collective-permute-done.9.qu
  77.0 0.5 shard_map.94
  77.5 2.7 %collective-permute-start.23 = (bf16[40,1792]{1,0:T(8,128)(2,1)S(1)}, bf16[40,1792]{1,0:T(8,128)(2,1)S(1)}, u32[]{:S(2)}, u32[]{:S(2)}) collective-permute-start(bf16[40,1792]{1,0:T(8,128)(2,1)S(1)} %get-tuple-element.26), channel_id=1, source_target_pairs={{0,224},{2,226},{4,228},{6,230},{8,232},{10,234},{12,236},{14,238}... | collective-permute-start | bytes 430088 | tf_op jit(solution)/shard_map/ppermute | solution.py:46
  80.2 3.0 %collective-permute-start.24 = (bf16[40,1792]{1,0:T(8,128)(2,1)S(1)}, bf16[40,1792]{1,0:T(8,128)(2,1)S(1)}, u32[]{:S(2)}, u32[]{:S(2)}) collective-permute-start(bf16[40,1792]{1,0:T(8,128)(2,1)S(1)} %get-tuple-element.27), channel_id=1, source_target_pairs={{0,248},{2,250},{4,252},{6,254},{8,224},{10,226},{12,228},{14,230}... | collective-permute-start | bytes 430088 | tf_op jit(solution)/shard_map/ppermute | solution.py:46
  83.2 1.0 collective-permute-done.ids_ref
  84.2 3.9 %collective-permute-start.25 = (bf16[40,1792]{1,0:T(8,128)(2,1)S(1)}, bf16[40,1792]{1,0:T(8,128)(2,1)S(1)}, u32[]{:S(2)}, u32[]{:S(2)}) collective-permute-start(bf16[40,1792]{1,0:T(8,128)(2,1)S(1)} %get-tuple-element.28), channel_id=1, source_target_pairs={{0,240},{2,242},{4,244},{6,246},{8,248},{10,250},{12,252},{14,254}... | collective-permute-start | bytes 430088 | tf_op jit(solution)/shard_map/ppermute | solution.py:46
  88.1 0.0 collective-permute-done.21.rows_ref
  88.1 0.8 collective-permute-start.26
  89.0 0.4 shard_map.91
  89.4 0.0 collective-permute-done.23.f0
  89.4 0.8 collective-permute-start.16
  90.2 2.2 %collective-permute-start.17 = (bf16[40,1792]{1,0:T(8,128)(2,1)S(1)}, bf16[40,1792]{1,0:T(8,128)(2,1)S(1)}, u32[]{:S(2)}, u32[]{:S(2)}) collective-permute-start(bf16[40,1792]{1,0:T(8,128)(2,1)S(1)} %get-tuple-element.22), channel_id=1, source_target_pairs={{0,56},{2,58},{4,60},{6,62},{8,32},{10,34},{12,36},{14,38},{16,40}... | collective-permute-start | bytes 430088 | tf_op jit(solution)/shard_map/ppermute | solution.py:46
  92.4 0.3 collective-permute-start.18
  92.7 1.7 %collective-permute-done.26.f3 = bf16[40,1792]{1,0:T(8,128)(2,1)S(1)} collective-permute-done((bf16[40,1792]{1,0:T(8,128)(2,1)S(1)}, bf16[40,1792]{1,0:T(8,128)(2,1)S(1)}, u32[]{:S(2)}, u32[]{:S(2)}) %collective-permute-start.26) | collective-permute-done | bytes 143392 | tf_op jit(solution)/shard_map/ppermute | solution.py:46
  94.4 1.3 %collective-permute-start.19 = (bf16[40,1792]{1,0:T(8,128)(2,1)S(1)}, bf16[40,1792]{1,0:T(8,128)(2,1)S(1)}, u32[]{:S(2)}, u32[]{:S(2)}) collective-permute-start(bf16[40,1792]{1,0:T(8,128)(2,1)S(1)} %get-tuple-element.24), channel_id=1, source_target_pairs={{0,40},{2,42},{4,44},{6,46},{8,48},{10,50},{12,52},{14,54},{16,56}... | collective-permute-start | bytes 430088 | tf_op jit(solution)/shard_map/ppermute | solution.py:46
  95.7 1.2 %shard_map.95 = bf16[128,1792]{1,0:T(8,128)(2,1)} custom-call(s32[1]{0:T(128)} %bitcast.y_ref, s32[1,128]{1,0:T(1,128)S(1)} %collective-permute-done.20.ids_ref, bf16[128,1792]{1,0:T(8,128)(2,1)S(1)} %collective-permute-done.21.rows_ref, bf16[40,1792]{1,0:T(8,128)(2,1)S(1)} %collective-permute-done.23.f0, bf16[40,1792]{1,0:T(8,128)(2,1)S(1)} %collective-permute-done.24.f1, ...), custom_call_target="tpu_custom_call" | custom-call | flops 73400320 | bytes 2097152 | tf_op jit(solution)/shard_map/pallas_call | solution.py:54
  96.9 0.7 collective-permute-done.17.f1
  97.6 4.0 %collective-permute-done.18.f2 = bf16[40,1792]{1,0:T(8,128)(2,1)S(1)} collective-permute-done((bf16[40,1792]{1,0:T(8,128)(2,1)S(1)}, bf16[40,1792]{1,0:T(8,128)(2,1)S(1)}, u32[]{:S(2)}, u32[]{:S(2)}) %collective-permute-start.18) | collective-permute-done | bytes 143392 | tf_op jit(solution)/shard_map/ppermute | solution.py:46
  101.6 3.9 %collective-permute-done.19.f3 = bf16[40,1792]{1,0:T(8,128)(2,1)S(1)} collective-permute-done((bf16[40,1792]{1,0:T(8,128)(2,1)S(1)}, bf16[40,1792]{1,0:T(8,128)(2,1)S(1)}, u32[]{:S(2)}, u32[]{:S(2)}) %collective-permute-start.19) | collective-permute-done | bytes 143392 | tf_op jit(solution)/shard_map/ppermute | solution.py:46
  105.5 1.2 %shard_map.92 = bf16[128,1792]{1,0:T(8,128)(2,1)} custom-call(s32[1]{0:T(128)} %bitcast.y_ref, s32[1,128]{1,0:T(1,128)S(1)} %collective-permute-done.ids_ref, bf16[128,1792]{1,0:T(8,128)(2,1)S(1)} %collective-permute-done.1.rows_ref, bf16[40,1792]{1,0:T(8,128)(2,1)S(1)} %collective-permute-done.16.f0, bf16[40,1792]{1,0:T(8,128)(2,1)S(1)} %collective-permute-done.17.f1, ...), custom_call_target="tpu_custom_call" | custom-call | flops 73400320 | bytes 2097152 | tf_op jit(solution)/shard_map/pallas_call | solution.py:54
  (26 shorter events, 0.1 us)
Async XLA Ops:
  0.6 21.4 %collective-permute-start.5 = (bf16[1792,256]{1,0:T(8,128)(2,1)}, bf16[1792,256]{1,0:T(8,128)(2,1)S(1)}, u32[]{:S(2)}, u32[]{:S(2)}) collective-permute-start(bf16[1792,256]{1,0:T(8,128)(2,1)} %bitcast.10), channel_id=1, source_target_pairs={{0,2},{2,4},{4,6},{6,0},{8,10},{10,12},{12,14},{14,8},{16,18},{18,... | collective-permute-start | bytes 2752520 | tf_op jit(solution)/shard_map/ppermute | solution.py:23
  2.7 24.3 %collective-permute-start.7 = (bf16[1792,256]{1,0:T(8,128)(2,1)}, bf16[1792,256]{1,0:T(8,128)(2,1)S(1)}, u32[]{:S(2)}, u32[]{:S(2)}) collective-permute-start(bf16[1792,256]{1,0:T(8,128)(2,1)} %bitcast.11), channel_id=1, source_target_pairs={{0,6},{2,0},{4,2},{6,4},{8,14},{10,8},{12,10},{14,12},{16,22},{18,... | collective-permute-start | bytes 2752520 | tf_op jit(solution)/shard_map/ppermute | solution.py:23
  4.1 37.6 %collective-permute-start.10 = (bf16[256,1792]{1,0:T(8,128)(2,1)}, bf16[256,1792]{1,0:T(8,128)(2,1)S(1)}, u32[]{:S(2)}, u32[]{:S(2)}) collective-permute-start(bf16[256,1792]{1,0:T(8,128)(2,1)} %bitcast.14), channel_id=1, source_target_pairs={{0,2},{2,4},{4,6},{6,0},{8,10},{10,12},{12,14},{14,8},{16,18},{18,... | collective-permute-start | bytes 2752520 | tf_op jit(solution)/shard_map/ppermute | solution.py:23
  4.2 39.5 %collective-permute-start.12 = (bf16[256,1792]{1,0:T(8,128)(2,1)}, bf16[256,1792]{1,0:T(8,128)(2,1)}, u32[]{:S(2)}, u32[]{:S(2)}) collective-permute-start(bf16[256,1792]{1,0:T(8,128)(2,1)} %bitcast.15), channel_id=1, source_target_pairs={{0,6},{2,0},{4,2},{6,4},{8,14},{10,8},{12,10},{14,12},{16,22},{18,... | collective-permute-start | bytes 2752520 | tf_op jit(solution)/shard_map/ppermute | solution.py:23
  6.8 1.0 copy-start.2
  7.8 1.0 copy-start.3
  8.8 1.0 copy-start.5
  9.8 0.7 copy-start.7
  10.5 0.7 copy-start.9
  11.9 34.6 %collective-permute-start.2 = (bf16[128,1792]{1,0:T(8,128)(2,1)S(1)}, bf16[128,1792]{1,0:T(8,128)(2,1)S(1)}, u32[]{:S(2)}, u32[]{:S(2)}) collective-permute-start(bf16[128,1792]{1,0:T(8,128)(2,1)S(1)} %get-tuple-element.17), channel_id=1, source_target_pairs={{0,8},{2,10},{4,12},{6,14},{8,16},{10,18},{12,20},{14,22},{16,24},... | collective-permute-start | bytes 1376264 | tf_op jit(solution)/shard_map/ppermute | solution.py:29
  22.0 24.6 %collective-permute-start.3 = (bf16[128,1792]{1,0:T(8,128)(2,1)S(1)}, bf16[128,1792]{1,0:T(8,128)(2,1)S(1)}, u32[]{:S(2)}, u32[]{:S(2)}) collective-permute-start(bf16[128,1792]{1,0:T(8,128)(2,1)S(1)} %get-tuple-element.18), channel_id=1, source_target_pairs={{0,16},{2,18},{4,20},{6,22},{8,24},{10,26},{12,28},{14,30},{16,0},... | collective-permute-start | bytes 1376264 | tf_op jit(solution)/shard_map/ppermute | solution.py:29
  27.1 22.1 %collective-permute-start.4 = (bf16[128,1792]{1,0:T(8,128)(2,1)S(1)}, bf16[128,1792]{1,0:T(8,128)(2,1)S(1)}, u32[]{:S(2)}, u32[]{:S(2)}) collective-permute-start(bf16[128,1792]{1,0:T(8,128)(2,1)S(1)} %get-tuple-element.19), channel_id=1, source_target_pairs={{0,24},{2,26},{4,28},{6,30},{8,0},{10,2},{12,4},{14,6},{16,8},{18,... | collective-permute-start | bytes 1376264 | tf_op jit(solution)/shard_map/ppermute | solution.py:29
  41.7 12.5 %collective-permute-start.6 = (bf16[896,256]{1,0:T(8,128)(2,1)S(1)}, bf16[896,256]{1,0:T(8,128)(2,1)S(1)}, u32[]{:S(2)}, u32[]{:S(2)}) collective-permute-start(bf16[896,256]{1,0:T(8,128)(2,1)S(1)} %slice.16), channel_id=1, source_target_pairs={{0,2},{2,4},{4,6},{6,0},{8,10},{10,12},{12,14},{14,8},{16,18},{18,... | collective-permute-start | bytes 1376264 | tf_op jit(solution)/shard_map/ppermute | solution.py:23
  43.7 5.5 %copy-start = (bf16[1,1,1792,256]{3,2,1,0:T(8,128)(2,1)S(1)}, bf16[1,1,1792,256]{3,2,1,0:T(8,128)(2,1)}, u32[]{:S(2)}) copy-start(bf16[1,1,1792,256]{3,2,1,0:T(8,128)(2,1)} %param.12) | copy-start | bytes 2752516
  43.7 19.6 %collective-permute-start.8 = (bf16[896,256]{1,0:T(8,128)(2,1)S(1)}, bf16[896,256]{1,0:T(8,128)(2,1)S(1)}, u32[]{:S(2)}, u32[]{:S(2)}) collective-permute-start(bf16[896,256]{1,0:T(8,128)(2,1)S(1)} %slice.17), channel_id=1, source_target_pairs={{0,6},{2,0},{4,2},{6,4},{8,14},{10,8},{12,10},{14,12},{16,22},{18,... | collective-permute-start | bytes 1376264 | tf_op jit(solution)/shard_map/ppermute | solution.py:23
  46.4 22.5 %collective-permute-start.11 = (bf16[128,1792]{1,0:T(8,128)(2,1)S(1)}, bf16[128,1792]{1,0:T(8,128)(2,1)S(1)}, u32[]{:S(2)}, u32[]{:S(2)}) collective-permute-start(bf16[128,1792]{1,0:T(8,128)(2,1)S(1)} %slice.18), channel_id=1, source_target_pairs={{0,2},{2,4},{4,6},{6,0},{8,10},{10,12},{12,14},{14,8},{16,18},{18,... | collective-permute-start | bytes 1376264 | tf_op jit(solution)/shard_map/ppermute | solution.py:23
  46.6 22.5 %collective-permute-start.13 = (bf16[128,1792]{1,0:T(8,128)(2,1)S(1)}, bf16[128,1792]{1,0:T(8,128)(2,1)S(1)}, u32[]{:S(2)}, u32[]{:S(2)}) collective-permute-start(bf16[128,1792]{1,0:T(8,128)(2,1)S(1)} %slice.19), channel_id=1, source_target_pairs={{0,6},{2,0},{4,2},{6,4},{8,14},{10,8},{12,10},{14,12},{16,22},{18,... | collective-permute-start | bytes 1376264 | tf_op jit(solution)/shard_map/ppermute | solution.py:23
  49.2 4.9 %copy-start.4 = (bf16[1,128,1792]{2,1,0:T(8,128)(2,1)S(1)}, bf16[1,128,1792]{2,1,0:T(8,128)(2,1)}, u32[]{:S(2)}) copy-start(bf16[1,128,1792]{2,1,0:T(8,128)(2,1)} %param.9) | copy-start | bytes 1376260
  49.2 11.9 %copy-start.1 = (bf16[1,1,256,1792]{3,2,1,0:T(8,128)(2,1)S(1)}, bf16[1,1,256,1792]{3,2,1,0:T(8,128)(2,1)}, u32[]{:S(2)}) copy-start(bf16[1,1,256,1792]{3,2,1,0:T(8,128)(2,1)} %param.13) | copy-start | bytes 2752516
  50.3 20.2 %collective-permute-start.14 = (bf16[320,768]{1,0:T(8,128)(2,1)S(1)}, bf16[320,768]{1,0:T(8,128)(2,1)S(1)}, u32[]{:S(2)}, u32[]{:S(2)}) collective-permute-start(bf16[320,768]{1,0:T(8,128)(2,1)S(1)} %shard_map.88.pu), channel_id=1, source_target_pairs={{0,1},{1,0},{2,3},{3,2},{4,5},{5,4},{6,7},{7,6},{8,9},{9,8},{10,11... | collective-permute-start | bytes 1474568 | tf_op jit(solution)/shard_map/ppermute | solution.py:50
  54.2 34.0 %collective-permute-start.21 = (bf16[128,1792]{1,0:T(8,128)(2,1)S(1)}, bf16[128,1792]{1,0:T(8,128)(2,1)S(1)}, u32[]{:S(2)}, u32[]{:S(2)}) collective-permute-start(bf16[128,1792]{1,0:T(8,128)(2,1)S(1)} %bitcast.20), channel_id=1, source_target_pairs={{0,224},{32,0},{64,32},{96,64},{128,96},{160,128},{192,160},{224,1... | collective-permute-start | bytes 1376264 | tf_op jit(solution)/shard_map/ppermute | solution.py:35
  63.3 5.7 %copy-start.6 = (bf16[1,128,1792]{2,1,0:T(8,128)(2,1)S(1)}, bf16[1,128,1792]{2,1,0:T(8,128)(2,1)}, u32[]{:S(2)}) copy-start(bf16[1,128,1792]{2,1,0:T(8,128)(2,1)} %param.7) | copy-start | bytes 1376260
  63.4 6.7 %collective-permute-start.15 = (bf16[192,768]{1,0:T(8,128)(2,1)S(1)}, bf16[192,768]{1,0:T(8,128)(2,1)S(1)}, u32[]{:S(2)}, u32[]{:S(2)}) collective-permute-start(bf16[192,768]{1,0:T(8,128)(2,1)S(1)} %shard_map.89.pv), channel_id=1, source_target_pairs={{0,1},{1,0},{2,3},{3,2},{4,5},{5,4},{6,7},{7,6},{8,9},{9,8},{10,11... | collective-permute-start | bytes 884744 | tf_op jit(solution)/shard_map/ppermute | solution.py:50
  68.9 1.5 %copy-start.8 = (s32[1,1,128,1]{2,3,1,0:T(1,128)S(1)}, s32[1,1,128,1]{2,3,1,0:T(1,128)}, u32[]{:S(2)}) copy-start(s32[1,1,128,1]{2,3,1,0:T(1,128)} %param.11) | copy-start | bytes 1540
  69.0 8.0 %collective-permute-start.9 = (bf16[320,256]{1,0:T(8,128)(2,1)S(1)}, bf16[320,256]{1,0:T(8,128)(2,1)S(1)}, u32[]{:S(2)}, u32[]{:S(2)}) collective-permute-start(bf16[320,256]{1,0:T(8,128)(2,1)S(1)} %shard_map.87.pu), channel_id=1, source_target_pairs={{0,1},{1,0},{2,3},{3,2},{4,5},{5,4},{6,7},{7,6},{8,9},{9,8},{10,11... | collective-permute-start | bytes 491528 | tf_op jit(solution)/shard_map/ppermute | solution.py:50
  69.1 27.8 %collective-permute-start.1 = (bf16[128,1792]{1,0:T(8,128)(2,1)S(1)}, bf16[128,1792]{1,0:T(8,128)(2,1)S(1)}, u32[]{:S(2)}, u32[]{:S(2)}) collective-permute-start(bf16[128,1792]{1,0:T(8,128)(2,1)S(1)} %bitcast.22), channel_id=1, source_target_pairs={{0,32},{32,64},{64,96},{96,128},{128,160},{160,192},{192,224},{224... | collective-permute-start | bytes 1376264 | tf_op jit(solution)/shard_map/ppermute | solution.py:35
  70.0 6.9 %copy-start.10 = (s32[1,1,128,1]{2,3,1,0:T(1,128)S(1)}, s32[1,1,128,1]{2,3,1,0:T(1,128)}, u32[]{:S(2)}) copy-start(s32[1,1,128,1]{2,3,1,0:T(1,128)} %param.8) | copy-start | bytes 1540
  70.0 6.9 %collective-permute-start.22 = (bf16[192,256]{1,0:T(8,128)(2,1)S(1)}, bf16[192,256]{1,0:T(8,128)(2,1)S(1)}, u32[]{:S(2)}, u32[]{:S(2)}) collective-permute-start(bf16[192,256]{1,0:T(8,128)(2,1)S(1)} %shard_map.93.pv), channel_id=1, source_target_pairs={{0,1},{1,0},{2,3},{3,2},{4,5},{5,4},{6,7},{7,6},{8,9},{9,8},{10,11... | collective-permute-start | bytes 294920 | tf_op jit(solution)/shard_map/ppermute | solution.py:50
  70.5 9.8 %collective-permute-start.20 = (s32[1,128]{1,0:T(1,128)S(1)}, s32[1,128]{1,0:T(1,128)S(1)}, u32[]{:S(2)}, u32[]{:S(2)}) collective-permute-start(s32[1,128]{1,0:T(1,128)S(1)} %bitcast.24), channel_id=1, source_target_pairs={{0,224},{32,0},{64,32},{96,64},{128,96},{160,128},{192,160},{224,1... | collective-permute-start | bytes 1544 | tf_op jit(solution)/shard_map/ppermute | solution.py:35
  76.9 7.3 %collective-permute-start = (s32[1,128]{1,0:T(1,128)S(1)}, s32[1,128]{1,0:T(1,128)S(1)}, u32[]{:S(2)}, u32[]{:S(2)}) collective-permute-start(s32[1,128]{1,0:T(1,128)S(1)} %bitcast.26), channel_id=1, source_target_pairs={{0,32},{32,64},{64,96},{96,128},{128,160},{160,192},{192,224},{224... | collective-permute-start | bytes 1544 | tf_op jit(solution)/shard_map/ppermute | solution.py:35
  77.5 11.9 %collective-permute-start.23 = (bf16[40,1792]{1,0:T(8,128)(2,1)S(1)}, bf16[40,1792]{1,0:T(8,128)(2,1)S(1)}, u32[]{:S(2)}, u32[]{:S(2)}) collective-permute-start(bf16[40,1792]{1,0:T(8,128)(2,1)S(1)} %get-tuple-element.26), channel_id=1, source_target_pairs={{0,224},{2,226},{4,228},{6,230},{8,232},{10,234},{12,236},{14,238}... | collective-permute-start | bytes 430088 | tf_op jit(solution)/shard_map/ppermute | solution.py:46
  80.2 10.0 %collective-permute-start.24 = (bf16[40,1792]{1,0:T(8,128)(2,1)S(1)}, bf16[40,1792]{1,0:T(8,128)(2,1)S(1)}, u32[]{:S(2)}, u32[]{:S(2)}) collective-permute-start(bf16[40,1792]{1,0:T(8,128)(2,1)S(1)} %get-tuple-element.27), channel_id=1, source_target_pairs={{0,248},{2,250},{4,252},{6,254},{8,224},{10,226},{12,228},{14,230}... | collective-permute-start | bytes 430088 | tf_op jit(solution)/shard_map/ppermute | solution.py:46
  84.2 8.2 %collective-permute-start.25 = (bf16[40,1792]{1,0:T(8,128)(2,1)S(1)}, bf16[40,1792]{1,0:T(8,128)(2,1)S(1)}, u32[]{:S(2)}, u32[]{:S(2)}) collective-permute-start(bf16[40,1792]{1,0:T(8,128)(2,1)S(1)} %get-tuple-element.28), channel_id=1, source_target_pairs={{0,240},{2,242},{4,244},{6,246},{8,248},{10,250},{12,252},{14,254}... | collective-permute-start | bytes 430088 | tf_op jit(solution)/shard_map/ppermute | solution.py:46
  88.1 6.2 %collective-permute-start.26 = (bf16[40,1792]{1,0:T(8,128)(2,1)S(1)}, bf16[40,1792]{1,0:T(8,128)(2,1)S(1)}, u32[]{:S(2)}, u32[]{:S(2)}) collective-permute-start(bf16[40,1792]{1,0:T(8,128)(2,1)S(1)} %get-tuple-element.29), channel_id=1, source_target_pairs={{0,232},{2,234},{4,236},{6,238},{8,240},{10,242},{12,244},{14,246}... | collective-permute-start | bytes 430088 | tf_op jit(solution)/shard_map/ppermute | solution.py:46
  89.4 7.5 %collective-permute-start.16 = (bf16[40,1792]{1,0:T(8,128)(2,1)S(1)}, bf16[40,1792]{1,0:T(8,128)(2,1)S(1)}, u32[]{:S(2)}, u32[]{:S(2)}) collective-permute-start(bf16[40,1792]{1,0:T(8,128)(2,1)S(1)} %get-tuple-element.21), channel_id=1, source_target_pairs={{0,32},{2,34},{4,36},{6,38},{8,40},{10,42},{12,44},{14,46},{16,48}... | collective-permute-start | bytes 430088 | tf_op jit(solution)/shard_map/ppermute | solution.py:46
  90.2 7.4 %collective-permute-start.17 = (bf16[40,1792]{1,0:T(8,128)(2,1)S(1)}, bf16[40,1792]{1,0:T(8,128)(2,1)S(1)}, u32[]{:S(2)}, u32[]{:S(2)}) collective-permute-start(bf16[40,1792]{1,0:T(8,128)(2,1)S(1)} %get-tuple-element.22), channel_id=1, source_target_pairs={{0,56},{2,58},{4,60},{6,62},{8,32},{10,34},{12,36},{14,38},{16,40}... | collective-permute-start | bytes 430088 | tf_op jit(solution)/shard_map/ppermute | solution.py:46
  92.4 9.2 %collective-permute-start.18 = (bf16[40,1792]{1,0:T(8,128)(2,1)S(1)}, bf16[40,1792]{1,0:T(8,128)(2,1)S(1)}, u32[]{:S(2)}, u32[]{:S(2)}) collective-permute-start(bf16[40,1792]{1,0:T(8,128)(2,1)S(1)} %get-tuple-element.23), channel_id=1, source_target_pairs={{0,48},{2,50},{4,52},{6,54},{8,56},{10,58},{12,60},{14,62},{16,32}... | collective-permute-start | bytes 430088 | tf_op jit(solution)/shard_map/ppermute | solution.py:46
  94.4 11.2 %collective-permute-start.19 = (bf16[40,1792]{1,0:T(8,128)(2,1)S(1)}, bf16[40,1792]{1,0:T(8,128)(2,1)S(1)}, u32[]{:S(2)}, u32[]{:S(2)}) collective-permute-start(bf16[40,1792]{1,0:T(8,128)(2,1)S(1)} %get-tuple-element.24), channel_id=1, source_target_pairs={{0,40},{2,42},{4,44},{6,46},{8,48},{10,50},{12,52},{14,54},{16,56}... | collective-permute-start | bytes 430088 | tf_op jit(solution)/shard_map/ppermute | solution.py:46

commit v2 on v1

--- a/solution.py
+++ b/solution.py
@@ -15,7 +15,11 @@
 BF = jnp.bfloat16
 F32 = jnp.float32
 VM = pl.BlockSpec(memory_space=pltpu.VMEM)
+ANY = pl.BlockSpec(memory_space=pl.ANY)
+HBM = pl.BlockSpec(memory_space=pltpu.HBM)
 SM = pl.BlockSpec(memory_space=pltpu.SMEM)
+
+CU = 8 * 10**9
 LIMIT = 24 * 1024 * 1024
 
 
@@ -50,10 +54,11 @@
     return lax.ppermute(v, "dp", [(0, 1), (1, 0)])
 
 
-def call(kernel, outs, flops, nbytes, in_specs, *args):
+def call(kernel, outs, flops, nbytes, in_specs, *args, scratch=()):
     return pl.pallas_call(
         kernel,
         out_shape=outs,
+        scratch_shapes=scratch,
         in_specs=in_specs,
         out_specs=jax.tree.map(lambda _: VM, outs),
         compiler_params=pltpu.CompilerParams(vmem_limit_bytes=LIMIT),
@@ -95,21 +100,48 @@
     return [slice(c, c + step) for c in range(0, width, step)]
 
 
-def dispatch_kernel(y_ref, up_ref, down_ref, fwd_ref, saved_ref, grad_ref, *outs):
+def dispatch_kernel(y_ref, *refs):
+    ins, outs, scratch, sems = refs[:5], refs[5:9], refs[9:14], refs[14]
+    copies = [pltpu.make_async_copy(i, s, sems.at[k]) for k, (i, s) in enumerate(zip(ins, scratch))]
+    for c in copies:
+        c.start()
+    up, down, fwd, saved, grad = scratch
     y = y_ref[0]
-    table_up = slot_table(up_ref[...], y)
-    table_down = slot_table(down_ref[...], y)
-    for c in columns(fwd_ref.shape[1]):
-        f = nn(table_up, fwd_ref[:, c])
-        s = nn(table_down, saved_ref[:, c])
-        g = nn(table_down, grad_ref[:, c])
+    copies[0].wait()
+    copies[1].wait()
+    table_up = slot_table(up[...], y)
+    table_down = slot_table(down[...], y)
+    for c in copies[2:]:
+        c.wait()
+    for c in columns(fwd.shape[1]):
+        f = nn(table_up, fwd[:, c])
+        s = nn(table_down, saved[:, c])
+        g = nn(table_down, grad[:, c])
         pad = jnp.zeros((ROWS - 3 * CAP, f.shape[1]), F32)
         for rel in range(NY):
             r = slice(rel * CAP, (rel + 1) * CAP)
             outs[rel][:, c] = jnp.concatenate([f[r], s[r], g[r], pad], axis=0).astype(BF)
 
 
-def up_kernel(r0, r1, r2, r3, *refs):
+def table_kernel(y_ref, ids_f, ids_b, out_f, out_b):
+    out_f[...] = slot_table(ids_f[...], y_ref[0])
+    out_b[...] = slot_table(ids_b[...], y_ref[0])
+
+
+def held_kernel(v_ref, *refs):
+    out, sem = refs[-2:]
+    c = pltpu.make_async_copy(v_ref, out, sem)
+    c.start()
+    c.wait()
+
+
+def parts_kernel(left, right, out_a, out_b):
+    half = out_a.shape[0]
+    out_a[...] = left[:half, :]
+    out_b[...] = right[half:, :]
+
+
+def up_kernel(r0, r1, r2, r3, token, *refs):
     *weights, out = refs
     rows = jnp.concatenate([r[0 : 2 * CAP, :] for r in (r0, r1, r2, r3)], axis=0)
     for i, w in enumerate(weights):
@@ -122,7 +154,7 @@
     out[...] = (nn(rows[:, :half], wa[...]) + nn(rows[:, half:], wb[...])).astype(BF)
 
 
-def down_kernel(r0, r1, r2, r3, *refs):
+def down_kernel(r0, r1, r2, r3, token, *refs):
     *weights, out = refs
     rows = jnp.concatenate([r[2 * CAP : ROWS, :] for r in (r0, r1, r2, r3)], axis=0)
     at = 0
@@ -138,8 +170,8 @@
     )
 
 
-def added(a_ref, b_ref):
-    return a_ref[...].astype(F32) + b_ref[...].astype(F32)
+def added(a, b):
+    return a.astype(F32) + b.astype(F32)
 
 
 def activate(pu):
@@ -154,44 +186,45 @@
     return (g * (q * (1.0 + v * (1.0 - q)))).astype(BF)
 
 
-def mid_kernel(pu, qu, pv, qv, u0, u1, u2, v0, v1, v2, acc_f, acc_b):
-    su = added(pu, qu)
+def mid_kernel(r0, r1, r2, r3, pu, qu, pv, qv, u0, u1, u2, v0, v1, v2, acc_f, acc_b):
+    su = added(pu[...], qu[...])
     act = activate(su)
-    hid = grad_hidden(su, added(pv, qv))
+    hid = grad_hidden(su, added(pv[...], qv[...]))
     for c in columns(acc_f.shape[1]):
-        acc_f[:, c] = sum(
-            nn(act[:, i * 256 : (i + 1) * 256], v[:, c]) for i, v in enumerate((v0, v1, v2))
-        )
-        acc_b[:, c] = sum(
-            nt(hid[:, i * 256 : (i + 1) * 256], u[c, :]) for i, u in enumerate((u0, u1, u2))
-        )
-
-
-def last_f_kernel(pu, qu, va, vb, acc, *outs):
-    act = activate(added(pu, qu))
+        rows = [r[:, c].astype(F32) for r in (r0, r1, r2, r3)]
+        f = jnp.concatenate([r[:CAP] for r in rows], axis=0)
+        b = jnp.concatenate([r[2 * CAP : 3 * CAP] for r in rows], axis=0)
+        for i, (u, v) in enumerate(((u0, v0), (u1, v1), (u2, v2))):
+            f += nn(act[:, i * 256 : (i + 1) * 256], v[:, c])
+            b += nt(hid[:, i * 256 : (i + 1) * 256], u[c, :])
+        acc_f[:, c] = f
+        acc_b[:, c] = b
+
+
+def last_f_kernel(pu, qu, va, vb, acc, token, *outs):
+    act = activate(added(pu[...], qu[...]))
     half = va.shape[0]
     for c in columns(acc.shape[1]):
         t = acc[:, c] + nn(act[:, :half], va[:, c]) + nn(act[:, half:], vb[:, c])
-        for i in range(NY):
-            outs[i][:, c] = t[i * CAP : (i + 1) * CAP].astype(BF)
-
-
-def last_b_kernel(pu, qu, pv, qv, ua, ub, acc, *outs):
-    hid = grad_hidden(added(pu, qu), added(pv, qv))
+        for i, o in enumerate(outs):
+            o[:, c] = t[i * CAP : (i + 1) * CAP].astype(BF)
+
+
+def last_b_kernel(pu, qu, pv, qv, ua, ub, acc, token, *outs):
+    hid = grad_hidden(added(pu[...], qu[...]), added(pv[...], qv[...]))
     half = ua.shape[0]
     for u, base in ((ua, 0), (ub, half)):
         for c in columns(half, 128):
             o = slice(base + c.start, base + c.stop)
             t = acc[:, o] + nt(hid, u[c, :])
-            for i in range(NY):
-                outs[i][:, o] = t[i * CAP : (i + 1) * CAP].astype(BF)
-
-
-def combine_kernel(y_ref, ids_ref, rows_ref, f0, f1, f2, f3, out):
-    table = slot_table(ids_ref[...], y_ref[0])
-    for c in columns(rows_ref.shape[1]):
+            for i, out in enumerate(outs):
+                out[:, o] = t[i * CAP : (i + 1) * CAP].astype(BF)
+
+
+def combine_kernel(table, f0, f1, f2, f3, out):
+    for c in columns(out.shape[1]):
         got = jnp.concatenate([f[:, c].astype(F32) for f in (f0, f1, f2, f3)], axis=0).astype(BF)
-        out[:, c] = (rows_ref[:, c].astype(F32) + tn(table, got)).astype(BF)
+        out[:, c] = tn(table[...], got).astype(BF)
 
 
 def per_device(
@@ -207,34 +240,72 @@
     ids_up = routes_up.reshape(1, n)
     ids_down = routes_down.reshape(1, n)
     y = (lax.axis_index("expert") // NX).reshape(1)
+    mm = 2 * 320 * width * hp
+
+    def parts(left, right, cost):
+        half = sds((left.shape[0] // 2, left.shape[1]))
+        return call(
+            parts_kernel, [half] * 2, cost, 4 * half.shape[0] * half.shape[1], [VM] * 2, left, right
+        )
 
     u_l, u_r = move_x(u_own, 1), move_x(u_own, -1)
     v_l, v_r = move_x(v_own, 1), move_x(v_own, -1)
+    to_r, to_l = parts(u_l, u_r, CU)
+    to_u = to_r
+    u_a, u_b = move_x(to_r, 1), move_x(to_l, -1)
+    to_r, to_l = parts(v_l, v_r, 0)
+    to_v = to_r
+    v_a, v_b = move_x(to_r, 1), move_x(to_l, -1)
+
+    ids_f, ids_b = move_z(ids_up, 1), move_z(ids_down, -1)
+    table_f, table_b = call(
+        table_kernel, [sds((NY * CAP, n))] * 2, 0, 4 * NY * CAP * n, [SM, VM, VM], y, ids_f, ids_b
+    )
+
+    def held(v, cost, *tokens):
+        return call(
+            held_kernel,
+            sds(v.shape),
+            cost,
+            4 * ROWS * width,
+            [ANY] * (1 + len(tokens)),
+            v,
+            *tokens,
+            scratch=[pltpu.SemaphoreType.DMA],
+        )
 
     sent = call(
         dispatch_kernel,
         [sds((ROWS, width))] * NY,
         6 * 160 * 128 * width,
         7 * 128 * width * 2,
-        [SM] + [VM] * 5,
+        [SM] + [ANY] * 5,
         y,
         ids_up,
         ids_down,
         fwd,
         saved,
         cot,
-    )
-    rows = [sent[0]] + [move_y(sent[d], d) for d in range(1, NY)]
-
-    fwd_next, ids_up_next = move_z(fwd, 1), move_z(ids_up, 1)
-    cot_next, ids_down_next = move_z(cot, -1), move_z(ids_down, -1)
-
-    u_a, u_b = move_x(u_l[: width // 2], 1), move_x(u_r[width // 2 :], -1)
-    v_a, v_b = move_x(v_l[: hp // 2], 1), move_x(v_r[hp // 2 :], -1)
-
-    mm = 2 * 320 * width * hp
+        scratch=[pltpu.VMEM((1, n), jnp.int32)] * 2
+        + [pltpu.VMEM((n, width), BF)] * 3
+        + [pltpu.SemaphoreType.DMA((5,))],
+    )
+    row2 = move_y(sent[2], 2)
+    row1 = move_y(held(sent[1], 0, row2, table_f), 1)
+    row3 = move_y(held(sent[3], 0, row1, to_u), 3)
+    rows = [sent[0], row1, row2, row3]
+
     pu = call(
-        up_kernel, sds((2 * CAP * NY, 3 * hp)), 3 * mm, 4 << 20, [VM] * 7, *rows, u_own, u_l, u_r
+        up_kernel,
+        sds((2 * CAP * NY, 3 * hp)),
+        3 * mm,
+        4 << 20,
+        [VM] * 4 + [ANY] + [VM] * 3,
+        *rows,
+        to_v,
+        u_own,
+        u_l,
+        u_r,
     )
     qu = swap(pu)
     pv = call(
@@ -242,8 +313,9 @@
         sds(((ROWS - 2 * CAP) * NY, 3 * hp)),
         2 * mm,
         4 << 20,
-        [VM] * 7,
+        [VM] * 4 + [ANY] + [VM] * 3,
         *rows,
+        pu,
         v_own,
         v_l,
         v_r,
@@ -254,7 +326,8 @@
         [sds((NY * CAP, width), F32)] * 2,
         3 * mm,
         8 << 20,
-        [VM] * 10,
+        [VM] * 14,
+        *rows,
         pu,
         qu,
         pv,
@@ -273,32 +346,49 @@
         sds(((ROWS - 2 * CAP) * NY, hp)),
         mm // 2,
         2 << 20,
-        [VM] * 6,
+        [VM] * 4 + [ANY] + [VM] * 2,
         *rows,
+        acc_b,
         v_a,
         v_b,
     )
     qv2 = swap(pv2)
     outs = [sds((CAP, width))] * NY
     res_f = call(
-        last_f_kernel, outs, mm // 2, 2 << 20, [VM] * 5, pu2, qu2, v_a, v_b, acc_f
-    )
+        last_f_kernel,
+        outs,
+        mm // 2,
+        2 << 20,
+        [VM] * 5 + [ANY],
+        pu2,
+        qu2,
+        v_a,
+        v_b,
+        acc_f,
+        pv2,
+    )
+    got_f = [move_zy(r, 1, -d) for d, r in enumerate(res_f)]
     res_b = call(
-        last_b_kernel, outs, mm // 2, 2 << 20, [VM] * 7, pu2, qu2, pv2, qv2, u_a, u_b, acc_b
-    )
-    got_f = [move_zy(r, 1, -d) for d, r in enumerate(res_f)]
+        last_b_kernel,
+        outs,
+        mm // 2,
+        2 << 20,
+        [VM] * 7 + [ANY],
+        pu2,
+        qu2,
+        pv2,
+        qv2,
+        u_a,
+        u_b,
+        acc_b,
+        res_f[2],
+    )
     got_b = [move_zy(r, -1, -d) for d, r in enumerate(res_b)]
     final = functools.partial(
-        call,
-        combine_kernel,
-        sds((n, width)),
-        2 * 160 * 128 * width,
-        2 << 20,
-        [SM] + [VM] * 6,
-        y,
-    )
-    out_f = final(ids_up_next, fwd_next, *got_f)
-    out_b = final(ids_down_next, cot_next, *got_b)
+        call, combine_kernel, sds((n, width)), 2 * 160 * 128 * width, 2 << 20, [VM] * 5
+    )
+    out_f = final(table_f, *got_f)
+    out_b = final(table_b, *got_b)
     return (out_f[None], out_b[None])
 
 

time: 107 us -> 95.5 us (0.89)
  starting transfers between devices: 55.5 us -> 49.9 us
  waiting for transfers between devices: 33.8 us -> 30.1 us
  local copies, waits for them, and re-layouts: 5.54 us -> 4.37 us
    ppermute x8, waiting for transfers between devices: 22.4 us -> 9.87 us  [move_x(): lax.ppermute(v, 'expert', [(y * NX + x, y * NX + (x + d) % NX) for y in r...]
    ppermute x3, waiting for transfers between devices: 0.01 us -> 9.51 us  [move_y(): lax.ppermute(v, 'expert', [(y * NX + x, (y + d) % NY * NX + x) for y in r...]
    ppermute x4 -> x2, starting transfers between devices: 11.1 us -> 5.58 us  [move_z(): return lax.ppermute(v, 'section', [(z, (z + d) % NZ) for z in range(NZ)])]
    ppermute x8, starting transfers between devices: 15 us -> 16.6 us  [move_zy(): return lax.ppermute(v, ('section', 'expert'), pairs)]
    ppermute x3, starting transfers between devices: 7.33 us -> 5.96 us  [move_y(): lax.ppermute(v, 'expert', [(y * NX + x, (y + d) % NY * NX + x) for y in r...]
    slice x4 -> x0, local copies, waits for them, and re-layouts: 1.14 us -> none  [the longest x2 1.08 us: per_device(): v_a, v_b = (move_x(v_l[:hp // 2], 1), move_x(v_r[hp // 2:], -1))]
    pallas_call x10 -> x15, Pallas kernels: 11.1 us -> 10.1 us  [call(): pl.pallas_call(kernel, out_shape=outs, scratch_shapes=scratch, in_specs=i...]
    unnamed x22 -> x14, local copies, waits for them, and re-layouts: 4.39 us -> 4.37 us
  transfers between devices with their start and end apart: 27 -> 25, of which waited for: 7 -> 9; matrix products, arithmetic and copies ran while one was open for 1% -> 0% of each run, Pallas kernels for 9% -> 9%
where the time goes in v2:
time: 95.5 us; the launch traced here: 95.3 us
  starting transfers between devices  49.9 us (52%)
  waiting for transfers between devices  30.1 us (32%)
  Pallas kernels  10.1 us (11%)
  local copies, waits for them, and re-layouts  4.37 us (5%)
    ppermute x8, starting transfers between devices, move_zy(): return lax.ppermute(v, ('section', 'expert'), pairs)  16.6 us
    ppermute x8, starting transfers between devices, move_x(): lax.ppermute(v, 'expert', [(y * NX + x, y * NX + (x + d) % NX) for y in r...  11.5 us
    ppermute x4, starting transfers between devices, swap(): return lax.ppermute(v, 'dp', [(0, 1), (1, 0)])  10.2 us
    pallas_call x15, Pallas kernels, call(): pl.pallas_call(kernel, out_shape=outs, scratch_shapes=scratch, in_specs=i...  10.1 us
    ppermute x8, waiting for transfers between devices, move_x(): lax.ppermute(v, 'expert', [(y * NX + x, y * NX + (x + d) % NX) for y in r...  9.87 us
    ppermute x3, waiting for transfers between devices, move_y(): lax.ppermute(v, 'expert', [(y * NX + x, (y + d) % NY * NX + x) for y in r...  9.51 us
    ppermute x8, waiting for transfers between devices, move_zy(): return lax.ppermute(v, ('section', 'expert'), pairs)  9.51 us
    ppermute x3, starting transfers between devices, move_y(): lax.ppermute(v, 'expert', [(y * NX + x, (y + d) % NY * NX + x) for y in r...  5.96 us
  transfers between devices with their start and end apart: 25, of which 9 were waited for; matrix products, arithmetic and copies ran while one was open for 0% of the time, Pallas kernels for 9%

profile of v2, /device:TPU:1, one launch (start us, length us, event | category | flops | bytes accessed | tf_op | source)
XLA Modules:
  0.0 95.3 jit_solution(548522592565399171)
XLA Ops:
  0.6 2.1 %collective-permute-start.4 = (bf16[1792,256]{1,0:T(8,128)(2,1)}, bf16[1792,256]{1,0:T(8,128)(2,1)S(1)}, u32[]{:S(2)}, u32[]{:S(2)}) collective-permute-start(bf16[1792,256]{1,0:T(8,128)(2,1)} %bitcast.10), channel_id=1, source_target_pairs={{0,2},{2,4},{4,6},{6,0},{8,10},{10,12},{12,14},{14,8},{16,18},{18,... | collective-permute-start | bytes 2752520 | tf_op jit(solution)/shard_map/ppermute | solution.py:27
  2.8 1.4 %collective-permute-start.5 = (bf16[1792,256]{1,0:T(8,128)(2,1)}, bf16[1792,256]{1,0:T(8,128)(2,1)S(1)}, u32[]{:S(2)}, u32[]{:S(2)}) collective-permute-start(bf16[1792,256]{1,0:T(8,128)(2,1)} %bitcast.11), channel_id=1, source_target_pairs={{0,6},{2,0},{4,2},{6,4},{8,14},{10,8},{12,10},{14,12},{16,22},{18,... | collective-permute-start | bytes 2752520 | tf_op jit(solution)/shard_map/ppermute | solution.py:27
  4.1 1.0 %copy-done.2 = bf16[1,128,1792]{2,1,0:T(8,128)(2,1)S(1)} copy-done((bf16[1,128,1792]{2,1,0:T(8,128)(2,1)S(1)}, bf16[1,128,1792]{2,1,0:T(8,128)(2,1)}, u32[]{:S(2)}) %copy-start.2) | copy-done | bytes 458776
  5.1 1.0 %copy-done.3 = bf16[1,1,128,1792]{3,2,1,0:T(8,128)(2,1)S(1)} copy-done((bf16[1,1,128,1792]{3,2,1,0:T(8,128)(2,1)S(1)}, bf16[1,1,128,1792]{3,2,1,0:T(8,128)(2,1)}, u32[]{:S(2)}) %copy-start.3) | copy-done | bytes 458776
  6.2 1.0 %copy-done.4 = bf16[1,128,1792]{2,1,0:T(8,128)(2,1)S(1)} copy-done((bf16[1,128,1792]{2,1,0:T(8,128)(2,1)S(1)}, bf16[1,128,1792]{2,1,0:T(8,128)(2,1)}, u32[]{:S(2)}) %copy-start.4) | copy-done | bytes 458776
  7.2 0.7 copy-done.5
  7.8 0.7 copy-done.6
  8.5 1.6 %shard_map.87 = (bf16[128,1792]{1,0:T(8,128)(2,1)S(1)}, bf16[128,1792]{1,0:T(8,128)(2,1)S(1)}, bf16[128,1792]{1,0:T(8,128)(2,1)S(1)}, bf16[128,1792]{1,0:T(8,128)(2,1)S(1)}) custom-call(s32[1]{0:T(128)} %bitcast.y_ref, s32[1,128]{1,0:T(1,128)S(1)} %bitcast.21, s32[1,128]{1,0:T(1,128)S(1)} %bitcast.23, bf16[128,1792]{1,0:T(8,128)(2,1)S(1)} %bitcast.18, ...), custom_call_target="tpu_custom_call" | custom-call | flops 220200960 | bytes 3211264 | tf_op jit(solution)/shard_map/pallas_call | solution.py:58
  10.1 3.1 %collective-permute-start.2 = (bf16[128,1792]{1,0:T(8,128)(2,1)S(1)}, bf16[128,1792]{1,0:T(8,128)(2,1)S(1)}, u32[]{:S(2)}, u32[]{:S(2)}) collective-permute-start(bf16[128,1792]{1,0:T(8,128)(2,1)S(1)} %get-tuple-element.25), channel_id=1, source_target_pairs={{0,16},{2,18},{4,20},{6,22},{8,24},{10,26},{12,28},{14,30},{16,0},... | collective-permute-start | bytes 1376264 | tf_op jit(solution)/shard_map/ppermute | solution.py:33
  13.2 1.6 %collective-permute-start = (s32[1,128]{1,0:T(1,128)S(1)}, s32[1,128]{1,0:T(1,128)S(1)}, u32[]{:S(2)}, u32[]{:S(2)}) collective-permute-start(s32[1,128]{1,0:T(1,128)S(1)} %bitcast.22), channel_id=1, source_target_pairs={{0,32},{32,64},{64,96},{96,128},{128,160},{160,192},{192,224},{224... | collective-permute-start | bytes 1544 | tf_op jit(solution)/shard_map/ppermute | solution.py:39
  14.9 3.9 %collective-permute-start.1 = (s32[1,128]{1,0:T(1,128)S(1)}, s32[1,128]{1,0:T(1,128)S(1)}, u32[]{:S(2)}, u32[]{:S(2)}) collective-permute-start(s32[1,128]{1,0:T(1,128)S(1)} %bitcast.24), channel_id=1, source_target_pairs={{0,224},{32,0},{64,32},{96,64},{128,96},{160,128},{192,160},{224,1... | collective-permute-start | bytes 1544 | tf_op jit(solution)/shard_map/ppermute | solution.py:39
  18.8 1.2 %collective-permute-done.ids_f = s32[1,128]{1,0:T(1,128)S(1)} collective-permute-done((s32[1,128]{1,0:T(1,128)S(1)}, s32[1,128]{1,0:T(1,128)S(1)}, u32[]{:S(2)}, u32[]{:S(2)}) %collective-permute-start) | collective-permute-done | bytes 544 | tf_op jit(solution)/shard_map/ppermute | solution.py:39
  20.0 0.0 collective-permute-start.10
  20.0 0.0 collective-permute-done.1.ids_b
  20.0 2.7 %collective-permute-start.11 = (bf16[256,1792]{1,0:T(8,128)(2,1)S(1)}, bf16[256,1792]{1,0:T(8,128)(2,1)S(1)}, u32[]{:S(2)}, u32[]{:S(2)}) collective-permute-start(bf16[256,1792]{1,0:T(8,128)(2,1)S(1)} %bitcast.15), channel_id=1, source_target_pairs={{0,6},{2,0},{4,2},{6,4},{8,14},{10,8},{12,10},{14,12},{16,22},{18,... | collective-permute-start | bytes 2752520 | tf_op jit(solution)/shard_map/ppermute | solution.py:27
  22.7 0.2 shard_map.86
  22.9 0.3 shard_map.88
  23.2 1.1 %collective-permute-start.3 = (bf16[128,1792]{1,0:T(8,128)(2,1)S(1)}, bf16[128,1792]{1,0:T(8,128)(2,1)S(1)}, u32[]{:S(2)}, u32[]{:S(2)}) collective-permute-start(bf16[128,1792]{1,0:T(8,128)(2,1)S(1)} %shard_map.88), channel_id=1, source_target_pairs={{0,8},{2,10},{4,12},{6,14},{8,16},{10,18},{12,20},{14,22},{16,24},... | collective-permute-start | bytes 1376264 | tf_op jit(solution)/shard_map/ppermute | solution.py:33
  24.2 0.0 collective-permute-done.4.left.refs_1_.u1
  24.2 0.1 shard_map.89
  24.3 9.5 %collective-permute-done.3.refs_0_.r1 = bf16[128,1792]{1,0:T(8,128)(2,1)S(1)} collective-permute-done((bf16[128,1792]{1,0:T(8,128)(2,1)S(1)}, bf16[128,1792]{1,0:T(8,128)(2,1)S(1)}, u32[]{:S(2)}, u32[]{:S(2)}) %collective-permute-start.3) | collective-permute-done | bytes 458784 | tf_op jit(solution)/shard_map/ppermute | solution.py:33
  33.8 0.3 shard_map.90
  34.1 0.0 copy-start
  34.1 1.8 %collective-permute-start.6 = (bf16[128,1792]{1,0:T(8,128)(2,1)S(1)}, bf16[128,1792]{1,0:T(8,128)(2,1)S(1)}, u32[]{:S(2)}, u32[]{:S(2)}) collective-permute-start(bf16[128,1792]{1,0:T(8,128)(2,1)S(1)} %shard_map.90), channel_id=1, source_target_pairs={{0,24},{2,26},{4,28},{6,30},{8,0},{10,2},{12,4},{14,6},{16,8},{18,... | collective-permute-start | bytes 1376264 | tf_op jit(solution)/shard_map/ppermute | solution.py:33
  35.9 0.0 collective-permute-start.7
  35.9 2.7 %collective-permute-start.8 = (bf16[896,256]{1,0:T(8,128)(2,1)S(1)}, bf16[896,256]{1,0:T(8,128)(2,1)S(1)}, u32[]{:S(2)}, u32[]{:S(2)}) collective-permute-start(bf16[896,256]{1,0:T(8,128)(2,1)S(1)} %get-tuple-element.28), channel_id=1, source_target_pairs={{0,6},{2,0},{4,2},{6,4},{8,14},{10,8},{12,10},{14,12},{16,22},{18,... | collective-permute-start | bytes 1376264 | tf_op jit(solution)/shard_map/ppermute | solution.py:27
  38.6 4.8 %collective-permute-done.10.left.refs_1_.v1 = bf16[256,1792]{1,0:T(8,128)(2,1)S(1)} collective-permute-done((bf16[256,1792]{1,0:T(8,128)(2,1)S(1)}, bf16[256,1792]{1,0:T(8,128)(2,1)S(1)}, u32[]{:S(2)}, u32[]{:S(2)}) %collective-permute-start.10) | collective-permute-done | bytes 917536 | tf_op jit(solution)/shard_map/ppermute | solution.py:27
  43.4 0.0 collective-permute-done.11.right.refs_2_.v2
  43.4 0.1 shard_map.92
  43.5 0.0 collective-permute-done.6.r3
  43.5 1.1 %shard_map.93.token.pu = bf16[320,768]{1,0:T(8,128)(2,1)S(1)} custom-call(bf16[128,1792]{1,0:T(8,128)(2,1)S(1)} %get-tuple-element.23.r0, bf16[128,1792]{1,0:T(8,128)(2,1)S(1)} %collective-permute-done.3.refs_0_.r1, bf16[128,1792]{1,0:T(8,128)(2,1)S(1)} %collective-permute-done.2.refs_0_.r2, bf16[128,1792]{1,0:T(8,128)(2,1)S(1)} %collective-permute-done.6.r3, ...), custom_call_target="tpu_custom_call" | custom-call | flops 880803840 | bytes 4194304 | tf_op jit(solution)/shard_map/pallas_call | solution.py:58
  44.6 3.9 %collective-permute-start.14 = (bf16[320,768]{1,0:T(8,128)(2,1)S(1)}, bf16[320,768]{1,0:T(8,128)(2,1)S(1)}, u32[]{:S(2)}, u32[]{:S(2)}) collective-permute-start(bf16[320,768]{1,0:T(8,128)(2,1)S(1)} %shard_map.93.token.pu), channel_id=1, source_target_pairs={{0,1},{1,0},{2,3},{3,2},{4,5},{5,4},{6,7},{7,6},{8,9},{9,8},{10,11... | collective-permute-start | bytes 1474568 | tf_op jit(solution)/shard_map/ppermute | solution.py:54
  48.5 0.9 collective-permute-start.12
  49.3 1.8 %collective-permute-start.13 = (bf16[128,1792]{1,0:T(8,128)(2,1)S(1)}, bf16[128,1792]{1,0:T(8,128)(2,1)S(1)}, u32[]{:S(2)}, u32[]{:S(2)}) collective-permute-start(bf16[128,1792]{1,0:T(8,128)(2,1)S(1)} %get-tuple-element.30), channel_id=1, source_target_pairs={{0,6},{2,0},{4,2},{6,4},{8,14},{10,8},{12,10},{14,12},{16,22},{18,... | collective-permute-start | bytes 1376264 | tf_op jit(solution)/shard_map/ppermute | solution.py:27
  51.1 1.1 %shard_map.94.pv = bf16[192,768]{1,0:T(8,128)(2,1)S(1)} custom-call(bf16[128,1792]{1,0:T(8,128)(2,1)S(1)} %get-tuple-element.23.r0, bf16[128,1792]{1,0:T(8,128)(2,1)S(1)} %collective-permute-done.3.refs_0_.r1, bf16[128,1792]{1,0:T(8,128)(2,1)S(1)} %collective-permute-done.2.refs_0_.r2, bf16[128,1792]{1,0:T(8,128)(2,1)S(1)} %collective-permute-done.6.r3, ...), custom_call_target="tpu_custom_call" | custom-call | flops 587202560 | bytes 4194304 | tf_op jit(solution)/shard_map/pallas_call | solution.py:58
  52.2 1.0 %collective-permute-done.7.wa.ua = bf16[896,256]{1,0:T(8,128)(2,1)S(1)} collective-permute-done((bf16[896,256]{1,0:T(8,128)(2,1)S(1)}, bf16[896,256]{1,0:T(8,128)(2,1)S(1)}, u32[]{:S(2)}, u32[]{:S(2)}) %collective-permute-start.7) | collective-permute-done | bytes 458784 | tf_op jit(solution)/shard_map/ppermute | solution.py:27
  53.2 3.2 %collective-permute-start.15 = (bf16[192,768]{1,0:T(8,128)(2,1)S(1)}, bf16[192,768]{1,0:T(8,128)(2,1)S(1)}, u32[]{:S(2)}, u32[]{:S(2)}) collective-permute-start(bf16[192,768]{1,0:T(8,128)(2,1)S(1)} %shard_map.94.pv), channel_id=1, source_target_pairs={{0,1},{1,0},{2,3},{3,2},{4,5},{5,4},{6,7},{7,6},{8,9},{9,8},{10,11... | collective-permute-start | bytes 884744 | tf_op jit(solution)/shard_map/ppermute | solution.py:54
  56.4 0.0 collective-permute-done.8.wb.ub
  56.4 0.5 shard_map.91.pu
  56.9 0.7 collective-permute-start.9
  57.6 0.0 collective-permute-done.15.qv
  57.6 0.0 collective-permute-done.14.qu
  57.6 1.4 %shard_map.95 = (f32[160,1792]{1,0:T(8,128)S(1)}, f32[160,1792]{1,0:T(8,128)S(1)}) custom-call(bf16[128,1792]{1,0:T(8,128)(2,1)S(1)} %get-tuple-element.23.r0, bf16[128,1792]{1,0:T(8,128)(2,1)S(1)} %collective-permute-done.3.refs_0_.r1, bf16[128,1792]{1,0:T(8,128)(2,1)S(1)} %collective-permute-done.2.refs_0_.r2, ...), custom_call_target="tpu_custom_call" | custom-call | flops 880803840 | bytes 8388608 | tf_op jit(solution)/shard_map/pallas_call | solution.py:58
  59.1 4.0 %collective-permute-done.12.refs_0_.va = bf16[128,1792]{1,0:T(8,128)(2,1)S(1)} collective-permute-done((bf16[128,1792]{1,0:T(8,128)(2,1)S(1)}, bf16[128,1792]{1,0:T(8,128)(2,1)S(1)}, u32[]{:S(2)}, u32[]{:S(2)}) %collective-permute-start.12) | collective-permute-done | bytes 458784 | tf_op jit(solution)/shard_map/ppermute | solution.py:27
  63.1 0.5 shard_map.96.token.pv
  63.6 0.0 collective-permute-done.9.qu
  63.6 0.5 shard_map.97
  64.1 2.2 %collective-permute-start.16 = (bf16[40,1792]{1,0:T(8,128)(2,1)S(1)}, bf16[40,1792]{1,0:T(8,128)(2,1)S(1)}, u32[]{:S(2)}, u32[]{:S(2)}) collective-permute-start(bf16[40,1792]{1,0:T(8,128)(2,1)S(1)} %get-tuple-element.33), channel_id=1, source_target_pairs={{0,32},{2,34},{4,36},{6,38},{8,40},{10,42},{12,44},{14,46},{16,48}... | collective-permute-start | bytes 430088 | tf_op jit(solution)/shard_map/ppermute | solution.py:50
  66.2 4.1 %collective-permute-start.17 = (bf16[40,1792]{1,0:T(8,128)(2,1)S(1)}, bf16[40,1792]{1,0:T(8,128)(2,1)S(1)}, u32[]{:S(2)}, u32[]{:S(2)}) collective-permute-start(bf16[40,1792]{1,0:T(8,128)(2,1)S(1)} %get-tuple-element.34), channel_id=1, source_target_pairs={{0,56},{2,58},{4,60},{6,62},{8,32},{10,34},{12,36},{14,38},{16,40}... | collective-permute-start | bytes 430088 | tf_op jit(solution)/shard_map/ppermute | solution.py:50
  70.3 1.7 %collective-permute-start.18 = (bf16[40,1792]{1,0:T(8,128)(2,1)S(1)}, bf16[40,1792]{1,0:T(8,128)(2,1)S(1)}, u32[]{:S(2)}, u32[]{:S(2)}) collective-permute-start(bf16[40,1792]{1,0:T(8,128)(2,1)S(1)} %get-tuple-element.35.token), channel_id=1, source_target_pairs={{0,48},{2,50},{4,52},{6,54},{8,56},{10,58},{12,60},{14,62},{16,32}... | collective-permute-start | bytes 430088 | tf_op jit(solution)/shard_map/ppermute | solution.py:50
  72.0 2.4 %collective-permute-start.20 = (bf16[192,256]{1,0:T(8,128)(2,1)S(1)}, bf16[192,256]{1,0:T(8,128)(2,1)S(1)}, u32[]{:S(2)}, u32[]{:S(2)}) collective-permute-start(bf16[192,256]{1,0:T(8,128)(2,1)S(1)} %shard_map.96.token.pv), channel_id=1, source_target_pairs={{0,1},{1,0},{2,3},{3,2},{4,5},{5,4},{6,7},{7,6},{8,9},{9,8},{10,11... | collective-permute-start | bytes 294920 | tf_op jit(solution)/shard_map/ppermute | solution.py:54
  74.4 3.3 %collective-permute-start.19 = (bf16[40,1792]{1,0:T(8,128)(2,1)S(1)}, bf16[40,1792]{1,0:T(8,128)(2,1)S(1)}, u32[]{:S(2)}, u32[]{:S(2)}) collective-permute-start(bf16[40,1792]{1,0:T(8,128)(2,1)S(1)} %get-tuple-element.36), channel_id=1, source_target_pairs={{0,40},{2,42},{4,44},{6,46},{8,48},{10,50},{12,52},{14,54},{16,56}... | collective-permute-start | bytes 430088 | tf_op jit(solution)/shard_map/ppermute | solution.py:50
  77.7 0.0 collective-permute-done.20.qv
  77.7 0.5 shard_map.99
  78.1 0.1 collective-permute-start.21
  78.2 1.6 %collective-permute-start.22 = (bf16[40,1792]{1,0:T(8,128)(2,1)S(1)}, bf16[40,1792]{1,0:T(8,128)(2,1)S(1)}, u32[]{:S(2)}, u32[]{:S(2)}) collective-permute-start(bf16[40,1792]{1,0:T(8,128)(2,1)S(1)} %get-tuple-element.39), channel_id=1, source_target_pairs={{0,248},{2,250},{4,252},{6,254},{8,224},{10,226},{12,228},{14,230}... | collective-permute-start | bytes 430088 | tf_op jit(solution)/shard_map/ppermute | solution.py:50
  79.9 1.4 %collective-permute-start.23 = (bf16[40,1792]{1,0:T(8,128)(2,1)S(1)}, bf16[40,1792]{1,0:T(8,128)(2,1)S(1)}, u32[]{:S(2)}, u32[]{:S(2)}) collective-permute-start(bf16[40,1792]{1,0:T(8,128)(2,1)S(1)} %get-tuple-element.40), channel_id=1, source_target_pairs={{0,240},{2,242},{4,244},{6,246},{8,248},{10,250},{12,252},{14,254}... | collective-permute-start | bytes 430088 | tf_op jit(solution)/shard_map/ppermute | solution.py:50
  81.2 2.4 %collective-permute-start.24 = (bf16[40,1792]{1,0:T(8,128)(2,1)S(1)}, bf16[40,1792]{1,0:T(8,128)(2,1)S(1)}, u32[]{:S(2)}, u32[]{:S(2)}) collective-permute-start(bf16[40,1792]{1,0:T(8,128)(2,1)S(1)} %get-tuple-element.41), channel_id=1, source_target_pairs={{0,232},{2,234},{4,236},{6,238},{8,240},{10,242},{12,244},{14,246}... | collective-permute-start | bytes 430088 | tf_op jit(solution)/shard_map/ppermute | solution.py:50
  83.6 0.7 collective-permute-done.19.f3
  84.3 1.1 %shard_map.98 = bf16[128,1792]{1,0:T(8,128)(2,1)} custom-call(bf16[160,128]{1,0:T(8,128)(2,1)S(1)} %get-tuple-element.22.refs_1_.table, bf16[40,1792]{1,0:T(8,128)(2,1)S(1)} %collective-permute-done.16.f0, bf16[40,1792]{1,0:T(8,128)(2,1)S(1)} %collective-permute-done.17.f1, bf16[40,1792]{1,0:T(8,128)(2,1)S(1)} %collective-permute-done.18.f2, ...), custom_call_target="tpu_custom_call" | custom-call | flops 73400320 | bytes 2097152 | tf_op jit(solution)/shard_map/pallas_call | solution.py:58
  85.4 2.2 %collective-permute-done.22.f1 = bf16[40,1792]{1,0:T(8,128)(2,1)S(1)} collective-permute-done((bf16[40,1792]{1,0:T(8,128)(2,1)S(1)}, bf16[40,1792]{1,0:T(8,128)(2,1)S(1)}, u32[]{:S(2)}, u32[]{:S(2)}) %collective-permute-start.22) | collective-permute-done | bytes 143392 | tf_op jit(solution)/shard_map/ppermute | solution.py:50
  87.7 3.4 %collective-permute-done.23.f2 = bf16[40,1792]{1,0:T(8,128)(2,1)S(1)} collective-permute-done((bf16[40,1792]{1,0:T(8,128)(2,1)S(1)}, bf16[40,1792]{1,0:T(8,128)(2,1)S(1)}, u32[]{:S(2)}, u32[]{:S(2)}) %collective-permute-start.23) | collective-permute-done | bytes 143392 | tf_op jit(solution)/shard_map/ppermute | solution.py:50
  91.1 3.1 %collective-permute-done.24.f3 = bf16[40,1792]{1,0:T(8,128)(2,1)S(1)} collective-permute-done((bf16[40,1792]{1,0:T(8,128)(2,1)S(1)}, bf16[40,1792]{1,0:T(8,128)(2,1)S(1)}, u32[]{:S(2)}, u32[]{:S(2)}) %collective-permute-start.24) | collective-permute-done | bytes 143392 | tf_op jit(solution)/shard_map/ppermute | solution.py:50
  94.2 1.1 %shard_map.100 = bf16[128,1792]{1,0:T(8,128)(2,1)} custom-call(bf16[160,128]{1,0:T(8,128)(2,1)S(1)} %get-tuple-element.37.table, bf16[40,1792]{1,0:T(8,128)(2,1)S(1)} %collective-permute-done.21.f0, bf16[40,1792]{1,0:T(8,128)(2,1)S(1)} %collective-permute-done.22.f1, bf16[40,1792]{1,0:T(8,128)(2,1)S(1)} %collective-permute-done.23.f2, ...), custom_call_target="tpu_custom_call" | custom-call | flops 73400320 | bytes 2097152 | tf_op jit(solution)/shard_map/pallas_call | solution.py:58
  (15 shorter events, 0.0 us)
Async XLA Ops:
  0.6 19.4 %copy-start.1 = (bf16[1,1,256,1792]{3,2,1,0:T(8,128)(2,1)S(1)}, bf16[1,1,256,1792]{3,2,1,0:T(8,128)(2,1)}, u32[]{:S(2)}) copy-start(bf16[1,1,256,1792]{3,2,1,0:T(8,128)(2,1)} %param.13) | copy-start | bytes 2752516
  0.6 23.6 %collective-permute-start.4 = (bf16[1792,256]{1,0:T(8,128)(2,1)}, bf16[1792,256]{1,0:T(8,128)(2,1)S(1)}, u32[]{:S(2)}, u32[]{:S(2)}) collective-permute-start(bf16[1792,256]{1,0:T(8,128)(2,1)} %bitcast.10), channel_id=1, source_target_pairs={{0,2},{2,4},{4,6},{6,0},{8,10},{10,12},{12,14},{14,8},{16,18},{18,... | collective-permute-start | bytes 2752520 | tf_op jit(solution)/shard_map/ppermute | solution.py:27
  2.8 21.5 %collective-permute-start.5 = (bf16[1792,256]{1,0:T(8,128)(2,1)}, bf16[1792,256]{1,0:T(8,128)(2,1)S(1)}, u32[]{:S(2)}, u32[]{:S(2)}) collective-permute-start(bf16[1792,256]{1,0:T(8,128)(2,1)} %bitcast.11), channel_id=1, source_target_pairs={{0,6},{2,0},{4,2},{6,4},{8,14},{10,8},{12,10},{14,12},{16,22},{18,... | collective-permute-start | bytes 2752520 | tf_op jit(solution)/shard_map/ppermute | solution.py:27
  4.1 1.0 %copy-start.2 = (bf16[1,128,1792]{2,1,0:T(8,128)(2,1)S(1)}, bf16[1,128,1792]{2,1,0:T(8,128)(2,1)}, u32[]{:S(2)}) copy-start(bf16[1,128,1792]{2,1,0:T(8,128)(2,1)} %param.7) | copy-start | bytes 1376260
  5.1 1.0 %copy-start.3 = (bf16[1,1,128,1792]{3,2,1,0:T(8,128)(2,1)S(1)}, bf16[1,1,128,1792]{3,2,1,0:T(8,128)(2,1)}, u32[]{:S(2)}) copy-start(bf16[1,1,128,1792]{3,2,1,0:T(8,128)(2,1)} %param.10) | copy-start | bytes 1376260
  6.2 1.0 %copy-start.4 = (bf16[1,128,1792]{2,1,0:T(8,128)(2,1)S(1)}, bf16[1,128,1792]{2,1,0:T(8,128)(2,1)}, u32[]{:S(2)}) copy-start(bf16[1,128,1792]{2,1,0:T(8,128)(2,1)} %param.9) | copy-start | bytes 1376260
  7.2 0.7 copy-start.5
  7.8 0.7 copy-start.6
  10.1 12.8 %collective-permute-start.2 = (bf16[128,1792]{1,0:T(8,128)(2,1)S(1)}, bf16[128,1792]{1,0:T(8,128)(2,1)S(1)}, u32[]{:S(2)}, u32[]{:S(2)}) collective-permute-start(bf16[128,1792]{1,0:T(8,128)(2,1)S(1)} %get-tuple-element.25), channel_id=1, source_target_pairs={{0,16},{2,18},{4,20},{6,22},{8,24},{10,26},{12,28},{14,30},{16,0},... | collective-permute-start | bytes 1376264 | tf_op jit(solution)/shard_map/ppermute | solution.py:33
  13.2 6.8 %collective-permute-start = (s32[1,128]{1,0:T(1,128)S(1)}, s32[1,128]{1,0:T(1,128)S(1)}, u32[]{:S(2)}, u32[]{:S(2)}) collective-permute-start(s32[1,128]{1,0:T(1,128)S(1)} %bitcast.22), channel_id=1, source_target_pairs={{0,32},{32,64},{64,96},{96,128},{128,160},{160,192},{192,224},{224... | collective-permute-start | bytes 1544 | tf_op jit(solution)/shard_map/ppermute | solution.py:39
  14.9 5.2 %collective-permute-start.1 = (s32[1,128]{1,0:T(1,128)S(1)}, s32[1,128]{1,0:T(1,128)S(1)}, u32[]{:S(2)}, u32[]{:S(2)}) collective-permute-start(s32[1,128]{1,0:T(1,128)S(1)} %bitcast.24), channel_id=1, source_target_pairs={{0,224},{32,0},{64,32},{96,64},{128,96},{160,128},{192,160},{224,1... | collective-permute-start | bytes 1544 | tf_op jit(solution)/shard_map/ppermute | solution.py:39
  20.0 23.4 %collective-permute-start.10 = (bf16[256,1792]{1,0:T(8,128)(2,1)S(1)}, bf16[256,1792]{1,0:T(8,128)(2,1)S(1)}, u32[]{:S(2)}, u32[]{:S(2)}) collective-permute-start(bf16[256,1792]{1,0:T(8,128)(2,1)S(1)} %bitcast.14), channel_id=1, source_target_pairs={{0,2},{2,4},{4,6},{6,0},{8,10},{10,12},{12,14},{14,8},{16,18},{18,... | collective-permute-start | bytes 2752520 | tf_op jit(solution)/shard_map/ppermute | solution.py:27
  20.0 23.4 %collective-permute-start.11 = (bf16[256,1792]{1,0:T(8,128)(2,1)S(1)}, bf16[256,1792]{1,0:T(8,128)(2,1)S(1)}, u32[]{:S(2)}, u32[]{:S(2)}) collective-permute-start(bf16[256,1792]{1,0:T(8,128)(2,1)S(1)} %bitcast.15), channel_id=1, source_target_pairs={{0,6},{2,0},{4,2},{6,4},{8,14},{10,8},{12,10},{14,12},{16,22},{18,... | collective-permute-start | bytes 2752520 | tf_op jit(solution)/shard_map/ppermute | solution.py:27
  23.2 10.7 %collective-permute-start.3 = (bf16[128,1792]{1,0:T(8,128)(2,1)S(1)}, bf16[128,1792]{1,0:T(8,128)(2,1)S(1)}, u32[]{:S(2)}, u32[]{:S(2)}) collective-permute-start(bf16[128,1792]{1,0:T(8,128)(2,1)S(1)} %shard_map.88), channel_id=1, source_target_pairs={{0,8},{2,10},{4,12},{6,14},{8,16},{10,18},{12,20},{14,22},{16,24},... | collective-permute-start | bytes 1376264 | tf_op jit(solution)/shard_map/ppermute | solution.py:33
  34.1 9.4 %copy-start = (bf16[1,1,1792,256]{3,2,1,0:T(8,128)(2,1)S(1)}, bf16[1,1,1792,256]{3,2,1,0:T(8,128)(2,1)}, u32[]{:S(2)}) copy-start(bf16[1,1,1792,256]{3,2,1,0:T(8,128)(2,1)} %param.12) | copy-start | bytes 2752516
  34.1 9.4 %collective-permute-start.6 = (bf16[128,1792]{1,0:T(8,128)(2,1)S(1)}, bf16[128,1792]{1,0:T(8,128)(2,1)S(1)}, u32[]{:S(2)}, u32[]{:S(2)}) collective-permute-start(bf16[128,1792]{1,0:T(8,128)(2,1)S(1)} %shard_map.90), channel_id=1, source_target_pairs={{0,24},{2,26},{4,28},{6,30},{8,0},{10,2},{12,4},{14,6},{16,8},{18,... | collective-permute-start | bytes 1376264 | tf_op jit(solution)/shard_map/ppermute | solution.py:33
  35.9 17.3 %collective-permute-start.7 = (bf16[896,256]{1,0:T(8,128)(2,1)S(1)}, bf16[896,256]{1,0:T(8,128)(2,1)S(1)}, u32[]{:S(2)}, u32[]{:S(2)}) collective-permute-start(bf16[896,256]{1,0:T(8,128)(2,1)S(1)} %get-tuple-element.27.refs_1_), channel_id=1, source_target_pairs={{0,2},{2,4},{4,6},{6,0},{8,10},{10,12},{12,14},{14,8},{16,18},{18,... | collective-permute-start | bytes 1376264 | tf_op jit(solution)/shard_map/ppermute | solution.py:27
  35.9 20.5 %collective-permute-start.8 = (bf16[896,256]{1,0:T(8,128)(2,1)S(1)}, bf16[896,256]{1,0:T(8,128)(2,1)S(1)}, u32[]{:S(2)}, u32[]{:S(2)}) collective-permute-start(bf16[896,256]{1,0:T(8,128)(2,1)S(1)} %get-tuple-element.28), channel_id=1, source_target_pairs={{0,6},{2,0},{4,2},{6,4},{8,14},{10,8},{12,10},{14,12},{16,22},{18,... | collective-permute-start | bytes 1376264 | tf_op jit(solution)/shard_map/ppermute | solution.py:27
  44.6 13.1 %collective-permute-start.14 = (bf16[320,768]{1,0:T(8,128)(2,1)S(1)}, bf16[320,768]{1,0:T(8,128)(2,1)S(1)}, u32[]{:S(2)}, u32[]{:S(2)}) collective-permute-start(bf16[320,768]{1,0:T(8,128)(2,1)S(1)} %shard_map.93.token.pu), channel_id=1, source_target_pairs={{0,1},{1,0},{2,3},{3,2},{4,5},{5,4},{6,7},{7,6},{8,9},{9,8},{10,11... | collective-permute-start | bytes 1474568 | tf_op jit(solution)/shard_map/ppermute | solution.py:54
  48.5 14.6 %collective-permute-start.12 = (bf16[128,1792]{1,0:T(8,128)(2,1)S(1)}, bf16[128,1792]{1,0:T(8,128)(2,1)S(1)}, u32[]{:S(2)}, u32[]{:S(2)}) collective-permute-start(bf16[128,1792]{1,0:T(8,128)(2,1)S(1)} %get-tuple-element.29.token), channel_id=1, source_target_pairs={{0,2},{2,4},{4,6},{6,0},{8,10},{10,12},{12,14},{14,8},{16,18},{18,... | collective-permute-start | bytes 1376264 | tf_op jit(solution)/shard_map/ppermute | solution.py:27
  49.3 13.7 %collective-permute-start.13 = (bf16[128,1792]{1,0:T(8,128)(2,1)S(1)}, bf16[128,1792]{1,0:T(8,128)(2,1)S(1)}, u32[]{:S(2)}, u32[]{:S(2)}) collective-permute-start(bf16[128,1792]{1,0:T(8,128)(2,1)S(1)} %get-tuple-element.30), channel_id=1, source_target_pairs={{0,6},{2,0},{4,2},{6,4},{8,14},{10,8},{12,10},{14,12},{16,22},{18,... | collective-permute-start | bytes 1376264 | tf_op jit(solution)/shard_map/ppermute | solution.py:27
  53.2 4.4 %collective-permute-start.15 = (bf16[192,768]{1,0:T(8,128)(2,1)S(1)}, bf16[192,768]{1,0:T(8,128)(2,1)S(1)}, u32[]{:S(2)}, u32[]{:S(2)}) collective-permute-start(bf16[192,768]{1,0:T(8,128)(2,1)S(1)} %shard_map.94.pv), channel_id=1, source_target_pairs={{0,1},{1,0},{2,3},{3,2},{4,5},{5,4},{6,7},{7,6},{8,9},{9,8},{10,11... | collective-permute-start | bytes 884744 | tf_op jit(solution)/shard_map/ppermute | solution.py:54
  56.9 6.7 %collective-permute-start.9 = (bf16[320,256]{1,0:T(8,128)(2,1)S(1)}, bf16[320,256]{1,0:T(8,128)(2,1)S(1)}, u32[]{:S(2)}, u32[]{:S(2)}) collective-permute-start(bf16[320,256]{1,0:T(8,128)(2,1)S(1)} %shard_map.91.pu), channel_id=1, source_target_pairs={{0,1},{1,0},{2,3},{3,2},{4,5},{5,4},{6,7},{7,6},{8,9},{9,8},{10,11... | collective-permute-start | bytes 491528 | tf_op jit(solution)/shard_map/ppermute | solution.py:54
  64.1 14.2 %collective-permute-start.16 = (bf16[40,1792]{1,0:T(8,128)(2,1)S(1)}, bf16[40,1792]{1,0:T(8,128)(2,1)S(1)}, u32[]{:S(2)}, u32[]{:S(2)}) collective-permute-start(bf16[40,1792]{1,0:T(8,128)(2,1)S(1)} %get-tuple-element.33), channel_id=1, source_target_pairs={{0,32},{2,34},{4,36},{6,38},{8,40},{10,42},{12,44},{14,46},{16,48}... | collective-permute-start | bytes 430088 | tf_op jit(solution)/shard_map/ppermute | solution.py:50
  66.2 13.6 %collective-permute-start.17 = (bf16[40,1792]{1,0:T(8,128)(2,1)S(1)}, bf16[40,1792]{1,0:T(8,128)(2,1)S(1)}, u32[]{:S(2)}, u32[]{:S(2)}) collective-permute-start(bf16[40,1792]{1,0:T(8,128)(2,1)S(1)} %get-tuple-element.34), channel_id=1, source_target_pairs={{0,56},{2,58},{4,60},{6,62},{8,32},{10,34},{12,36},{14,38},{16,40}... | collective-permute-start | bytes 430088 | tf_op jit(solution)/shard_map/ppermute | solution.py:50
  70.3 10.9 %collective-permute-start.18 = (bf16[40,1792]{1,0:T(8,128)(2,1)S(1)}, bf16[40,1792]{1,0:T(8,128)(2,1)S(1)}, u32[]{:S(2)}, u32[]{:S(2)}) collective-permute-start(bf16[40,1792]{1,0:T(8,128)(2,1)S(1)} %get-tuple-element.35.token), channel_id=1, source_target_pairs={{0,48},{2,50},{4,52},{6,54},{8,56},{10,58},{12,60},{14,62},{16,32}... | collective-permute-start | bytes 430088 | tf_op jit(solution)/shard_map/ppermute | solution.py:50
  72.0 5.6 %collective-permute-start.20 = (bf16[192,256]{1,0:T(8,128)(2,1)S(1)}, bf16[192,256]{1,0:T(8,128)(2,1)S(1)}, u32[]{:S(2)}, u32[]{:S(2)}) collective-permute-start(bf16[192,256]{1,0:T(8,128)(2,1)S(1)} %shard_map.96.token.pv), channel_id=1, source_target_pairs={{0,1},{1,0},{2,3},{3,2},{4,5},{5,4},{6,7},{7,6},{8,9},{9,8},{10,11... | collective-permute-start | bytes 294920 | tf_op jit(solution)/shard_map/ppermute | solution.py:54
  74.4 10.0 %collective-permute-start.19 = (bf16[40,1792]{1,0:T(8,128)(2,1)S(1)}, bf16[40,1792]{1,0:T(8,128)(2,1)S(1)}, u32[]{:S(2)}, u32[]{:S(2)}) collective-permute-start(bf16[40,1792]{1,0:T(8,128)(2,1)S(1)} %get-tuple-element.36), channel_id=1, source_target_pairs={{0,40},{2,42},{4,44},{6,46},{8,48},{10,50},{12,52},{14,54},{16,56}... | collective-permute-start | bytes 430088 | tf_op jit(solution)/shard_map/ppermute | solution.py:50
  78.1 7.3 %collective-permute-start.21 = (bf16[40,1792]{1,0:T(8,128)(2,1)S(1)}, bf16[40,1792]{1,0:T(8,128)(2,1)S(1)}, u32[]{:S(2)}, u32[]{:S(2)}) collective-permute-start(bf16[40,1792]{1,0:T(8,128)(2,1)S(1)} %get-tuple-element.38), channel_id=1, source_target_pairs={{0,224},{2,226},{4,228},{6,230},{8,232},{10,234},{12,236},{14,238}... | collective-permute-start | bytes 430088 | tf_op jit(solution)/shard_map/ppermute | solution.py:50
  78.2 9.4 %collective-permute-start.22 = (bf16[40,1792]{1,0:T(8,128)(2,1)S(1)}, bf16[40,1792]{1,0:T(8,128)(2,1)S(1)}, u32[]{:S(2)}, u32[]{:S(2)}) collective-permute-start(bf16[40,1792]{1,0:T(8,128)(2,1)S(1)} %get-tuple-element.39), channel_id=1, source_target_pairs={{0,248},{2,250},{4,252},{6,254},{8,224},{10,226},{12,228},{14,230}... | collective-permute-start | bytes 430088 | tf_op jit(solution)/shard_map/ppermute | solution.py:50
  79.9 11.2 %collective-permute-start.23 = (bf16[40,1792]{1,0:T(8,128)(2,1)S(1)}, bf16[40,1792]{1,0:T(8,128)(2,1)S(1)}, u32[]{:S(2)}, u32[]{:S(2)}) collective-permute-start(bf16[40,1792]{1,0:T(8,128)(2,1)S(1)} %get-tuple-element.40), channel_id=1, source_target_pairs={{0,240},{2,242},{4,244},{6,246},{8,248},{10,250},{12,252},{14,254}... | collective-permute-start | bytes 430088 | tf_op jit(solution)/shard_map/ppermute | solution.py:50
  81.2 13.0 %collective-permute-start.24 = (bf16[40,1792]{1,0:T(8,128)(2,1)S(1)}, bf16[40,1792]{1,0:T(8,128)(2,1)S(1)}, u32[]{:S(2)}, u32[]{:S(2)}) collective-permute-start(bf16[40,1792]{1,0:T(8,128)(2,1)S(1)} %get-tuple-element.41), channel_id=1, source_target_pairs={{0,232},{2,234},{4,236},{6,238},{8,240},{10,242},{12,244},{14,246}... | collective-permute-start | bytes 430088 | tf_op jit(solution)/shard_map/ppermute | solution.py:50

commit v3 on v2

--- a/solution.py
+++ b/solution.py
@@ -20,6 +20,7 @@
 SM = pl.BlockSpec(memory_space=pltpu.SMEM)
 
 CU = 8 * 10**9
+CU2 = 6 * 10**9
 LIMIT = 24 * 1024 * 1024
 
 
@@ -54,13 +55,13 @@
     return lax.ppermute(v, "dp", [(0, 1), (1, 0)])
 
 
-def call(kernel, outs, flops, nbytes, in_specs, *args, scratch=()):
+def call(kernel, outs, flops, nbytes, in_specs, *args, scratch=(), out_specs=None):
     return pl.pallas_call(
         kernel,
         out_shape=outs,
         scratch_shapes=scratch,
         in_specs=in_specs,
-        out_specs=jax.tree.map(lambda _: VM, outs),
+        out_specs=out_specs or jax.tree.map(lambda _: VM, outs),
         compiler_params=pltpu.CompilerParams(vmem_limit_bytes=LIMIT),
         cost_estimate=pl.CostEstimate(flops=flops, bytes_accessed=nbytes, transcendentals=0),
     )(*args)
@@ -124,8 +125,15 @@
 
 
 def table_kernel(y_ref, ids_f, ids_b, out_f, out_b):
-    out_f[...] = slot_table(ids_f[...], y_ref[0])
-    out_b[...] = slot_table(ids_b[...], y_ref[0])
+    n = ids_f.shape[1]
+    eye = lax.broadcasted_iota(jnp.int32, (n, n), 0) == lax.broadcasted_iota(
+        jnp.int32, (n, n), 1
+    )
+    eye = eye.astype(F32)
+    for ids, out in ((ids_f, out_f), (ids_b, out_b)):
+        table = slot_table(ids[...], y_ref[0]).astype(F32)
+        for d in range(NY):
+            out[d] = nt(eye, table[d * CAP : (d + 1) * CAP]).astype(BF)
 
 
 def held_kernel(v_ref, *refs):
@@ -201,30 +209,50 @@
         acc_b[:, c] = b
 
 
-def last_f_kernel(pu, qu, va, vb, acc, token, *outs):
+def last_f_kernel(r0, r1, r2, r3, pu, qu, va, vb, acc, token, out, *outs):
+    rows = jnp.concatenate([r[2 * CAP : ROWS, :] for r in (r0, r1, r2, r3)], axis=0)
+    half = va.shape[0]
+    out[:, :half] = nt(rows, va[...]).astype(BF)
+    out[:, half:] = nt(rows, vb[...]).astype(BF)
     act = activate(added(pu[...], qu[...]))
-    half = va.shape[0]
     for c in columns(acc.shape[1]):
         t = acc[:, c] + nn(act[:, :half], va[:, c]) + nn(act[:, half:], vb[:, c])
         for i, o in enumerate(outs):
             o[:, c] = t[i * CAP : (i + 1) * CAP].astype(BF)
 
 
-def last_b_kernel(pu, qu, pv, qv, ua, ub, acc, token, *outs):
+def last_b_kernel(pu, qu, pv, qv, ua, ub, acc, token, *outs, parts):
     hid = grad_hidden(added(pu[...], qu[...]), added(pv[...], qv[...]))
     half = ua.shape[0]
     for u, base in ((ua, 0), (ub, half)):
         for c in columns(half, 128):
             o = slice(base + c.start, base + c.stop)
             t = acc[:, o] + nt(hid, u[c, :])
-            for i, out in enumerate(outs):
+            for i, out in zip(parts, outs):
                 out[:, o] = t[i * CAP : (i + 1) * CAP].astype(BF)
 
 
-def combine_kernel(table, f0, f1, f2, f3, out):
+def finish_kernel(table, token, total, *refs, parts):
+    *rows, out, held, sems = refs
+    copies = []
+    for i, c in enumerate(columns(out.shape[1])):
+        t = total[:, c]
+        for d, r in zip(parts, rows):
+            t += nn(table[d], r[:, c])
+        held[:, c] = t.astype(held.dtype)
+        copies.append(pltpu.make_async_copy(held.at[:, c], out.at[:, c], sems.at[i]))
+        copies[-1].start()
+    for c in copies:
+        c.wait()
+
+
+def combine_kernel(table, token, *refs, parts, first):
+    *rows, out = refs if first else refs[1:]
     for c in columns(out.shape[1]):
-        got = jnp.concatenate([f[:, c].astype(F32) for f in (f0, f1, f2, f3)], axis=0).astype(BF)
-        out[:, c] = tn(table[...], got).astype(BF)
+        t = 0.0 if first else refs[0][:, c]
+        for d, r in zip(parts, rows):
+            t += nn(table[d], r[:, c])
+        out[:, c] = t.astype(out.dtype)
 
 
 def per_device(
@@ -259,7 +287,7 @@
 
     ids_f, ids_b = move_z(ids_up, 1), move_z(ids_down, -1)
     table_f, table_b = call(
-        table_kernel, [sds((NY * CAP, n))] * 2, 0, 4 * NY * CAP * n, [SM, VM, VM], y, ids_f, ids_b
+        table_kernel, [sds((NY, n, CAP))] * 2, 0, 4 * NY * CAP * n, [SM, VM, VM], y, ids_f, ids_b
     )
 
     def held(v, cost, *tokens):
@@ -339,38 +367,26 @@
         v_l,
         v_r,
     )
-    pu2 = call(up_halves_kernel, sds((2 * CAP * NY, hp)), mm, 2 << 20, [VM] * 6, *rows, u_a, u_b)
+    pu2 = call(up_halves_kernel, sds((2 * CAP * NY, hp)), CU2, 2 << 20, [VM] * 6, *rows, u_a, u_b)
     qu2 = swap(pu2)
-    pv2 = call(
-        down_kernel,
-        sds(((ROWS - 2 * CAP) * NY, hp)),
-        mm // 2,
+    pv2, *res_f = call(
+        last_f_kernel,
+        [sds(((ROWS - 2 * CAP) * NY, hp))] + [sds((CAP, width))] * NY,
+        mm,
         2 << 20,
-        [VM] * 4 + [ANY] + [VM] * 2,
+        [VM] * 9 + [ANY],
         *rows,
-        acc_b,
-        v_a,
-        v_b,
-    )
-    qv2 = swap(pv2)
-    outs = [sds((CAP, width))] * NY
-    res_f = call(
-        last_f_kernel,
-        outs,
-        mm // 2,
-        2 << 20,
-        [VM] * 5 + [ANY],
         pu2,
         qu2,
         v_a,
         v_b,
         acc_f,
-        pv2,
-    )
-    got_f = [move_zy(r, 1, -d) for d, r in enumerate(res_f)]
+        acc_b,
+    )
+    qv2 = swap(pv2)
     res_b = call(
-        last_b_kernel,
-        outs,
+        functools.partial(last_b_kernel, parts=range(NY)),
+        [sds((CAP, width))] * NY,
         mm // 2,
         2 << 20,
         [VM] * 7 + [ANY],
@@ -381,14 +397,45 @@
         u_a,
         u_b,
         acc_b,
-        res_f[2],
-    )
+        res_f[0],
+    )
+    got_f = [move_zy(r, 1, -d) for d, r in enumerate(res_f)]
     got_b = [move_zy(r, -1, -d) for d, r in enumerate(res_b)]
-    final = functools.partial(
-        call, combine_kernel, sds((n, width)), 2 * 160 * 128 * width, 2 << 20, [VM] * 5
-    )
-    out_f = final(table_f, *got_f)
-    out_b = final(table_b, *got_b)
+
+    def combine(table, got, parts, total, token):
+        return call(
+            functools.partial(combine_kernel, parts=parts, first=total is None),
+            sds((n, width), F32),
+            2 * CAP * n * width * len(parts),
+            8 * n * width,
+            [VM, ANY] + [VM] * (len(parts) + (total is not None)),
+            table,
+            token,
+            *(() if total is None else (total,)),
+            *[got[d] for d in parts],
+        )
+
+    def finish(table, got, parts, total, token):
+        return call(
+            functools.partial(finish_kernel, parts=parts),
+            sds((n, width)),
+            2 * CAP * n * width * len(parts),
+            8 * n * width,
+            [VM, ANY] + [VM] * (len(parts) + 1),
+            table,
+            token,
+            total,
+            *[got[d] for d in parts],
+            scratch=[pltpu.VMEM((n, width), BF), pltpu.SemaphoreType.DMA((width // 256,))],
+            out_specs=ANY,
+        )
+
+    sum_f = combine(table_f, got_f, (0, 2), None, table_b)
+    sum_b = combine(table_b, got_b, (0,), None, sum_f)
+    sum_f = combine(table_f, got_f, (1,), sum_f, sum_b)
+    out_f = finish(table_f, got_f, (3,), sum_f, sum_b)
+    sum_b = combine(table_b, got_b, (2, 1), sum_b, sum_f)
+    out_b = finish(table_b, got_b, (3,), sum_b, sum_f)
     return (out_f[None], out_b[None])
 
 

time: 95.5 us -> 94.1 us (0.985)
  waiting for transfers between devices: 30.1 us -> 27.7 us
  Pallas kernels: 10.1 us -> 11.3 us
    ppermute x8, waiting for transfers between devices: 9.51 us -> 7.53 us  [move_zy(): return lax.ppermute(v, ('section', 'expert'), pairs)]
    pallas_call x15 -> x18, Pallas kernels: 10.1 us -> 11.3 us  [call(): pl.pallas_call(kernel, out_shape=outs, scratch_shapes=scratch, in_specs=i...]
  transfers between devices with their start and end apart: 25 -> 25, of which waited for: 9 -> 8; matrix products, arithmetic and copies ran while one was open for 0% -> 0% of each run, Pallas kernels for 9% -> 10%
where the time goes in v3:
time: 94.1 us; the launch traced here: 93.4 us
  starting transfers between devices  49 us (52%)
  waiting for transfers between devices  27.7 us (29%)
  Pallas kernels  11.3 us (12%)
  local copies, waits for them, and re-layouts  4.37 us (5%)
  between operations  0.98 us (1%)
    ppermute x8, starting transfers between devices, move_zy(): return lax.ppermute(v, ('section', 'expert'), pairs)  16 us
    ppermute x8, starting transfers between devices, move_x(): lax.ppermute(v, 'expert', [(y * NX + x, y * NX + (x + d) % NX) for y in r...  11.6 us
    pallas_call x18, Pallas kernels, call(): pl.pallas_call(kernel, out_shape=outs, scratch_shapes=scratch, in_specs=i...  11.3 us
    ppermute x4, starting transfers between devices, swap(): return lax.ppermute(v, 'dp', [(0, 1), (1, 0)])  10.6 us
    ppermute x3, waiting for transfers between devices, move_y(): lax.ppermute(v, 'expert', [(y * NX + x, (y + d) % NY * NX + x) for y in r...  9.85 us
    ppermute x8, waiting for transfers between devices, move_x(): lax.ppermute(v, 'expert', [(y * NX + x, y * NX + (x + d) % NX) for y in r...  9.08 us
    ppermute x8, waiting for transfers between devices, move_zy(): return lax.ppermute(v, ('section', 'expert'), pairs)  7.53 us
    ppermute x2, starting transfers between devices, move_z(): return lax.ppermute(v, 'section', [(z, (z + d) % NZ) for z in range(NZ)])  5.58 us
  transfers between devices with their start and end apart: 25, of which 8 were waited for; matrix products, arithmetic and copies ran while one was open for 0% of the time, Pallas kernels for 10%

profile of v3, /device:TPU:1, one launch (start us, length us, event | category | flops | bytes accessed | tf_op | source)
XLA Modules:
  0.0 93.4 jit_solution(10147798914350770795)
XLA Ops:
  0.6 2.1 %collective-permute-start.4 = (bf16[1792,256]{1,0:T(8,128)(2,1)}, bf16[1792,256]{1,0:T(8,128)(2,1)S(1)}, u32[]{:S(2)}, u32[]{:S(2)}) collective-permute-start(bf16[1792,256]{1,0:T(8,128)(2,1)} %bitcast.10), channel_id=1, source_target_pairs={{0,2},{2,4},{4,6},{6,0},{8,10},{10,12},{12,14},{14,8},{16,18},{18,... | collective-permute-start | bytes 2752520 | tf_op jit(solution)/shard_map/ppermute | solution.py:28
  2.8 1.4 %collective-permute-start.5 = (bf16[1792,256]{1,0:T(8,128)(2,1)}, bf16[1792,256]{1,0:T(8,128)(2,1)S(1)}, u32[]{:S(2)}, u32[]{:S(2)}) collective-permute-start(bf16[1792,256]{1,0:T(8,128)(2,1)} %bitcast.11), channel_id=1, source_target_pairs={{0,6},{2,0},{4,2},{6,4},{8,14},{10,8},{12,10},{14,12},{16,22},{18,... | collective-permute-start | bytes 2752520 | tf_op jit(solution)/shard_map/ppermute | solution.py:28
  4.1 1.0 %copy-done.2 = bf16[1,128,1792]{2,1,0:T(8,128)(2,1)S(1)} copy-done((bf16[1,128,1792]{2,1,0:T(8,128)(2,1)S(1)}, bf16[1,128,1792]{2,1,0:T(8,128)(2,1)}, u32[]{:S(2)}) %copy-start.2) | copy-done | bytes 458776
  5.1 1.0 %copy-done.3 = bf16[1,1,128,1792]{3,2,1,0:T(8,128)(2,1)S(1)} copy-done((bf16[1,1,128,1792]{3,2,1,0:T(8,128)(2,1)S(1)}, bf16[1,1,128,1792]{3,2,1,0:T(8,128)(2,1)}, u32[]{:S(2)}) %copy-start.3) | copy-done | bytes 458776
  6.2 1.0 %copy-done.4 = bf16[1,128,1792]{2,1,0:T(8,128)(2,1)S(1)} copy-done((bf16[1,128,1792]{2,1,0:T(8,128)(2,1)S(1)}, bf16[1,128,1792]{2,1,0:T(8,128)(2,1)}, u32[]{:S(2)}) %copy-start.4) | copy-done | bytes 458776
  7.2 0.7 copy-done.5
  7.8 0.7 copy-done.6
  8.5 1.6 %shard_map.87 = (bf16[128,1792]{1,0:T(8,128)(2,1)S(1)}, bf16[128,1792]{1,0:T(8,128)(2,1)S(1)}, bf16[128,1792]{1,0:T(8,128)(2,1)S(1)}, bf16[128,1792]{1,0:T(8,128)(2,1)S(1)}) custom-call(s32[1]{0:T(128)} %bitcast.y_ref, s32[1,128]{1,0:T(1,128)S(1)} %bitcast.21, s32[1,128]{1,0:T(1,128)S(1)} %bitcast.23, bf16[128,1792]{1,0:T(8,128)(2,1)S(1)} %bitcast.18, ...), custom_call_target="tpu_custom_call" | custom-call | flops 220200960 | bytes 3211264 | tf_op jit(solution)/shard_map/pallas_call | solution.py:59
  10.1 3.1 %collective-permute-start.2 = (bf16[128,1792]{1,0:T(8,128)(2,1)S(1)}, bf16[128,1792]{1,0:T(8,128)(2,1)S(1)}, u32[]{:S(2)}, u32[]{:S(2)}) collective-permute-start(bf16[128,1792]{1,0:T(8,128)(2,1)S(1)} %get-tuple-element.27), channel_id=1, source_target_pairs={{0,16},{2,18},{4,20},{6,22},{8,24},{10,26},{12,28},{14,30},{16,0},... | collective-permute-start | bytes 1376264 | tf_op jit(solution)/shard_map/ppermute | solution.py:34
  13.2 1.6 %collective-permute-start = (s32[1,128]{1,0:T(1,128)S(1)}, s32[1,128]{1,0:T(1,128)S(1)}, u32[]{:S(2)}, u32[]{:S(2)}) collective-permute-start(s32[1,128]{1,0:T(1,128)S(1)} %bitcast.22), channel_id=1, source_target_pairs={{0,32},{32,64},{64,96},{96,128},{128,160},{160,192},{192,224},{224... | collective-permute-start | bytes 1544 | tf_op jit(solution)/shard_map/ppermute | solution.py:40
  14.9 3.9 %collective-permute-start.1 = (s32[1,128]{1,0:T(1,128)S(1)}, s32[1,128]{1,0:T(1,128)S(1)}, u32[]{:S(2)}, u32[]{:S(2)}) collective-permute-start(s32[1,128]{1,0:T(1,128)S(1)} %bitcast.24), channel_id=1, source_target_pairs={{0,224},{32,0},{64,32},{96,64},{128,96},{160,128},{192,160},{224,1... | collective-permute-start | bytes 1544 | tf_op jit(solution)/shard_map/ppermute | solution.py:40
  18.8 1.2 %collective-permute-done.ids_f = s32[1,128]{1,0:T(1,128)S(1)} collective-permute-done((s32[1,128]{1,0:T(1,128)S(1)}, s32[1,128]{1,0:T(1,128)S(1)}, u32[]{:S(2)}, u32[]{:S(2)}) %collective-permute-start) | collective-permute-done | bytes 544 | tf_op jit(solution)/shard_map/ppermute | solution.py:40
  20.0 0.0 collective-permute-start.10
  20.0 2.7 %collective-permute-start.11 = (bf16[256,1792]{1,0:T(8,128)(2,1)S(1)}, bf16[256,1792]{1,0:T(8,128)(2,1)S(1)}, u32[]{:S(2)}, u32[]{:S(2)}) collective-permute-start(bf16[256,1792]{1,0:T(8,128)(2,1)S(1)} %bitcast.15), channel_id=1, source_target_pairs={{0,6},{2,0},{4,2},{6,4},{8,14},{10,8},{12,10},{14,12},{16,22},{18,... | collective-permute-start | bytes 2752520 | tf_op jit(solution)/shard_map/ppermute | solution.py:28
  22.7 0.5 shard_map.86
  23.2 0.0 collective-permute-done.2.refs_0_.r2
  23.2 0.3 shard_map.88
  23.5 0.7 collective-permute-start.3
  24.2 0.0 collective-permute-done.5.right.refs_2_.u2
  24.2 0.1 shard_map.89
  24.3 9.8 %collective-permute-done.3.refs_0_.r1 = bf16[128,1792]{1,0:T(8,128)(2,1)S(1)} collective-permute-done((bf16[128,1792]{1,0:T(8,128)(2,1)S(1)}, bf16[128,1792]{1,0:T(8,128)(2,1)S(1)}, u32[]{:S(2)}, u32[]{:S(2)}) %collective-permute-start.3) | collective-permute-done | bytes 458784 | tf_op jit(solution)/shard_map/ppermute | solution.py:34
  34.2 0.3 shard_map.90
  34.4 0.0 copy-start
  34.4 1.5 %collective-permute-start.6 = (bf16[128,1792]{1,0:T(8,128)(2,1)S(1)}, bf16[128,1792]{1,0:T(8,128)(2,1)S(1)}, u32[]{:S(2)}, u32[]{:S(2)}) collective-permute-start(bf16[128,1792]{1,0:T(8,128)(2,1)S(1)} %shard_map.90), channel_id=1, source_target_pairs={{0,24},{2,26},{4,28},{6,30},{8,0},{10,2},{12,4},{14,6},{16,8},{18,... | collective-permute-start | bytes 1376264 | tf_op jit(solution)/shard_map/ppermute | solution.py:34
  35.9 2.7 %collective-permute-start.8 = (bf16[896,256]{1,0:T(8,128)(2,1)S(1)}, bf16[896,256]{1,0:T(8,128)(2,1)S(1)}, u32[]{:S(2)}, u32[]{:S(2)}) collective-permute-start(bf16[896,256]{1,0:T(8,128)(2,1)S(1)} %get-tuple-element.30), channel_id=1, source_target_pairs={{0,6},{2,0},{4,2},{6,4},{8,14},{10,8},{12,10},{14,12},{16,22},{18,... | collective-permute-start | bytes 1376264 | tf_op jit(solution)/shard_map/ppermute | solution.py:28
  38.6 4.8 %collective-permute-done.10.left.refs_1_.v1 = bf16[256,1792]{1,0:T(8,128)(2,1)S(1)} collective-permute-done((bf16[256,1792]{1,0:T(8,128)(2,1)S(1)}, bf16[256,1792]{1,0:T(8,128)(2,1)S(1)}, u32[]{:S(2)}, u32[]{:S(2)}) %collective-permute-start.10) | collective-permute-done | bytes 917536 | tf_op jit(solution)/shard_map/ppermute | solution.py:28
  43.4 0.0 collective-permute-done.11.right.refs_2_.v2
  43.4 0.1 shard_map.92
  43.5 1.4 %collective-permute-start.12 = (bf16[128,1792]{1,0:T(8,128)(2,1)S(1)}, bf16[128,1792]{1,0:T(8,128)(2,1)S(1)}, u32[]{:S(2)}, u32[]{:S(2)}) collective-permute-start(bf16[128,1792]{1,0:T(8,128)(2,1)S(1)} %get-tuple-element.31.token), channel_id=1, source_target_pairs={{0,2},{2,4},{4,6},{6,0},{8,10},{10,12},{12,14},{14,8},{16,18},{18,... | collective-permute-start | bytes 1376264 | tf_op jit(solution)/shard_map/ppermute | solution.py:28
  44.9 1.3 %collective-permute-start.13 = (bf16[128,1792]{1,0:T(8,128)(2,1)S(1)}, bf16[128,1792]{1,0:T(8,128)(2,1)S(1)}, u32[]{:S(2)}, u32[]{:S(2)}) collective-permute-start(bf16[128,1792]{1,0:T(8,128)(2,1)S(1)} %get-tuple-element.32), channel_id=1, source_target_pairs={{0,6},{2,0},{4,2},{6,4},{8,14},{10,8},{12,10},{14,12},{16,22},{18,... | collective-permute-start | bytes 1376264 | tf_op jit(solution)/shard_map/ppermute | solution.py:28
  46.2 1.1 %shard_map.93.token.pu = bf16[320,768]{1,0:T(8,128)(2,1)S(1)} custom-call(bf16[128,1792]{1,0:T(8,128)(2,1)S(1)} %get-tuple-element.25.r0, bf16[128,1792]{1,0:T(8,128)(2,1)S(1)} %collective-permute-done.3.refs_0_.r1, bf16[128,1792]{1,0:T(8,128)(2,1)S(1)} %collective-permute-done.2.refs_0_.r2, bf16[128,1792]{1,0:T(8,128)(2,1)S(1)} %collective-permute-done.6.r3, ...), custom_call_target="tpu_custom_call" | custom-call | flops 880803840 | bytes 4194304 | tf_op jit(solution)/shard_map/pallas_call | solution.py:59
  47.3 4.6 %collective-permute-start.14 = (bf16[320,768]{1,0:T(8,128)(2,1)S(1)}, bf16[320,768]{1,0:T(8,128)(2,1)S(1)}, u32[]{:S(2)}, u32[]{:S(2)}) collective-permute-start(bf16[320,768]{1,0:T(8,128)(2,1)S(1)} %shard_map.93.token.pu), channel_id=1, source_target_pairs={{0,1},{1,0},{2,3},{3,2},{4,5},{5,4},{6,7},{7,6},{8,9},{9,8},{10,11... | collective-permute-start | bytes 1474568 | tf_op jit(solution)/shard_map/ppermute | solution.py:55
  51.9 1.1 %shard_map.94.pv = bf16[192,768]{1,0:T(8,128)(2,1)S(1)} custom-call(bf16[128,1792]{1,0:T(8,128)(2,1)S(1)} %get-tuple-element.25.r0, bf16[128,1792]{1,0:T(8,128)(2,1)S(1)} %collective-permute-done.3.refs_0_.r1, bf16[128,1792]{1,0:T(8,128)(2,1)S(1)} %collective-permute-done.2.refs_0_.r2, bf16[128,1792]{1,0:T(8,128)(2,1)S(1)} %collective-permute-done.6.r3, ...), custom_call_target="tpu_custom_call" | custom-call | flops 587202560 | bytes 4194304 | tf_op jit(solution)/shard_map/pallas_call | solution.py:59
  53.0 0.2 collective-permute-done.7.wa.ua
  53.2 3.2 %collective-permute-start.15 = (bf16[192,768]{1,0:T(8,128)(2,1)S(1)}, bf16[192,768]{1,0:T(8,128)(2,1)S(1)}, u32[]{:S(2)}, u32[]{:S(2)}) collective-permute-start(bf16[192,768]{1,0:T(8,128)(2,1)S(1)} %shard_map.94.pv), channel_id=1, source_target_pairs={{0,1},{1,0},{2,3},{3,2},{4,5},{5,4},{6,7},{7,6},{8,9},{9,8},{10,11... | collective-permute-start | bytes 884744 | tf_op jit(solution)/shard_map/ppermute | solution.py:55
  56.4 0.0 collective-permute-done.8.wb.ub
  56.4 0.5 shard_map.91.pu
  56.9 0.7 collective-permute-start.9
  57.6 0.0 collective-permute-done.15.qv
  57.6 1.4 %shard_map.95 = (f32[160,1792]{1,0:T(8,128)S(1)}, f32[160,1792]{1,0:T(8,128)S(1)}) custom-call(bf16[128,1792]{1,0:T(8,128)(2,1)S(1)} %get-tuple-element.25.r0, bf16[128,1792]{1,0:T(8,128)(2,1)S(1)} %collective-permute-done.3.refs_0_.r1, bf16[128,1792]{1,0:T(8,128)(2,1)S(1)} %collective-permute-done.2.refs_0_.r2, ...), custom_call_target="tpu_custom_call" | custom-call | flops 880803840 | bytes 8388608 | tf_op jit(solution)/shard_map/pallas_call | solution.py:59
  59.1 4.0 %collective-permute-done.12.va = bf16[128,1792]{1,0:T(8,128)(2,1)S(1)} collective-permute-done((bf16[128,1792]{1,0:T(8,128)(2,1)S(1)}, bf16[128,1792]{1,0:T(8,128)(2,1)S(1)}, u32[]{:S(2)}, u32[]{:S(2)}) %collective-permute-start.12) | collective-permute-done | bytes 458784 | tf_op jit(solution)/shard_map/ppermute | solution.py:28
  63.1 0.0 collective-permute-done.13.vb
  63.1 0.0 collective-permute-done.9.qu
  63.1 0.8 shard_map.96
  63.9 2.1 %collective-permute-start.18 = (bf16[192,256]{1,0:T(8,128)(2,1)S(1)}, bf16[192,256]{1,0:T(8,128)(2,1)S(1)}, u32[]{:S(2)}, u32[]{:S(2)}) collective-permute-start(bf16[192,256]{1,0:T(8,128)(2,1)S(1)} %get-tuple-element.37.pv), channel_id=1, source_target_pairs={{0,1},{1,0},{2,3},{3,2},{4,5},{5,4},{6,7},{7,6},{8,9},{9,8},{10,11... | collective-permute-start | bytes 294920 | tf_op jit(solution)/shard_map/ppermute | solution.py:55
  66.0 1.7 %collective-permute-start.16 = (bf16[40,1792]{1,0:T(8,128)(2,1)S(1)}, bf16[40,1792]{1,0:T(8,128)(2,1)S(1)}, u32[]{:S(2)}, u32[]{:S(2)}) collective-permute-start(bf16[40,1792]{1,0:T(8,128)(2,1)S(1)} %get-tuple-element.35.token), channel_id=1, source_target_pairs={{0,32},{2,34},{4,36},{6,38},{8,40},{10,42},{12,44},{14,46},{16,48}... | collective-permute-start | bytes 430088 | tf_op jit(solution)/shard_map/ppermute | solution.py:51
  67.6 4.3 %collective-permute-start.17 = (bf16[40,1792]{1,0:T(8,128)(2,1)S(1)}, bf16[40,1792]{1,0:T(8,128)(2,1)S(1)}, u32[]{:S(2)}, u32[]{:S(2)}) collective-permute-start(bf16[40,1792]{1,0:T(8,128)(2,1)S(1)} %get-tuple-element.36), channel_id=1, source_target_pairs={{0,48},{2,50},{4,52},{6,54},{8,56},{10,58},{12,60},{14,62},{16,32}... | collective-permute-start | bytes 430088 | tf_op jit(solution)/shard_map/ppermute | solution.py:51
  71.9 0.0 collective-permute-done.18.qv
  71.9 0.5 shard_map.98
  72.4 1.1 %collective-permute-start.19 = (bf16[40,1792]{1,0:T(8,128)(2,1)S(1)}, bf16[40,1792]{1,0:T(8,128)(2,1)S(1)}, u32[]{:S(2)}, u32[]{:S(2)}) collective-permute-start(bf16[40,1792]{1,0:T(8,128)(2,1)S(1)} %get-tuple-element.38), channel_id=1, source_target_pairs={{0,224},{2,226},{4,228},{6,230},{8,232},{10,234},{12,236},{14,238}... | collective-permute-start | bytes 430088 | tf_op jit(solution)/shard_map/ppermute | solution.py:51
  73.5 1.2 %collective-permute-start.20 = (bf16[40,1792]{1,0:T(8,128)(2,1)S(1)}, bf16[40,1792]{1,0:T(8,128)(2,1)S(1)}, u32[]{:S(2)}, u32[]{:S(2)}) collective-permute-start(bf16[40,1792]{1,0:T(8,128)(2,1)S(1)} %get-tuple-element.39), channel_id=1, source_target_pairs={{0,56},{2,58},{4,60},{6,62},{8,32},{10,34},{12,36},{14,38},{16,40}... | collective-permute-start | bytes 430088 | tf_op jit(solution)/shard_map/ppermute | solution.py:51
  74.7 3.3 %collective-permute-start.21 = (bf16[40,1792]{1,0:T(8,128)(2,1)S(1)}, bf16[40,1792]{1,0:T(8,128)(2,1)S(1)}, u32[]{:S(2)}, u32[]{:S(2)}) collective-permute-start(bf16[40,1792]{1,0:T(8,128)(2,1)S(1)} %get-tuple-element.40), channel_id=1, source_target_pairs={{0,40},{2,42},{4,44},{6,46},{8,48},{10,50},{12,52},{14,54},{16,56}... | collective-permute-start | bytes 430088 | tf_op jit(solution)/shard_map/ppermute | solution.py:51
  77.9 1.6 %collective-permute-start.22 = (bf16[40,1792]{1,0:T(8,128)(2,1)S(1)}, bf16[40,1792]{1,0:T(8,128)(2,1)S(1)}, u32[]{:S(2)}, u32[]{:S(2)}) collective-permute-start(bf16[40,1792]{1,0:T(8,128)(2,1)S(1)} %get-tuple-element.41), channel_id=1, source_target_pairs={{0,240},{2,242},{4,244},{6,246},{8,248},{10,250},{12,252},{14,254}... | collective-permute-start | bytes 430088 | tf_op jit(solution)/shard_map/ppermute | solution.py:51
  79.5 1.8 %collective-permute-done.17.refs_1_ = bf16[40,1792]{1,0:T(8,128)(2,1)S(1)} collective-permute-done((bf16[40,1792]{1,0:T(8,128)(2,1)S(1)}, bf16[40,1792]{1,0:T(8,128)(2,1)S(1)}, u32[]{:S(2)}, u32[]{:S(2)}) %collective-permute-start.17) | collective-permute-done | bytes 143392 | tf_op jit(solution)/shard_map/ppermute | solution.py:51
  81.3 2.0 %collective-permute-start.23 = (bf16[40,1792]{1,0:T(8,128)(2,1)S(1)}, bf16[40,1792]{1,0:T(8,128)(2,1)S(1)}, u32[]{:S(2)}, u32[]{:S(2)}) collective-permute-start(bf16[40,1792]{1,0:T(8,128)(2,1)S(1)} %get-tuple-element.42), channel_id=1, source_target_pairs={{0,248},{2,250},{4,252},{6,254},{8,224},{10,226},{12,228},{14,230}... | collective-permute-start | bytes 430088 | tf_op jit(solution)/shard_map/ppermute | solution.py:51
  83.3 0.9 collective-permute-start.24
  84.2 0.4 shard_map.97.token.refs_0_
  84.6 0.2 shard_map.99.token.refs_0_
  84.8 0.3 shard_map.100.total.token
  85.1 3.5 %collective-permute-done.21.refs_0_ = bf16[40,1792]{1,0:T(8,128)(2,1)S(1)} collective-permute-done((bf16[40,1792]{1,0:T(8,128)(2,1)S(1)}, bf16[40,1792]{1,0:T(8,128)(2,1)S(1)}, u32[]{:S(2)}, u32[]{:S(2)}) %collective-permute-start.21) | collective-permute-done | bytes 143392 | tf_op jit(solution)/shard_map/ppermute | solution.py:51
  88.6 1.0 %shard_map.101 = bf16[128,1792]{1,0:T(8,128)(2,1)} custom-call(bf16[4,128,40]{2,1,0:T(8,128)(2,1)S(1)} %get-tuple-element.23.refs_1_.table, f32[128,1792]{1,0:T(8,128)S(1)} %shard_map.99.token.refs_0_, f32[128,1792]{1,0:T(8,128)S(1)} %shard_map.100.total.token, bf16[40,1792]{1,0:T(8,128)(2,1)S(1)} %collective-permute-done.21.refs_0_), custom_call_target="tpu_custom_call" | custom-call | flops 18350080 | bytes 1835008 | tf_op jit(solution)/shard_map/pallas_call | solution.py:59
  89.6 0.4 shard_map.102.total
  90.0 2.2 %collective-permute-done.24.refs_0_ = bf16[40,1792]{1,0:T(8,128)(2,1)S(1)} collective-permute-done((bf16[40,1792]{1,0:T(8,128)(2,1)S(1)}, bf16[40,1792]{1,0:T(8,128)(2,1)S(1)}, u32[]{:S(2)}, u32[]{:S(2)}) %collective-permute-start.24) | collective-permute-done | bytes 143392 | tf_op jit(solution)/shard_map/ppermute | solution.py:51
  92.2 1.0 %shard_map.103 = bf16[128,1792]{1,0:T(8,128)(2,1)} custom-call(bf16[4,128,40]{2,1,0:T(8,128)(2,1)S(1)} %get-tuple-element.24.token.table, f32[128,1792]{1,0:T(8,128)S(1)} %shard_map.100.total.token, f32[128,1792]{1,0:T(8,128)S(1)} %shard_map.102.total, bf16[40,1792]{1,0:T(8,128)(2,1)S(1)} %collective-permute-done.24.refs_0_), custom_call_target="tpu_custom_call" | custom-call | flops 18350080 | bytes 1835008 | tf_op jit(solution)/shard_map/pallas_call | solution.py:59
  (18 shorter events, 0.0 us)
Async XLA Ops:
  0.6 19.4 %copy-start.1 = (bf16[1,1,256,1792]{3,2,1,0:T(8,128)(2,1)S(1)}, bf16[1,1,256,1792]{3,2,1,0:T(8,128)(2,1)}, u32[]{:S(2)}) copy-start(bf16[1,1,256,1792]{3,2,1,0:T(8,128)(2,1)} %param.13) | copy-start | bytes 2752516
  0.6 23.6 %collective-permute-start.4 = (bf16[1792,256]{1,0:T(8,128)(2,1)}, bf16[1792,256]{1,0:T(8,128)(2,1)S(1)}, u32[]{:S(2)}, u32[]{:S(2)}) collective-permute-start(bf16[1792,256]{1,0:T(8,128)(2,1)} %bitcast.10), channel_id=1, source_target_pairs={{0,2},{2,4},{4,6},{6,0},{8,10},{10,12},{12,14},{14,8},{16,18},{18,... | collective-permute-start | bytes 2752520 | tf_op jit(solution)/shard_map/ppermute | solution.py:28
  2.8 21.5 %collective-permute-start.5 = (bf16[1792,256]{1,0:T(8,128)(2,1)}, bf16[1792,256]{1,0:T(8,128)(2,1)S(1)}, u32[]{:S(2)}, u32[]{:S(2)}) collective-permute-start(bf16[1792,256]{1,0:T(8,128)(2,1)} %bitcast.11), channel_id=1, source_target_pairs={{0,6},{2,0},{4,2},{6,4},{8,14},{10,8},{12,10},{14,12},{16,22},{18,... | collective-permute-start | bytes 2752520 | tf_op jit(solution)/shard_map/ppermute | solution.py:28
  4.1 1.0 %copy-start.2 = (bf16[1,128,1792]{2,1,0:T(8,128)(2,1)S(1)}, bf16[1,128,1792]{2,1,0:T(8,128)(2,1)}, u32[]{:S(2)}) copy-start(bf16[1,128,1792]{2,1,0:T(8,128)(2,1)} %param.7) | copy-start | bytes 1376260
  5.1 1.0 %copy-start.3 = (bf16[1,1,128,1792]{3,2,1,0:T(8,128)(2,1)S(1)}, bf16[1,1,128,1792]{3,2,1,0:T(8,128)(2,1)}, u32[]{:S(2)}) copy-start(bf16[1,1,128,1792]{3,2,1,0:T(8,128)(2,1)} %param.10) | copy-start | bytes 1376260
  6.2 1.0 %copy-start.4 = (bf16[1,128,1792]{2,1,0:T(8,128)(2,1)S(1)}, bf16[1,128,1792]{2,1,0:T(8,128)(2,1)}, u32[]{:S(2)}) copy-start(bf16[1,128,1792]{2,1,0:T(8,128)(2,1)} %param.9) | copy-start | bytes 1376260
  7.2 0.7 copy-start.5
  7.8 0.7 copy-start.6
  10.1 13.1 %collective-permute-start.2 = (bf16[128,1792]{1,0:T(8,128)(2,1)S(1)}, bf16[128,1792]{1,0:T(8,128)(2,1)S(1)}, u32[]{:S(2)}, u32[]{:S(2)}) collective-permute-start(bf16[128,1792]{1,0:T(8,128)(2,1)S(1)} %get-tuple-element.27), channel_id=1, source_target_pairs={{0,16},{2,18},{4,20},{6,22},{8,24},{10,26},{12,28},{14,30},{16,0},... | collective-permute-start | bytes 1376264 | tf_op jit(solution)/shard_map/ppermute | solution.py:34
  13.2 6.8 %collective-permute-start = (s32[1,128]{1,0:T(1,128)S(1)}, s32[1,128]{1,0:T(1,128)S(1)}, u32[]{:S(2)}, u32[]{:S(2)}) collective-permute-start(s32[1,128]{1,0:T(1,128)S(1)} %bitcast.22), channel_id=1, source_target_pairs={{0,32},{32,64},{64,96},{96,128},{128,160},{160,192},{192,224},{224... | collective-permute-start | bytes 1544 | tf_op jit(solution)/shard_map/ppermute | solution.py:40
  14.9 5.2 %collective-permute-start.1 = (s32[1,128]{1,0:T(1,128)S(1)}, s32[1,128]{1,0:T(1,128)S(1)}, u32[]{:S(2)}, u32[]{:S(2)}) collective-permute-start(s32[1,128]{1,0:T(1,128)S(1)} %bitcast.24), channel_id=1, source_target_pairs={{0,224},{32,0},{64,32},{96,64},{128,96},{160,128},{192,160},{224,1... | collective-permute-start | bytes 1544 | tf_op jit(solution)/shard_map/ppermute | solution.py:40
  20.0 23.4 %collective-permute-start.10 = (bf16[256,1792]{1,0:T(8,128)(2,1)S(1)}, bf16[256,1792]{1,0:T(8,128)(2,1)S(1)}, u32[]{:S(2)}, u32[]{:S(2)}) collective-permute-start(bf16[256,1792]{1,0:T(8,128)(2,1)S(1)} %bitcast.14), channel_id=1, source_target_pairs={{0,2},{2,4},{4,6},{6,0},{8,10},{10,12},{12,14},{14,8},{16,18},{18,... | collective-permute-start | bytes 2752520 | tf_op jit(solution)/shard_map/ppermute | solution.py:28
  20.0 23.4 %collective-permute-start.11 = (bf16[256,1792]{1,0:T(8,128)(2,1)S(1)}, bf16[256,1792]{1,0:T(8,128)(2,1)S(1)}, u32[]{:S(2)}, u32[]{:S(2)}) collective-permute-start(bf16[256,1792]{1,0:T(8,128)(2,1)S(1)} %bitcast.15), channel_id=1, source_target_pairs={{0,6},{2,0},{4,2},{6,4},{8,14},{10,8},{12,10},{14,12},{16,22},{18,... | collective-permute-start | bytes 2752520 | tf_op jit(solution)/shard_map/ppermute | solution.py:28
  23.5 10.7 %collective-permute-start.3 = (bf16[128,1792]{1,0:T(8,128)(2,1)S(1)}, bf16[128,1792]{1,0:T(8,128)(2,1)S(1)}, u32[]{:S(2)}, u32[]{:S(2)}) collective-permute-start(bf16[128,1792]{1,0:T(8,128)(2,1)S(1)} %shard_map.88), channel_id=1, source_target_pairs={{0,8},{2,10},{4,12},{6,14},{8,16},{10,18},{12,20},{14,22},{16,24},... | collective-permute-start | bytes 1376264 | tf_op jit(solution)/shard_map/ppermute | solution.py:34
  34.4 11.8 %copy-start = (bf16[1,1,1792,256]{3,2,1,0:T(8,128)(2,1)S(1)}, bf16[1,1,1792,256]{3,2,1,0:T(8,128)(2,1)}, u32[]{:S(2)}) copy-start(bf16[1,1,1792,256]{3,2,1,0:T(8,128)(2,1)} %param.12) | copy-start | bytes 2752516
  34.4 11.8 %collective-permute-start.6 = (bf16[128,1792]{1,0:T(8,128)(2,1)S(1)}, bf16[128,1792]{1,0:T(8,128)(2,1)S(1)}, u32[]{:S(2)}, u32[]{:S(2)}) collective-permute-start(bf16[128,1792]{1,0:T(8,128)(2,1)S(1)} %shard_map.90), channel_id=1, source_target_pairs={{0,24},{2,26},{4,28},{6,30},{8,0},{10,2},{12,4},{14,6},{16,8},{18,... | collective-permute-start | bytes 1376264 | tf_op jit(solution)/shard_map/ppermute | solution.py:34
  35.9 17.3 %collective-permute-start.7 = (bf16[896,256]{1,0:T(8,128)(2,1)S(1)}, bf16[896,256]{1,0:T(8,128)(2,1)S(1)}, u32[]{:S(2)}, u32[]{:S(2)}) collective-permute-start(bf16[896,256]{1,0:T(8,128)(2,1)S(1)} %get-tuple-element.29.refs_1_), channel_id=1, source_target_pairs={{0,2},{2,4},{4,6},{6,0},{8,10},{10,12},{12,14},{14,8},{16,18},{18,... | collective-permute-start | bytes 1376264 | tf_op jit(solution)/shard_map/ppermute | solution.py:28
  35.9 20.5 %collective-permute-start.8 = (bf16[896,256]{1,0:T(8,128)(2,1)S(1)}, bf16[896,256]{1,0:T(8,128)(2,1)S(1)}, u32[]{:S(2)}, u32[]{:S(2)}) collective-permute-start(bf16[896,256]{1,0:T(8,128)(2,1)S(1)} %get-tuple-element.30), channel_id=1, source_target_pairs={{0,6},{2,0},{4,2},{6,4},{8,14},{10,8},{12,10},{14,12},{16,22},{18,... | collective-permute-start | bytes 1376264 | tf_op jit(solution)/shard_map/ppermute | solution.py:28
  43.5 19.6 %collective-permute-start.12 = (bf16[128,1792]{1,0:T(8,128)(2,1)S(1)}, bf16[128,1792]{1,0:T(8,128)(2,1)S(1)}, u32[]{:S(2)}, u32[]{:S(2)}) collective-permute-start(bf16[128,1792]{1,0:T(8,128)(2,1)S(1)} %get-tuple-element.31.token), channel_id=1, source_target_pairs={{0,2},{2,4},{4,6},{6,0},{8,10},{10,12},{12,14},{14,8},{16,18},{18,... | collective-permute-start | bytes 1376264 | tf_op jit(solution)/shard_map/ppermute | solution.py:28
  44.9 18.2 %collective-permute-start.13 = (bf16[128,1792]{1,0:T(8,128)(2,1)S(1)}, bf16[128,1792]{1,0:T(8,128)(2,1)S(1)}, u32[]{:S(2)}, u32[]{:S(2)}) collective-permute-start(bf16[128,1792]{1,0:T(8,128)(2,1)S(1)} %get-tuple-element.32), channel_id=1, source_target_pairs={{0,6},{2,0},{4,2},{6,4},{8,14},{10,8},{12,10},{14,12},{16,22},{18,... | collective-permute-start | bytes 1376264 | tf_op jit(solution)/shard_map/ppermute | solution.py:28
  47.3 10.3 %collective-permute-start.14 = (bf16[320,768]{1,0:T(8,128)(2,1)S(1)}, bf16[320,768]{1,0:T(8,128)(2,1)S(1)}, u32[]{:S(2)}, u32[]{:S(2)}) collective-permute-start(bf16[320,768]{1,0:T(8,128)(2,1)S(1)} %shard_map.93.token.pu), channel_id=1, source_target_pairs={{0,1},{1,0},{2,3},{3,2},{4,5},{5,4},{6,7},{7,6},{8,9},{9,8},{10,11... | collective-permute-start | bytes 1474568 | tf_op jit(solution)/shard_map/ppermute | solution.py:55
  53.2 4.4 %collective-permute-start.15 = (bf16[192,768]{1,0:T(8,128)(2,1)S(1)}, bf16[192,768]{1,0:T(8,128)(2,1)S(1)}, u32[]{:S(2)}, u32[]{:S(2)}) collective-permute-start(bf16[192,768]{1,0:T(8,128)(2,1)S(1)} %shard_map.94.pv), channel_id=1, source_target_pairs={{0,1},{1,0},{2,3},{3,2},{4,5},{5,4},{6,7},{7,6},{8,9},{9,8},{10,11... | collective-permute-start | bytes 884744 | tf_op jit(solution)/shard_map/ppermute | solution.py:55
  56.9 6.1 %collective-permute-start.9 = (bf16[320,256]{1,0:T(8,128)(2,1)S(1)}, bf16[320,256]{1,0:T(8,128)(2,1)S(1)}, u32[]{:S(2)}, u32[]{:S(2)}) collective-permute-start(bf16[320,256]{1,0:T(8,128)(2,1)S(1)} %shard_map.91.pu), channel_id=1, source_target_pairs={{0,1},{1,0},{2,3},{3,2},{4,5},{5,4},{6,7},{7,6},{8,9},{9,8},{10,11... | collective-permute-start | bytes 491528 | tf_op jit(solution)/shard_map/ppermute | solution.py:55
  63.9 8.0 %collective-permute-start.18 = (bf16[192,256]{1,0:T(8,128)(2,1)S(1)}, bf16[192,256]{1,0:T(8,128)(2,1)S(1)}, u32[]{:S(2)}, u32[]{:S(2)}) collective-permute-start(bf16[192,256]{1,0:T(8,128)(2,1)S(1)} %get-tuple-element.37.pv), channel_id=1, source_target_pairs={{0,1},{1,0},{2,3},{3,2},{4,5},{5,4},{6,7},{7,6},{8,9},{9,8},{10,11... | collective-permute-start | bytes 294920 | tf_op jit(solution)/shard_map/ppermute | solution.py:55
  66.0 12.0 %collective-permute-start.16 = (bf16[40,1792]{1,0:T(8,128)(2,1)S(1)}, bf16[40,1792]{1,0:T(8,128)(2,1)S(1)}, u32[]{:S(2)}, u32[]{:S(2)}) collective-permute-start(bf16[40,1792]{1,0:T(8,128)(2,1)S(1)} %get-tuple-element.35.token), channel_id=1, source_target_pairs={{0,32},{2,34},{4,36},{6,38},{8,40},{10,42},{12,44},{14,46},{16,48}... | collective-permute-start | bytes 430088 | tf_op jit(solution)/shard_map/ppermute | solution.py:51
  67.6 13.7 %collective-permute-start.17 = (bf16[40,1792]{1,0:T(8,128)(2,1)S(1)}, bf16[40,1792]{1,0:T(8,128)(2,1)S(1)}, u32[]{:S(2)}, u32[]{:S(2)}) collective-permute-start(bf16[40,1792]{1,0:T(8,128)(2,1)S(1)} %get-tuple-element.36), channel_id=1, source_target_pairs={{0,48},{2,50},{4,52},{6,54},{8,56},{10,58},{12,60},{14,62},{16,32}... | collective-permute-start | bytes 430088 | tf_op jit(solution)/shard_map/ppermute | solution.py:51
  72.4 10.9 %collective-permute-start.19 = (bf16[40,1792]{1,0:T(8,128)(2,1)S(1)}, bf16[40,1792]{1,0:T(8,128)(2,1)S(1)}, u32[]{:S(2)}, u32[]{:S(2)}) collective-permute-start(bf16[40,1792]{1,0:T(8,128)(2,1)S(1)} %get-tuple-element.38), channel_id=1, source_target_pairs={{0,224},{2,226},{4,228},{6,230},{8,232},{10,234},{12,236},{14,238}... | collective-permute-start | bytes 430088 | tf_op jit(solution)/shard_map/ppermute | solution.py:51
  73.5 11.3 %collective-permute-start.20 = (bf16[40,1792]{1,0:T(8,128)(2,1)S(1)}, bf16[40,1792]{1,0:T(8,128)(2,1)S(1)}, u32[]{:S(2)}, u32[]{:S(2)}) collective-permute-start(bf16[40,1792]{1,0:T(8,128)(2,1)S(1)} %get-tuple-element.39), channel_id=1, source_target_pairs={{0,56},{2,58},{4,60},{6,62},{8,32},{10,34},{12,36},{14,38},{16,40}... | collective-permute-start | bytes 430088 | tf_op jit(solution)/shard_map/ppermute | solution.py:51
  74.7 13.9 %collective-permute-start.21 = (bf16[40,1792]{1,0:T(8,128)(2,1)S(1)}, bf16[40,1792]{1,0:T(8,128)(2,1)S(1)}, u32[]{:S(2)}, u32[]{:S(2)}) collective-permute-start(bf16[40,1792]{1,0:T(8,128)(2,1)S(1)} %get-tuple-element.40), channel_id=1, source_target_pairs={{0,40},{2,42},{4,44},{6,46},{8,48},{10,50},{12,52},{14,54},{16,56}... | collective-permute-start | bytes 430088 | tf_op jit(solution)/shard_map/ppermute | solution.py:51
  77.9 11.7 %collective-permute-start.22 = (bf16[40,1792]{1,0:T(8,128)(2,1)S(1)}, bf16[40,1792]{1,0:T(8,128)(2,1)S(1)}, u32[]{:S(2)}, u32[]{:S(2)}) collective-permute-start(bf16[40,1792]{1,0:T(8,128)(2,1)S(1)} %get-tuple-element.41), channel_id=1, source_target_pairs={{0,240},{2,242},{4,244},{6,246},{8,248},{10,250},{12,252},{14,254}... | collective-permute-start | bytes 430088 | tf_op jit(solution)/shard_map/ppermute | solution.py:51
  81.3 8.3 %collective-permute-start.23 = (bf16[40,1792]{1,0:T(8,128)(2,1)S(1)}, bf16[40,1792]{1,0:T(8,128)(2,1)S(1)}, u32[]{:S(2)}, u32[]{:S(2)}) collective-permute-start(bf16[40,1792]{1,0:T(8,128)(2,1)S(1)} %get-tuple-element.42), channel_id=1, source_target_pairs={{0,248},{2,250},{4,252},{6,254},{8,224},{10,226},{12,228},{14,230}... | collective-permute-start | bytes 430088 | tf_op jit(solution)/shard_map/ppermute | solution.py:51
  83.3 8.9 %collective-permute-start.24 = (bf16[40,1792]{1,0:T(8,128)(2,1)S(1)}, bf16[40,1792]{1,0:T(8,128)(2,1)S(1)}, u32[]{:S(2)}, u32[]{:S(2)}) collective-permute-start(bf16[40,1792]{1,0:T(8,128)(2,1)S(1)} %get-tuple-element.43), channel_id=1, source_target_pairs={{0,232},{2,234},{4,236},{6,238},{8,240},{10,242},{12,244},{14,246}... | collective-permute-start | bytes 430088 | tf_op jit(solution)/shard_map/ppermute | solution.py:51

commit v4 on v3

--- a/solution.py
+++ b/solution.py
@@ -18,7 +18,6 @@
 ANY = pl.BlockSpec(memory_space=pl.ANY)
 HBM = pl.BlockSpec(memory_space=pltpu.HBM)
 SM = pl.BlockSpec(memory_space=pltpu.SMEM)
-
 CU = 8 * 10**9
 CU2 = 6 * 10**9
 LIMIT = 24 * 1024 * 1024
@@ -232,16 +231,20 @@
                 out[:, o] = t[i * CAP : (i + 1) * CAP].astype(BF)
 
 
-def finish_kernel(table, token, total, *refs, parts):
-    *rows, out, held, sems = refs
+def finish_kernel(table, total_f, total_b, row, *refs, stream, group):
+    outs, held, sems = refs[:2], refs[2], refs[3]
     copies = []
-    for i, c in enumerate(columns(out.shape[1])):
-        t = total[:, c]
-        for d, r in zip(parts, rows):
-            t += nn(table[d], r[:, c])
-        held[:, c] = t.astype(held.dtype)
-        copies.append(pltpu.make_async_copy(held.at[:, c], out.at[:, c], sems.at[i]))
-        copies[-1].start()
+    for k in (1 - stream, stream):
+        total = (total_f, total_b)[k]
+        for i, c in enumerate(columns(total.shape[1])):
+            t = total[:, c]
+            if k == stream:
+                t += nn(table[group], row[:, c])
+            held[k, :, c] = t.astype(held.dtype)
+            copies.append(
+                pltpu.make_async_copy(held.at[k, :, c], outs[k].at[:, c], sems.at[k, i])
+            )
+            copies[-1].start()
     for c in copies:
         c.wait()
 
@@ -415,27 +418,32 @@
             *[got[d] for d in parts],
         )
 
-    def finish(table, got, parts, total, token):
+    def finish(total_f, total_b, stream, group):
         return call(
-            functools.partial(finish_kernel, parts=parts),
-            sds((n, width)),
-            2 * CAP * n * width * len(parts),
-            8 * n * width,
-            [VM, ANY] + [VM] * (len(parts) + 1),
-            table,
-            token,
-            total,
-            *[got[d] for d in parts],
-            scratch=[pltpu.VMEM((n, width), BF), pltpu.SemaphoreType.DMA((width // 256,))],
-            out_specs=ANY,
+            functools.partial(finish_kernel, stream=stream, group=group),
+            [sds((n, width))] * 2,
+            2 * CAP * n * width,
+            12 * n * width,
+            [VM] * 4,
+            (table_f, table_b)[stream],
+            total_f,
+            total_b,
+            (got_f, got_b)[stream][group],
+            scratch=[
+                pltpu.VMEM((2, n, width), BF),
+                pltpu.SemaphoreType.DMA((2, width // 256)),
+            ],
+            out_specs=[ANY, ANY],
         )
 
-    sum_f = combine(table_f, got_f, (0, 2), None, table_b)
-    sum_b = combine(table_b, got_b, (0,), None, sum_f)
+    sum_f = combine(table_f, got_f, (2,), None, table_b)
+    sum_b = combine(table_b, got_b, (3,), None, sum_f)
     sum_f = combine(table_f, got_f, (1,), sum_f, sum_b)
-    out_f = finish(table_f, got_f, (3,), sum_f, sum_b)
-    sum_b = combine(table_b, got_b, (2, 1), sum_b, sum_f)
-    out_b = finish(table_b, got_b, (3,), sum_b, sum_f)
+    sum_b = combine(table_b, got_b, (0,), sum_b, sum_f)
+    sum_f = combine(table_f, got_f, (3,), sum_f, sum_b)
+    sum_b = combine(table_b, got_b, (1,), sum_b, sum_f)
+    sum_b = combine(table_b, got_b, (2,), sum_b, sum_b)
+    out_f, out_b = finish(sum_f, sum_b, 0, 0)
     return (out_f[None], out_b[None])
 
 

time: 94.1 us -> 92.5 us (0.983)
  waiting for transfers between devices: 27.7 us -> 26.6 us
  starting transfers between devices: 49 us -> 48 us
    ppermute x8, waiting for transfers between devices: 7.53 us -> 6.42 us  [move_zy(): return lax.ppermute(v, ('section', 'expert'), pairs)]
    ppermute x8, starting transfers between devices: 16 us -> 14.9 us  [move_zy(): return lax.ppermute(v, ('section', 'expert'), pairs)]
    pallas_call x18 -> x20, Pallas kernels: 11.3 us -> 11 us  [call(): pl.pallas_call(kernel, out_shape=outs, scratch_shapes=scratch, in_specs=i...]
where the time goes in v4:
time: 92.5 us; the launch traced here: 90.9 us
  starting transfers between devices  48 us (52%)
  waiting for transfers between devices  26.6 us (29%)
  Pallas kernels  11 us (12%)
  local copies, waits for them, and re-layouts  4.37 us (5%)
  between operations  0.99 us (1%)
    ppermute x8, starting transfers between devices, move_zy(): return lax.ppermute(v, ('section', 'expert'), pairs)  14.9 us
    ppermute x8, starting transfers between devices, move_x(): lax.ppermute(v, 'expert', [(y * NX + x, y * NX + (x + d) % NX) for y in r...  11.6 us
    pallas_call x20, Pallas kernels, call(): pl.pallas_call(kernel, out_shape=outs, scratch_shapes=scratch, in_specs=i...  11 us
    ppermute x4, starting transfers between devices, swap(): return lax.ppermute(v, 'dp', [(0, 1), (1, 0)])  10.6 us
    ppermute x3, waiting for transfers between devices, move_y(): lax.ppermute(v, 'expert', [(y * NX + x, (y + d) % NY * NX + x) for y in r...  9.85 us
    ppermute x8, waiting for transfers between devices, move_x(): lax.ppermute(v, 'expert', [(y * NX + x, y * NX + (x + d) % NX) for y in r...  9.08 us
    ppermute x8, waiting for transfers between devices, move_zy(): return lax.ppermute(v, ('section', 'expert'), pairs)  6.42 us
    ppermute x2, starting transfers between devices, move_z(): return lax.ppermute(v, 'section', [(z, (z + d) % NZ) for z in range(NZ)])  5.58 us
  transfers between devices with their start and end apart: 25, of which 8 were waited for; matrix products, arithmetic and copies ran while one was open for 0% of the time, Pallas kernels for 10%

profile of v4, /device:TPU:1, one launch (start us, length us, event | category | flops | bytes accessed | tf_op | source)
XLA Modules:
  0.0 90.9 jit_solution(2505422492945784101)
XLA Ops:
  0.6 2.1 %collective-permute-start.4 = (bf16[1792,256]{1,0:T(8,128)(2,1)}, bf16[1792,256]{1,0:T(8,128)(2,1)S(1)}, u32[]{:S(2)}, u32[]{:S(2)}) collective-permute-start(bf16[1792,256]{1,0:T(8,128)(2,1)} %bitcast.10), channel_id=1, source_target_pairs={{0,2},{2,4},{4,6},{6,0},{8,10},{10,12},{12,14},{14,8},{16,18},{18,... | collective-permute-start | bytes 2752520 | tf_op jit(solution)/shard_map/ppermute | solution.py:27
  2.8 1.4 %collective-permute-start.5 = (bf16[1792,256]{1,0:T(8,128)(2,1)}, bf16[1792,256]{1,0:T(8,128)(2,1)S(1)}, u32[]{:S(2)}, u32[]{:S(2)}) collective-permute-start(bf16[1792,256]{1,0:T(8,128)(2,1)} %bitcast.11), channel_id=1, source_target_pairs={{0,6},{2,0},{4,2},{6,4},{8,14},{10,8},{12,10},{14,12},{16,22},{18,... | collective-permute-start | bytes 2752520 | tf_op jit(solution)/shard_map/ppermute | solution.py:27
  4.1 1.0 %copy-done.2 = bf16[1,128,1792]{2,1,0:T(8,128)(2,1)S(1)} copy-done((bf16[1,128,1792]{2,1,0:T(8,128)(2,1)S(1)}, bf16[1,128,1792]{2,1,0:T(8,128)(2,1)}, u32[]{:S(2)}) %copy-start.2) | copy-done | bytes 458776
  5.1 1.0 %copy-done.3 = bf16[1,1,128,1792]{3,2,1,0:T(8,128)(2,1)S(1)} copy-done((bf16[1,1,128,1792]{3,2,1,0:T(8,128)(2,1)S(1)}, bf16[1,1,128,1792]{3,2,1,0:T(8,128)(2,1)}, u32[]{:S(2)}) %copy-start.3) | copy-done | bytes 458776
  6.2 1.0 %copy-done.4 = bf16[1,128,1792]{2,1,0:T(8,128)(2,1)S(1)} copy-done((bf16[1,128,1792]{2,1,0:T(8,128)(2,1)S(1)}, bf16[1,128,1792]{2,1,0:T(8,128)(2,1)}, u32[]{:S(2)}) %copy-start.4) | copy-done | bytes 458776
  7.2 0.7 copy-done.5
  7.8 0.7 copy-done.6
  8.5 1.6 %shard_map.87 = (bf16[128,1792]{1,0:T(8,128)(2,1)S(1)}, bf16[128,1792]{1,0:T(8,128)(2,1)S(1)}, bf16[128,1792]{1,0:T(8,128)(2,1)S(1)}, bf16[128,1792]{1,0:T(8,128)(2,1)S(1)}) custom-call(s32[1]{0:T(128)} %bitcast.y_ref, s32[1,128]{1,0:T(1,128)S(1)} %bitcast.21, s32[1,128]{1,0:T(1,128)S(1)} %bitcast.23, bf16[128,1792]{1,0:T(8,128)(2,1)S(1)} %bitcast.18, ...), custom_call_target="tpu_custom_call" | custom-call | flops 220200960 | bytes 3211264 | tf_op jit(solution)/shard_map/pallas_call | solution.py:58
  10.1 3.1 %collective-permute-start.2 = (bf16[128,1792]{1,0:T(8,128)(2,1)S(1)}, bf16[128,1792]{1,0:T(8,128)(2,1)S(1)}, u32[]{:S(2)}, u32[]{:S(2)}) collective-permute-start(bf16[128,1792]{1,0:T(8,128)(2,1)S(1)} %get-tuple-element.29), channel_id=1, source_target_pairs={{0,16},{2,18},{4,20},{6,22},{8,24},{10,26},{12,28},{14,30},{16,0},... | collective-permute-start | bytes 1376264 | tf_op jit(solution)/shard_map/ppermute | solution.py:33
  13.2 1.6 %collective-permute-start = (s32[1,128]{1,0:T(1,128)S(1)}, s32[1,128]{1,0:T(1,128)S(1)}, u32[]{:S(2)}, u32[]{:S(2)}) collective-permute-start(s32[1,128]{1,0:T(1,128)S(1)} %bitcast.22), channel_id=1, source_target_pairs={{0,32},{32,64},{64,96},{96,128},{128,160},{160,192},{192,224},{224... | collective-permute-start | bytes 1544 | tf_op jit(solution)/shard_map/ppermute | solution.py:39
  14.9 3.9 %collective-permute-start.1 = (s32[1,128]{1,0:T(1,128)S(1)}, s32[1,128]{1,0:T(1,128)S(1)}, u32[]{:S(2)}, u32[]{:S(2)}) collective-permute-start(s32[1,128]{1,0:T(1,128)S(1)} %bitcast.24), channel_id=1, source_target_pairs={{0,224},{32,0},{64,32},{96,64},{128,96},{160,128},{192,160},{224,1... | collective-permute-start | bytes 1544 | tf_op jit(solution)/shard_map/ppermute | solution.py:39
  18.8 1.2 %collective-permute-done.ids_f = s32[1,128]{1,0:T(1,128)S(1)} collective-permute-done((s32[1,128]{1,0:T(1,128)S(1)}, s32[1,128]{1,0:T(1,128)S(1)}, u32[]{:S(2)}, u32[]{:S(2)}) %collective-permute-start) | collective-permute-done | bytes 544 | tf_op jit(solution)/shard_map/ppermute | solution.py:39
  20.0 0.0 collective-permute-start.10
  20.0 0.0 collective-permute-done.1.ids_b
  20.0 2.7 %collective-permute-start.11 = (bf16[256,1792]{1,0:T(8,128)(2,1)S(1)}, bf16[256,1792]{1,0:T(8,128)(2,1)S(1)}, u32[]{:S(2)}, u32[]{:S(2)}) collective-permute-start(bf16[256,1792]{1,0:T(8,128)(2,1)S(1)} %bitcast.15), channel_id=1, source_target_pairs={{0,6},{2,0},{4,2},{6,4},{8,14},{10,8},{12,10},{14,12},{16,22},{18,... | collective-permute-start | bytes 2752520 | tf_op jit(solution)/shard_map/ppermute | solution.py:27
  22.7 0.5 shard_map.86
  23.2 0.3 shard_map.88
  23.5 0.7 collective-permute-start.3
  24.2 0.1 shard_map.89
  24.3 9.8 %collective-permute-done.3.refs_0_.r1 = bf16[128,1792]{1,0:T(8,128)(2,1)S(1)} collective-permute-done((bf16[128,1792]{1,0:T(8,128)(2,1)S(1)}, bf16[128,1792]{1,0:T(8,128)(2,1)S(1)}, u32[]{:S(2)}, u32[]{:S(2)}) %collective-permute-start.3) | collective-permute-done | bytes 458784 | tf_op jit(solution)/shard_map/ppermute | solution.py:33
  34.2 0.3 shard_map.90
  34.4 0.0 copy-start
  34.4 1.5 %collective-permute-start.6 = (bf16[128,1792]{1,0:T(8,128)(2,1)S(1)}, bf16[128,1792]{1,0:T(8,128)(2,1)S(1)}, u32[]{:S(2)}, u32[]{:S(2)}) collective-permute-start(bf16[128,1792]{1,0:T(8,128)(2,1)S(1)} %shard_map.90), channel_id=1, source_target_pairs={{0,24},{2,26},{4,28},{6,30},{8,0},{10,2},{12,4},{14,6},{16,8},{18,... | collective-permute-start | bytes 1376264 | tf_op jit(solution)/shard_map/ppermute | solution.py:33
  35.9 0.0 collective-permute-start.7
  35.9 2.7 %collective-permute-start.8 = (bf16[896,256]{1,0:T(8,128)(2,1)S(1)}, bf16[896,256]{1,0:T(8,128)(2,1)S(1)}, u32[]{:S(2)}, u32[]{:S(2)}) collective-permute-start(bf16[896,256]{1,0:T(8,128)(2,1)S(1)} %get-tuple-element.32), channel_id=1, source_target_pairs={{0,6},{2,0},{4,2},{6,4},{8,14},{10,8},{12,10},{14,12},{16,22},{18,... | collective-permute-start | bytes 1376264 | tf_op jit(solution)/shard_map/ppermute | solution.py:27
  38.6 4.8 %collective-permute-done.10.left.refs_1_.v1 = bf16[256,1792]{1,0:T(8,128)(2,1)S(1)} collective-permute-done((bf16[256,1792]{1,0:T(8,128)(2,1)S(1)}, bf16[256,1792]{1,0:T(8,128)(2,1)S(1)}, u32[]{:S(2)}, u32[]{:S(2)}) %collective-permute-start.10) | collective-permute-done | bytes 917536 | tf_op jit(solution)/shard_map/ppermute | solution.py:27
  43.4 0.0 collective-permute-done.11.right.refs_2_.v2
  43.4 0.1 shard_map.92
  43.5 1.4 %collective-permute-start.12 = (bf16[128,1792]{1,0:T(8,128)(2,1)S(1)}, bf16[128,1792]{1,0:T(8,128)(2,1)S(1)}, u32[]{:S(2)}, u32[]{:S(2)}) collective-permute-start(bf16[128,1792]{1,0:T(8,128)(2,1)S(1)} %get-tuple-element.33.token), channel_id=1, source_target_pairs={{0,2},{2,4},{4,6},{6,0},{8,10},{10,12},{12,14},{14,8},{16,18},{18,... | collective-permute-start | bytes 1376264 | tf_op jit(solution)/shard_map/ppermute | solution.py:27
  44.9 1.3 %collective-permute-start.13 = (bf16[128,1792]{1,0:T(8,128)(2,1)S(1)}, bf16[128,1792]{1,0:T(8,128)(2,1)S(1)}, u32[]{:S(2)}, u32[]{:S(2)}) collective-permute-start(bf16[128,1792]{1,0:T(8,128)(2,1)S(1)} %get-tuple-element.34), channel_id=1, source_target_pairs={{0,6},{2,0},{4,2},{6,4},{8,14},{10,8},{12,10},{14,12},{16,22},{18,... | collective-permute-start | bytes 1376264 | tf_op jit(solution)/shard_map/ppermute | solution.py:27
  46.2 1.1 %shard_map.93.token.pu = bf16[320,768]{1,0:T(8,128)(2,1)S(1)} custom-call(bf16[128,1792]{1,0:T(8,128)(2,1)S(1)} %get-tuple-element.27.r0, bf16[128,1792]{1,0:T(8,128)(2,1)S(1)} %collective-permute-done.3.refs_0_.r1, bf16[128,1792]{1,0:T(8,128)(2,1)S(1)} %collective-permute-done.2.refs_0_.r2, bf16[128,1792]{1,0:T(8,128)(2,1)S(1)} %collective-permute-done.6.r3, ...), custom_call_target="tpu_custom_call" | custom-call | flops 880803840 | bytes 4194304 | tf_op jit(solution)/shard_map/pallas_call | solution.py:58
  47.3 4.6 %collective-permute-start.14 = (bf16[320,768]{1,0:T(8,128)(2,1)S(1)}, bf16[320,768]{1,0:T(8,128)(2,1)S(1)}, u32[]{:S(2)}, u32[]{:S(2)}) collective-permute-start(bf16[320,768]{1,0:T(8,128)(2,1)S(1)} %shard_map.93.token.pu), channel_id=1, source_target_pairs={{0,1},{1,0},{2,3},{3,2},{4,5},{5,4},{6,7},{7,6},{8,9},{9,8},{10,11... | collective-permute-start | bytes 1474568 | tf_op jit(solution)/shard_map/ppermute | solution.py:54
  51.9 1.1 %shard_map.94.pv = bf16[192,768]{1,0:T(8,128)(2,1)S(1)} custom-call(bf16[128,1792]{1,0:T(8,128)(2,1)S(1)} %get-tuple-element.27.r0, bf16[128,1792]{1,0:T(8,128)(2,1)S(1)} %collective-permute-done.3.refs_0_.r1, bf16[128,1792]{1,0:T(8,128)(2,1)S(1)} %collective-permute-done.2.refs_0_.r2, bf16[128,1792]{1,0:T(8,128)(2,1)S(1)} %collective-permute-done.6.r3, ...), custom_call_target="tpu_custom_call" | custom-call | flops 587202560 | bytes 4194304 | tf_op jit(solution)/shard_map/pallas_call | solution.py:58
  53.0 0.2 collective-permute-done.7.wa.ua
  53.2 3.2 %collective-permute-start.15 = (bf16[192,768]{1,0:T(8,128)(2,1)S(1)}, bf16[192,768]{1,0:T(8,128)(2,1)S(1)}, u32[]{:S(2)}, u32[]{:S(2)}) collective-permute-start(bf16[192,768]{1,0:T(8,128)(2,1)S(1)} %shard_map.94.pv), channel_id=1, source_target_pairs={{0,1},{1,0},{2,3},{3,2},{4,5},{5,4},{6,7},{7,6},{8,9},{9,8},{10,11... | collective-permute-start | bytes 884744 | tf_op jit(solution)/shard_map/ppermute | solution.py:54
  56.4 0.0 collective-permute-done.8.wb.ub
  56.4 0.5 shard_map.91.pu
  56.9 0.7 collective-permute-start.9
  57.6 0.0 collective-permute-done.15.qv
  57.6 1.4 %shard_map.95 = (f32[160,1792]{1,0:T(8,128)S(1)}, f32[160,1792]{1,0:T(8,128)S(1)}) custom-call(bf16[128,1792]{1,0:T(8,128)(2,1)S(1)} %get-tuple-element.27.r0, bf16[128,1792]{1,0:T(8,128)(2,1)S(1)} %collective-permute-done.3.refs_0_.r1, bf16[128,1792]{1,0:T(8,128)(2,1)S(1)} %collective-permute-done.2.refs_0_.r2, ...), custom_call_target="tpu_custom_call" | custom-call | flops 880803840 | bytes 8388608 | tf_op jit(solution)/shard_map/pallas_call | solution.py:58
  59.1 4.0 %collective-permute-done.12.va = bf16[128,1792]{1,0:T(8,128)(2,1)S(1)} collective-permute-done((bf16[128,1792]{1,0:T(8,128)(2,1)S(1)}, bf16[128,1792]{1,0:T(8,128)(2,1)S(1)}, u32[]{:S(2)}, u32[]{:S(2)}) %collective-permute-start.12) | collective-permute-done | bytes 458784 | tf_op jit(solution)/shard_map/ppermute | solution.py:27
  63.1 0.0 collective-permute-done.13.vb
  63.1 0.8 shard_map.96
  63.9 2.1 %collective-permute-start.17 = (bf16[192,256]{1,0:T(8,128)(2,1)S(1)}, bf16[192,256]{1,0:T(8,128)(2,1)S(1)}, u32[]{:S(2)}, u32[]{:S(2)}) collective-permute-start(bf16[192,256]{1,0:T(8,128)(2,1)S(1)} %get-tuple-element.38.pv), channel_id=1, source_target_pairs={{0,1},{1,0},{2,3},{3,2},{4,5},{5,4},{6,7},{7,6},{8,9},{9,8},{10,11... | collective-permute-start | bytes 294920 | tf_op jit(solution)/shard_map/ppermute | solution.py:54
  66.0 4.3 %collective-permute-start.16 = (bf16[40,1792]{1,0:T(8,128)(2,1)S(1)}, bf16[40,1792]{1,0:T(8,128)(2,1)S(1)}, u32[]{:S(2)}, u32[]{:S(2)}) collective-permute-start(bf16[40,1792]{1,0:T(8,128)(2,1)S(1)} %get-tuple-element.37), channel_id=1, source_target_pairs={{0,48},{2,50},{4,52},{6,54},{8,56},{10,58},{12,60},{14,62},{16,32}... | collective-permute-start | bytes 430088 | tf_op jit(solution)/shard_map/ppermute | solution.py:50
  70.3 2.1 %collective-permute-start.19 = (bf16[40,1792]{1,0:T(8,128)(2,1)S(1)}, bf16[40,1792]{1,0:T(8,128)(2,1)S(1)}, u32[]{:S(2)}, u32[]{:S(2)}) collective-permute-start(bf16[40,1792]{1,0:T(8,128)(2,1)S(1)} %get-tuple-element.41), channel_id=1, source_target_pairs={{0,56},{2,58},{4,60},{6,62},{8,32},{10,34},{12,36},{14,38},{16,40}... | collective-permute-start | bytes 430088 | tf_op jit(solution)/shard_map/ppermute | solution.py:50
  72.4 0.5 shard_map.98
  72.9 1.5 %collective-permute-start.18 = (bf16[40,1792]{1,0:T(8,128)(2,1)S(1)}, bf16[40,1792]{1,0:T(8,128)(2,1)S(1)}, u32[]{:S(2)}, u32[]{:S(2)}) collective-permute-start(bf16[40,1792]{1,0:T(8,128)(2,1)S(1)} %get-tuple-element.40), channel_id=1, source_target_pairs={{0,232},{2,234},{4,236},{6,238},{8,240},{10,242},{12,244},{14,246}... | collective-permute-start | bytes 430088 | tf_op jit(solution)/shard_map/ppermute | solution.py:50
  74.4 1.9 %collective-permute-start.20 = (bf16[40,1792]{1,0:T(8,128)(2,1)S(1)}, bf16[40,1792]{1,0:T(8,128)(2,1)S(1)}, u32[]{:S(2)}, u32[]{:S(2)}) collective-permute-start(bf16[40,1792]{1,0:T(8,128)(2,1)S(1)} %get-tuple-element.42), channel_id=1, source_target_pairs={{0,224},{2,226},{4,228},{6,230},{8,232},{10,234},{12,236},{14,238}... | collective-permute-start | bytes 430088 | tf_op jit(solution)/shard_map/ppermute | solution.py:50
  76.3 0.2 collective-permute-start.21
  76.5 2.8 %collective-permute-done.16.refs_0_ = bf16[40,1792]{1,0:T(8,128)(2,1)S(1)} collective-permute-done((bf16[40,1792]{1,0:T(8,128)(2,1)S(1)}, bf16[40,1792]{1,0:T(8,128)(2,1)S(1)}, u32[]{:S(2)}, u32[]{:S(2)}) %collective-permute-start.16) | collective-permute-done | bytes 143392 | tf_op jit(solution)/shard_map/ppermute | solution.py:50
  79.3 2.4 %collective-permute-start.22 = (bf16[40,1792]{1,0:T(8,128)(2,1)S(1)}, bf16[40,1792]{1,0:T(8,128)(2,1)S(1)}, u32[]{:S(2)}, u32[]{:S(2)}) collective-permute-start(bf16[40,1792]{1,0:T(8,128)(2,1)S(1)} %get-tuple-element.44), channel_id=1, source_target_pairs={{0,248},{2,250},{4,252},{6,254},{8,224},{10,226},{12,228},{14,230}... | collective-permute-start | bytes 430088 | tf_op jit(solution)/shard_map/ppermute | solution.py:50
  81.7 2.5 %collective-permute-start.23 = (bf16[40,1792]{1,0:T(8,128)(2,1)S(1)}, bf16[40,1792]{1,0:T(8,128)(2,1)S(1)}, u32[]{:S(2)}, u32[]{:S(2)}) collective-permute-start(bf16[40,1792]{1,0:T(8,128)(2,1)S(1)} %get-tuple-element.45), channel_id=1, source_target_pairs={{0,240},{2,242},{4,244},{6,246},{8,248},{10,250},{12,252},{14,254}... | collective-permute-start | bytes 430088 | tf_op jit(solution)/shard_map/ppermute | solution.py:50
  84.2 0.0 collective-permute-start.24
  84.2 0.2 shard_map.97.token.refs_0_
  84.5 0.2 shard_map.99.token.refs_0_
  84.7 0.2 shard_map.100.token.refs_0_
  85.0 0.3 shard_map.101.token.refs_0_
  85.3 0.2 shard_map.102.token.total_f
  85.5 0.3 shard_map.103.token.refs_0_
  85.8 3.5 %collective-permute-done.23.refs_1_ = bf16[40,1792]{1,0:T(8,128)(2,1)S(1)} collective-permute-done((bf16[40,1792]{1,0:T(8,128)(2,1)S(1)}, bf16[40,1792]{1,0:T(8,128)(2,1)S(1)}, u32[]{:S(2)}, u32[]{:S(2)}) %collective-permute-start.23) | collective-permute-done | bytes 143392 | tf_op jit(solution)/shard_map/ppermute | solution.py:50
  89.2 0.3 shard_map.104.total_b
  89.5 0.1 collective-permute-done.24.row
  89.6 1.1 %shard_map.105 = (bf16[128,1792]{1,0:T(8,128)(2,1)}, bf16[128,1792]{1,0:T(8,128)(2,1)}) custom-call(bf16[4,128,40]{2,1,0:T(8,128)(2,1)S(1)} %get-tuple-element.25.refs_1_.table, f32[128,1792]{1,0:T(8,128)S(1)} %shard_map.102.token.total_f, f32[128,1792]{1,0:T(8,128)S(1)} %shard_map.104.total_b, bf16[40,1792]{1,0:T(8,128)(2,1)S(1)} %collective-permute-done.24.row), custom_call_target="tpu_custom_call" | custom-call | flops 18350080 | bytes 2752512 | tf_op jit(solution)/shard_map/pallas_call | solution.py:58
  (20 shorter events, 0.0 us)
Async XLA Ops:
  0.6 19.4 %copy-start.1 = (bf16[1,1,256,1792]{3,2,1,0:T(8,128)(2,1)S(1)}, bf16[1,1,256,1792]{3,2,1,0:T(8,128)(2,1)}, u32[]{:S(2)}) copy-start(bf16[1,1,256,1792]{3,2,1,0:T(8,128)(2,1)} %param.13) | copy-start | bytes 2752516
  0.6 23.6 %collective-permute-start.4 = (bf16[1792,256]{1,0:T(8,128)(2,1)}, bf16[1792,256]{1,0:T(8,128)(2,1)S(1)}, u32[]{:S(2)}, u32[]{:S(2)}) collective-permute-start(bf16[1792,256]{1,0:T(8,128)(2,1)} %bitcast.10), channel_id=1, source_target_pairs={{0,2},{2,4},{4,6},{6,0},{8,10},{10,12},{12,14},{14,8},{16,18},{18,... | collective-permute-start | bytes 2752520 | tf_op jit(solution)/shard_map/ppermute | solution.py:27
  2.8 21.5 %collective-permute-start.5 = (bf16[1792,256]{1,0:T(8,128)(2,1)}, bf16[1792,256]{1,0:T(8,128)(2,1)S(1)}, u32[]{:S(2)}, u32[]{:S(2)}) collective-permute-start(bf16[1792,256]{1,0:T(8,128)(2,1)} %bitcast.11), channel_id=1, source_target_pairs={{0,6},{2,0},{4,2},{6,4},{8,14},{10,8},{12,10},{14,12},{16,22},{18,... | collective-permute-start | bytes 2752520 | tf_op jit(solution)/shard_map/ppermute | solution.py:27
  4.1 1.0 %copy-start.2 = (bf16[1,128,1792]{2,1,0:T(8,128)(2,1)S(1)}, bf16[1,128,1792]{2,1,0:T(8,128)(2,1)}, u32[]{:S(2)}) copy-start(bf16[1,128,1792]{2,1,0:T(8,128)(2,1)} %param.7) | copy-start | bytes 1376260
  5.1 1.0 %copy-start.3 = (bf16[1,1,128,1792]{3,2,1,0:T(8,128)(2,1)S(1)}, bf16[1,1,128,1792]{3,2,1,0:T(8,128)(2,1)}, u32[]{:S(2)}) copy-start(bf16[1,1,128,1792]{3,2,1,0:T(8,128)(2,1)} %param.10) | copy-start | bytes 1376260
  6.2 1.0 %copy-start.4 = (bf16[1,128,1792]{2,1,0:T(8,128)(2,1)S(1)}, bf16[1,128,1792]{2,1,0:T(8,128)(2,1)}, u32[]{:S(2)}) copy-start(bf16[1,128,1792]{2,1,0:T(8,128)(2,1)} %param.9) | copy-start | bytes 1376260
  7.2 0.7 copy-start.5
  7.8 0.7 copy-start.6
  10.1 13.1 %collective-permute-start.2 = (bf16[128,1792]{1,0:T(8,128)(2,1)S(1)}, bf16[128,1792]{1,0:T(8,128)(2,1)S(1)}, u32[]{:S(2)}, u32[]{:S(2)}) collective-permute-start(bf16[128,1792]{1,0:T(8,128)(2,1)S(1)} %get-tuple-element.29), channel_id=1, source_target_pairs={{0,16},{2,18},{4,20},{6,22},{8,24},{10,26},{12,28},{14,30},{16,0},... | collective-permute-start | bytes 1376264 | tf_op jit(solution)/shard_map/ppermute | solution.py:33
  13.2 6.8 %collective-permute-start = (s32[1,128]{1,0:T(1,128)S(1)}, s32[1,128]{1,0:T(1,128)S(1)}, u32[]{:S(2)}, u32[]{:S(2)}) collective-permute-start(s32[1,128]{1,0:T(1,128)S(1)} %bitcast.22), channel_id=1, source_target_pairs={{0,32},{32,64},{64,96},{96,128},{128,160},{160,192},{192,224},{224... | collective-permute-start | bytes 1544 | tf_op jit(solution)/shard_map/ppermute | solution.py:39
  14.9 5.2 %collective-permute-start.1 = (s32[1,128]{1,0:T(1,128)S(1)}, s32[1,128]{1,0:T(1,128)S(1)}, u32[]{:S(2)}, u32[]{:S(2)}) collective-permute-start(s32[1,128]{1,0:T(1,128)S(1)} %bitcast.24), channel_id=1, source_target_pairs={{0,224},{32,0},{64,32},{96,64},{128,96},{160,128},{192,160},{224,1... | collective-permute-start | bytes 1544 | tf_op jit(solution)/shard_map/ppermute | solution.py:39
  20.0 23.4 %collective-permute-start.10 = (bf16[256,1792]{1,0:T(8,128)(2,1)S(1)}, bf16[256,1792]{1,0:T(8,128)(2,1)S(1)}, u32[]{:S(2)}, u32[]{:S(2)}) collective-permute-start(bf16[256,1792]{1,0:T(8,128)(2,1)S(1)} %bitcast.14), channel_id=1, source_target_pairs={{0,2},{2,4},{4,6},{6,0},{8,10},{10,12},{12,14},{14,8},{16,18},{18,... | collective-permute-start | bytes 2752520 | tf_op jit(solution)/shard_map/ppermute | solution.py:27
  20.0 23.4 %collective-permute-start.11 = (bf16[256,1792]{1,0:T(8,128)(2,1)S(1)}, bf16[256,1792]{1,0:T(8,128)(2,1)S(1)}, u32[]{:S(2)}, u32[]{:S(2)}) collective-permute-start(bf16[256,1792]{1,0:T(8,128)(2,1)S(1)} %bitcast.15), channel_id=1, source_target_pairs={{0,6},{2,0},{4,2},{6,4},{8,14},{10,8},{12,10},{14,12},{16,22},{18,... | collective-permute-start | bytes 2752520 | tf_op jit(solution)/shard_map/ppermute | solution.py:27
  23.5 10.7 %collective-permute-start.3 = (bf16[128,1792]{1,0:T(8,128)(2,1)S(1)}, bf16[128,1792]{1,0:T(8,128)(2,1)S(1)}, u32[]{:S(2)}, u32[]{:S(2)}) collective-permute-start(bf16[128,1792]{1,0:T(8,128)(2,1)S(1)} %shard_map.88), channel_id=1, source_target_pairs={{0,8},{2,10},{4,12},{6,14},{8,16},{10,18},{12,20},{14,22},{16,24},... | collective-permute-start | bytes 1376264 | tf_op jit(solution)/shard_map/ppermute | solution.py:33
  34.4 11.8 %copy-start = (bf16[1,1,1792,256]{3,2,1,0:T(8,128)(2,1)S(1)}, bf16[1,1,1792,256]{3,2,1,0:T(8,128)(2,1)}, u32[]{:S(2)}) copy-start(bf16[1,1,1792,256]{3,2,1,0:T(8,128)(2,1)} %param.12) | copy-start | bytes 2752516
  34.4 11.8 %collective-permute-start.6 = (bf16[128,1792]{1,0:T(8,128)(2,1)S(1)}, bf16[128,1792]{1,0:T(8,128)(2,1)S(1)}, u32[]{:S(2)}, u32[]{:S(2)}) collective-permute-start(bf16[128,1792]{1,0:T(8,128)(2,1)S(1)} %shard_map.90), channel_id=1, source_target_pairs={{0,24},{2,26},{4,28},{6,30},{8,0},{10,2},{12,4},{14,6},{16,8},{18,... | collective-permute-start | bytes 1376264 | tf_op jit(solution)/shard_map/ppermute | solution.py:33
  35.9 17.3 %collective-permute-start.7 = (bf16[896,256]{1,0:T(8,128)(2,1)S(1)}, bf16[896,256]{1,0:T(8,128)(2,1)S(1)}, u32[]{:S(2)}, u32[]{:S(2)}) collective-permute-start(bf16[896,256]{1,0:T(8,128)(2,1)S(1)} %get-tuple-element.31.refs_1_), channel_id=1, source_target_pairs={{0,2},{2,4},{4,6},{6,0},{8,10},{10,12},{12,14},{14,8},{16,18},{18,... | collective-permute-start | bytes 1376264 | tf_op jit(solution)/shard_map/ppermute | solution.py:27
  35.9 20.5 %collective-permute-start.8 = (bf16[896,256]{1,0:T(8,128)(2,1)S(1)}, bf16[896,256]{1,0:T(8,128)(2,1)S(1)}, u32[]{:S(2)}, u32[]{:S(2)}) collective-permute-start(bf16[896,256]{1,0:T(8,128)(2,1)S(1)} %get-tuple-element.32), channel_id=1, source_target_pairs={{0,6},{2,0},{4,2},{6,4},{8,14},{10,8},{12,10},{14,12},{16,22},{18,... | collective-permute-start | bytes 1376264 | tf_op jit(solution)/shard_map/ppermute | solution.py:27
  43.5 19.6 %collective-permute-start.12 = (bf16[128,1792]{1,0:T(8,128)(2,1)S(1)}, bf16[128,1792]{1,0:T(8,128)(2,1)S(1)}, u32[]{:S(2)}, u32[]{:S(2)}) collective-permute-start(bf16[128,1792]{1,0:T(8,128)(2,1)S(1)} %get-tuple-element.33.token), channel_id=1, source_target_pairs={{0,2},{2,4},{4,6},{6,0},{8,10},{10,12},{12,14},{14,8},{16,18},{18,... | collective-permute-start | bytes 1376264 | tf_op jit(solution)/shard_map/ppermute | solution.py:27
  44.9 18.2 %collective-permute-start.13 = (bf16[128,1792]{1,0:T(8,128)(2,1)S(1)}, bf16[128,1792]{1,0:T(8,128)(2,1)S(1)}, u32[]{:S(2)}, u32[]{:S(2)}) collective-permute-start(bf16[128,1792]{1,0:T(8,128)(2,1)S(1)} %get-tuple-element.34), channel_id=1, source_target_pairs={{0,6},{2,0},{4,2},{6,4},{8,14},{10,8},{12,10},{14,12},{16,22},{18,... | collective-permute-start | bytes 1376264 | tf_op jit(solution)/shard_map/ppermute | solution.py:27
  47.3 10.3 %collective-permute-start.14 = (bf16[320,768]{1,0:T(8,128)(2,1)S(1)}, bf16[320,768]{1,0:T(8,128)(2,1)S(1)}, u32[]{:S(2)}, u32[]{:S(2)}) collective-permute-start(bf16[320,768]{1,0:T(8,128)(2,1)S(1)} %shard_map.93.token.pu), channel_id=1, source_target_pairs={{0,1},{1,0},{2,3},{3,2},{4,5},{5,4},{6,7},{7,6},{8,9},{9,8},{10,11... | collective-permute-start | bytes 1474568 | tf_op jit(solution)/shard_map/ppermute | solution.py:54
  53.2 4.4 %collective-permute-start.15 = (bf16[192,768]{1,0:T(8,128)(2,1)S(1)}, bf16[192,768]{1,0:T(8,128)(2,1)S(1)}, u32[]{:S(2)}, u32[]{:S(2)}) collective-permute-start(bf16[192,768]{1,0:T(8,128)(2,1)S(1)} %shard_map.94.pv), channel_id=1, source_target_pairs={{0,1},{1,0},{2,3},{3,2},{4,5},{5,4},{6,7},{7,6},{8,9},{9,8},{10,11... | collective-permute-start | bytes 884744 | tf_op jit(solution)/shard_map/ppermute | solution.py:54
  56.9 6.1 %collective-permute-start.9 = (bf16[320,256]{1,0:T(8,128)(2,1)S(1)}, bf16[320,256]{1,0:T(8,128)(2,1)S(1)}, u32[]{:S(2)}, u32[]{:S(2)}) collective-permute-start(bf16[320,256]{1,0:T(8,128)(2,1)S(1)} %shard_map.91.pu), channel_id=1, source_target_pairs={{0,1},{1,0},{2,3},{3,2},{4,5},{5,4},{6,7},{7,6},{8,9},{9,8},{10,11... | collective-permute-start | bytes 491528 | tf_op jit(solution)/shard_map/ppermute | solution.py:54
  63.9 8.5 %collective-permute-start.17 = (bf16[192,256]{1,0:T(8,128)(2,1)S(1)}, bf16[192,256]{1,0:T(8,128)(2,1)S(1)}, u32[]{:S(2)}, u32[]{:S(2)}) collective-permute-start(bf16[192,256]{1,0:T(8,128)(2,1)S(1)} %get-tuple-element.38.pv), channel_id=1, source_target_pairs={{0,1},{1,0},{2,3},{3,2},{4,5},{5,4},{6,7},{7,6},{8,9},{9,8},{10,11... | collective-permute-start | bytes 294920 | tf_op jit(solution)/shard_map/ppermute | solution.py:54
  66.0 13.4 %collective-permute-start.16 = (bf16[40,1792]{1,0:T(8,128)(2,1)S(1)}, bf16[40,1792]{1,0:T(8,128)(2,1)S(1)}, u32[]{:S(2)}, u32[]{:S(2)}) collective-permute-start(bf16[40,1792]{1,0:T(8,128)(2,1)S(1)} %get-tuple-element.37), channel_id=1, source_target_pairs={{0,48},{2,50},{4,52},{6,54},{8,56},{10,58},{12,60},{14,62},{16,32}... | collective-permute-start | bytes 430088 | tf_op jit(solution)/shard_map/ppermute | solution.py:50
  70.3 11.5 %collective-permute-start.19 = (bf16[40,1792]{1,0:T(8,128)(2,1)S(1)}, bf16[40,1792]{1,0:T(8,128)(2,1)S(1)}, u32[]{:S(2)}, u32[]{:S(2)}) collective-permute-start(bf16[40,1792]{1,0:T(8,128)(2,1)S(1)} %get-tuple-element.41), channel_id=1, source_target_pairs={{0,56},{2,58},{4,60},{6,62},{8,32},{10,34},{12,36},{14,38},{16,40}... | collective-permute-start | bytes 430088 | tf_op jit(solution)/shard_map/ppermute | solution.py:50
  72.9 11.3 %collective-permute-start.18 = (bf16[40,1792]{1,0:T(8,128)(2,1)S(1)}, bf16[40,1792]{1,0:T(8,128)(2,1)S(1)}, u32[]{:S(2)}, u32[]{:S(2)}) collective-permute-start(bf16[40,1792]{1,0:T(8,128)(2,1)S(1)} %get-tuple-element.40), channel_id=1, source_target_pairs={{0,232},{2,234},{4,236},{6,238},{8,240},{10,242},{12,244},{14,246}... | collective-permute-start | bytes 430088 | tf_op jit(solution)/shard_map/ppermute | solution.py:50
  74.4 10.6 %collective-permute-start.20 = (bf16[40,1792]{1,0:T(8,128)(2,1)S(1)}, bf16[40,1792]{1,0:T(8,128)(2,1)S(1)}, u32[]{:S(2)}, u32[]{:S(2)}) collective-permute-start(bf16[40,1792]{1,0:T(8,128)(2,1)S(1)} %get-tuple-element.42), channel_id=1, source_target_pairs={{0,224},{2,226},{4,228},{6,230},{8,232},{10,234},{12,236},{14,238}... | collective-permute-start | bytes 430088 | tf_op jit(solution)/shard_map/ppermute | solution.py:50
  76.3 8.9 %collective-permute-start.21 = (bf16[40,1792]{1,0:T(8,128)(2,1)S(1)}, bf16[40,1792]{1,0:T(8,128)(2,1)S(1)}, u32[]{:S(2)}, u32[]{:S(2)}) collective-permute-start(bf16[40,1792]{1,0:T(8,128)(2,1)S(1)} %get-tuple-element.43), channel_id=1, source_target_pairs={{0,40},{2,42},{4,44},{6,46},{8,48},{10,50},{12,52},{14,54},{16,56}... | collective-permute-start | bytes 430088 | tf_op jit(solution)/shard_map/ppermute | solution.py:50
  79.3 6.2 %collective-permute-start.22 = (bf16[40,1792]{1,0:T(8,128)(2,1)S(1)}, bf16[40,1792]{1,0:T(8,128)(2,1)S(1)}, u32[]{:S(2)}, u32[]{:S(2)}) collective-permute-start(bf16[40,1792]{1,0:T(8,128)(2,1)S(1)} %get-tuple-element.44), channel_id=1, source_target_pairs={{0,248},{2,250},{4,252},{6,254},{8,224},{10,226},{12,228},{14,230}... | collective-permute-start | bytes 430088 | tf_op jit(solution)/shard_map/ppermute | solution.py:50
  81.7 7.5 %collective-permute-start.23 = (bf16[40,1792]{1,0:T(8,128)(2,1)S(1)}, bf16[40,1792]{1,0:T(8,128)(2,1)S(1)}, u32[]{:S(2)}, u32[]{:S(2)}) collective-permute-start(bf16[40,1792]{1,0:T(8,128)(2,1)S(1)} %get-tuple-element.45), channel_id=1, source_target_pairs={{0,240},{2,242},{4,244},{6,246},{8,248},{10,250},{12,252},{14,254}... | collective-permute-start | bytes 430088 | tf_op jit(solution)/shard_map/ppermute | solution.py:50
  84.2 5.5 %collective-permute-start.24 = (bf16[40,1792]{1,0:T(8,128)(2,1)S(1)}, bf16[40,1792]{1,0:T(8,128)(2,1)S(1)}, u32[]{:S(2)}, u32[]{:S(2)}) collective-permute-start(bf16[40,1792]{1,0:T(8,128)(2,1)S(1)} %get-tuple-element.39.token), channel_id=1, source_target_pairs={{0,32},{2,34},{4,36},{6,38},{8,40},{10,42},{12,44},{14,46},{16,48}... | collective-permute-start | bytes 430088 | tf_op jit(solution)/shard_map/ppermute | solution.py:50

commit v5 on v4

--- a/solution.py
+++ b/solution.py
@@ -210,12 +210,10 @@
 
 def last_f_kernel(r0, r1, r2, r3, pu, qu, va, vb, acc, token, out, *outs):
     rows = jnp.concatenate([r[2 * CAP : ROWS, :] for r in (r0, r1, r2, r3)], axis=0)
-    half = va.shape[0]
-    out[:, :half] = nt(rows, va[...]).astype(BF)
-    out[:, half:] = nt(rows, vb[...]).astype(BF)
+    out[...] = nt(rows, jnp.concatenate([va[...], vb[...]], axis=0)).astype(BF)
     act = activate(added(pu[...], qu[...]))
     for c in columns(acc.shape[1]):
-        t = acc[:, c] + nn(act[:, :half], va[:, c]) + nn(act[:, half:], vb[:, c])
+        t = acc[:, c] + nn(act, jnp.concatenate([va[:, c], vb[:, c]], axis=0))
         for i, o in enumerate(outs):
             o[:, c] = t[i * CAP : (i + 1) * CAP].astype(BF)
 
@@ -223,12 +221,15 @@
 def last_b_kernel(pu, qu, pv, qv, ua, ub, acc, token, *outs, parts):
     hid = grad_hidden(added(pu[...], qu[...]), added(pv[...], qv[...]))
     half = ua.shape[0]
-    for u, base in ((ua, 0), (ub, half)):
-        for c in columns(half, 128):
-            o = slice(base + c.start, base + c.stop)
-            t = acc[:, o] + nt(hid, u[c, :])
-            for i, out in zip(parts, outs):
-                out[:, o] = t[i * CAP : (i + 1) * CAP].astype(BF)
+    for c in columns(acc.shape[1]):
+        pieces = []
+        if c.start < half:
+            pieces.append(ua[c.start : min(c.stop, half), :])
+        if c.stop > half:
+            pieces.append(ub[max(c.start, half) - half : c.stop - half, :])
+        t = acc[:, c] + nt(hid, jnp.concatenate(pieces, axis=0))
+        for i, out in zip(parts, outs):
+            out[:, c] = t[i * CAP : (i + 1) * CAP].astype(BF)
 
 
 def finish_kernel(table, total_f, total_b, row, *refs, stream, group):
@@ -236,15 +237,13 @@
     copies = []
     for k in (1 - stream, stream):
         total = (total_f, total_b)[k]
-        for i, c in enumerate(columns(total.shape[1])):
+        for c in columns(total.shape[1]):
             t = total[:, c]
             if k == stream:
                 t += nn(table[group], row[:, c])
             held[k, :, c] = t.astype(held.dtype)
-            copies.append(
-                pltpu.make_async_copy(held.at[k, :, c], outs[k].at[:, c], sems.at[k, i])
-            )
-            copies[-1].start()
+        copies.append(pltpu.make_async_copy(held.at[k], outs[k], sems.at[k]))
+        copies[-1].start()
     for c in copies:
         c.wait()
 
@@ -431,7 +430,7 @@
             (got_f, got_b)[stream][group],
             scratch=[
                 pltpu.VMEM((2, n, width), BF),
-                pltpu.SemaphoreType.DMA((2, width // 256)),
+                pltpu.SemaphoreType.DMA((2,)),
             ],
             out_specs=[ANY, ANY],
         )

time: 92.5 us -> 92.3 us (level)
  no operation moved by 1% of the time
where the time goes in v5:
time: 92.3 us; the launch traced here: 90.6 us
  starting transfers between devices  48 us (52%)
  waiting for transfers between devices  26.6 us (29%)
  Pallas kernels  10.7 us (12%)
  local copies, waits for them, and re-layouts  4.37 us (5%)
  between operations  0.98 us (1%)
    ppermute x8, starting transfers between devices, move_zy(): return lax.ppermute(v, ('section', 'expert'), pairs)  14.9 us
    ppermute x8, starting transfers between devices, move_x(): lax.ppermute(v, 'expert', [(y * NX + x, y * NX + (x + d) % NX) for y in r...  11.6 us
    pallas_call x20, Pallas kernels, call(): pl.pallas_call(kernel, out_shape=outs, scratch_shapes=scratch, in_specs=i...  10.7 us
    ppermute x4, starting transfers between devices, swap(): return lax.ppermute(v, 'dp', [(0, 1), (1, 0)])  10.6 us
    ppermute x3, waiting for transfers between devices, move_y(): lax.ppermute(v, 'expert', [(y * NX + x, (y + d) % NY * NX + x) for y in r...  9.85 us
    ppermute x8, waiting for transfers between devices, move_x(): lax.ppermute(v, 'expert', [(y * NX + x, y * NX + (x + d) % NX) for y in r...  9.08 us
    ppermute x8, waiting for transfers between devices, move_zy(): return lax.ppermute(v, ('section', 'expert'), pairs)  6.45 us
    ppermute x2, starting transfers between devices, move_z(): return lax.ppermute(v, 'section', [(z, (z + d) % NZ) for z in range(NZ)])  5.58 us
  transfers between devices with their start and end apart: 25, of which 8 were waited for; matrix products, arithmetic and copies ran while one was open for 0% of the time, Pallas kernels for 10%

profile of v5, /device:TPU:1, one launch (start us, length us, event | category | flops | bytes accessed | tf_op | source)
XLA Modules:
  0.0 90.6 jit_solution(16916952945607629761)
XLA Ops:
  0.6 2.1 %collective-permute-start.4 = (bf16[1792,256]{1,0:T(8,128)(2,1)}, bf16[1792,256]{1,0:T(8,128)(2,1)S(1)}, u32[]{:S(2)}, u32[]{:S(2)}) collective-permute-start(bf16[1792,256]{1,0:T(8,128)(2,1)} %bitcast.10), channel_id=1, source_target_pairs={{0,2},{2,4},{4,6},{6,0},{8,10},{10,12},{12,14},{14,8},{16,18},{18,... | collective-permute-start | bytes 2752520 | tf_op jit(solution)/shard_map/ppermute | solution.py:27
  2.8 1.4 %collective-permute-start.5 = (bf16[1792,256]{1,0:T(8,128)(2,1)}, bf16[1792,256]{1,0:T(8,128)(2,1)S(1)}, u32[]{:S(2)}, u32[]{:S(2)}) collective-permute-start(bf16[1792,256]{1,0:T(8,128)(2,1)} %bitcast.11), channel_id=1, source_target_pairs={{0,6},{2,0},{4,2},{6,4},{8,14},{10,8},{12,10},{14,12},{16,22},{18,... | collective-permute-start | bytes 2752520 | tf_op jit(solution)/shard_map/ppermute | solution.py:27
  4.1 1.0 %copy-done.2 = bf16[1,128,1792]{2,1,0:T(8,128)(2,1)S(1)} copy-done((bf16[1,128,1792]{2,1,0:T(8,128)(2,1)S(1)}, bf16[1,128,1792]{2,1,0:T(8,128)(2,1)}, u32[]{:S(2)}) %copy-start.2) | copy-done | bytes 458776
  5.1 1.0 %copy-done.3 = bf16[1,1,128,1792]{3,2,1,0:T(8,128)(2,1)S(1)} copy-done((bf16[1,1,128,1792]{3,2,1,0:T(8,128)(2,1)S(1)}, bf16[1,1,128,1792]{3,2,1,0:T(8,128)(2,1)}, u32[]{:S(2)}) %copy-start.3) | copy-done | bytes 458776
  6.2 1.0 %copy-done.4 = bf16[1,128,1792]{2,1,0:T(8,128)(2,1)S(1)} copy-done((bf16[1,128,1792]{2,1,0:T(8,128)(2,1)S(1)}, bf16[1,128,1792]{2,1,0:T(8,128)(2,1)}, u32[]{:S(2)}) %copy-start.4) | copy-done | bytes 458776
  7.2 0.7 copy-done.5
  7.8 0.7 copy-done.6
  8.5 1.6 %shard_map.87 = (bf16[128,1792]{1,0:T(8,128)(2,1)S(1)}, bf16[128,1792]{1,0:T(8,128)(2,1)S(1)}, bf16[128,1792]{1,0:T(8,128)(2,1)S(1)}, bf16[128,1792]{1,0:T(8,128)(2,1)S(1)}) custom-call(s32[1]{0:T(128)} %bitcast.y_ref, s32[1,128]{1,0:T(1,128)S(1)} %bitcast.21, s32[1,128]{1,0:T(1,128)S(1)} %bitcast.23, bf16[128,1792]{1,0:T(8,128)(2,1)S(1)} %bitcast.18, ...), custom_call_target="tpu_custom_call" | custom-call | flops 220200960 | bytes 3211264 | tf_op jit(solution)/shard_map/pallas_call | solution.py:58
  10.1 3.1 %collective-permute-start.2 = (bf16[128,1792]{1,0:T(8,128)(2,1)S(1)}, bf16[128,1792]{1,0:T(8,128)(2,1)S(1)}, u32[]{:S(2)}, u32[]{:S(2)}) collective-permute-start(bf16[128,1792]{1,0:T(8,128)(2,1)S(1)} %get-tuple-element.29), channel_id=1, source_target_pairs={{0,16},{2,18},{4,20},{6,22},{8,24},{10,26},{12,28},{14,30},{16,0},... | collective-permute-start | bytes 1376264 | tf_op jit(solution)/shard_map/ppermute | solution.py:33
  13.2 1.6 %collective-permute-start = (s32[1,128]{1,0:T(1,128)S(1)}, s32[1,128]{1,0:T(1,128)S(1)}, u32[]{:S(2)}, u32[]{:S(2)}) collective-permute-start(s32[1,128]{1,0:T(1,128)S(1)} %bitcast.22), channel_id=1, source_target_pairs={{0,32},{32,64},{64,96},{96,128},{128,160},{160,192},{192,224},{224... | collective-permute-start | bytes 1544 | tf_op jit(solution)/shard_map/ppermute | solution.py:39
  14.9 3.9 %collective-permute-start.1 = (s32[1,128]{1,0:T(1,128)S(1)}, s32[1,128]{1,0:T(1,128)S(1)}, u32[]{:S(2)}, u32[]{:S(2)}) collective-permute-start(s32[1,128]{1,0:T(1,128)S(1)} %bitcast.24), channel_id=1, source_target_pairs={{0,224},{32,0},{64,32},{96,64},{128,96},{160,128},{192,160},{224,1... | collective-permute-start | bytes 1544 | tf_op jit(solution)/shard_map/ppermute | solution.py:39
  18.8 1.2 %collective-permute-done.ids_f = s32[1,128]{1,0:T(1,128)S(1)} collective-permute-done((s32[1,128]{1,0:T(1,128)S(1)}, s32[1,128]{1,0:T(1,128)S(1)}, u32[]{:S(2)}, u32[]{:S(2)}) %collective-permute-start) | collective-permute-done | bytes 544 | tf_op jit(solution)/shard_map/ppermute | solution.py:39
  20.0 0.0 collective-permute-start.10
  20.0 0.0 collective-permute-done.1.ids_b
  20.0 2.7 %collective-permute-start.11 = (bf16[256,1792]{1,0:T(8,128)(2,1)S(1)}, bf16[256,1792]{1,0:T(8,128)(2,1)S(1)}, u32[]{:S(2)}, u32[]{:S(2)}) collective-permute-start(bf16[256,1792]{1,0:T(8,128)(2,1)S(1)} %bitcast.15), channel_id=1, source_target_pairs={{0,6},{2,0},{4,2},{6,4},{8,14},{10,8},{12,10},{14,12},{16,22},{18,... | collective-permute-start | bytes 2752520 | tf_op jit(solution)/shard_map/ppermute | solution.py:27
  22.7 0.5 shard_map.86
  23.2 0.3 shard_map.88
  23.5 0.7 collective-permute-start.3
  24.2 0.1 shard_map.89
  24.3 9.8 %collective-permute-done.3.refs_0_.r1 = bf16[128,1792]{1,0:T(8,128)(2,1)S(1)} collective-permute-done((bf16[128,1792]{1,0:T(8,128)(2,1)S(1)}, bf16[128,1792]{1,0:T(8,128)(2,1)S(1)}, u32[]{:S(2)}, u32[]{:S(2)}) %collective-permute-start.3) | collective-permute-done | bytes 458784 | tf_op jit(solution)/shard_map/ppermute | solution.py:33
  34.2 0.3 shard_map.90
  34.4 0.0 copy-start
  34.4 1.5 %collective-permute-start.6 = (bf16[128,1792]{1,0:T(8,128)(2,1)S(1)}, bf16[128,1792]{1,0:T(8,128)(2,1)S(1)}, u32[]{:S(2)}, u32[]{:S(2)}) collective-permute-start(bf16[128,1792]{1,0:T(8,128)(2,1)S(1)} %shard_map.90), channel_id=1, source_target_pairs={{0,24},{2,26},{4,28},{6,30},{8,0},{10,2},{12,4},{14,6},{16,8},{18,... | collective-permute-start | bytes 1376264 | tf_op jit(solution)/shard_map/ppermute | solution.py:33
  35.9 0.0 collective-permute-start.7
  35.9 2.7 %collective-permute-start.8 = (bf16[896,256]{1,0:T(8,128)(2,1)S(1)}, bf16[896,256]{1,0:T(8,128)(2,1)S(1)}, u32[]{:S(2)}, u32[]{:S(2)}) collective-permute-start(bf16[896,256]{1,0:T(8,128)(2,1)S(1)} %get-tuple-element.32), channel_id=1, source_target_pairs={{0,6},{2,0},{4,2},{6,4},{8,14},{10,8},{12,10},{14,12},{16,22},{18,... | collective-permute-start | bytes 1376264 | tf_op jit(solution)/shard_map/ppermute | solution.py:27
  38.6 4.8 %collective-permute-done.10.left.refs_1_.v1 = bf16[256,1792]{1,0:T(8,128)(2,1)S(1)} collective-permute-done((bf16[256,1792]{1,0:T(8,128)(2,1)S(1)}, bf16[256,1792]{1,0:T(8,128)(2,1)S(1)}, u32[]{:S(2)}, u32[]{:S(2)}) %collective-permute-start.10) | collective-permute-done | bytes 917536 | tf_op jit(solution)/shard_map/ppermute | solution.py:27
  43.4 0.0 collective-permute-done.11.right.refs_2_.v2
  43.4 0.1 shard_map.92
  43.5 1.4 %collective-permute-start.12 = (bf16[128,1792]{1,0:T(8,128)(2,1)S(1)}, bf16[128,1792]{1,0:T(8,128)(2,1)S(1)}, u32[]{:S(2)}, u32[]{:S(2)}) collective-permute-start(bf16[128,1792]{1,0:T(8,128)(2,1)S(1)} %get-tuple-element.33.token), channel_id=1, source_target_pairs={{0,2},{2,4},{4,6},{6,0},{8,10},{10,12},{12,14},{14,8},{16,18},{18,... | collective-permute-start | bytes 1376264 | tf_op jit(solution)/shard_map/ppermute | solution.py:27
  44.9 1.3 %collective-permute-start.13 = (bf16[128,1792]{1,0:T(8,128)(2,1)S(1)}, bf16[128,1792]{1,0:T(8,128)(2,1)S(1)}, u32[]{:S(2)}, u32[]{:S(2)}) collective-permute-start(bf16[128,1792]{1,0:T(8,128)(2,1)S(1)} %get-tuple-element.34), channel_id=1, source_target_pairs={{0,6},{2,0},{4,2},{6,4},{8,14},{10,8},{12,10},{14,12},{16,22},{18,... | collective-permute-start | bytes 1376264 | tf_op jit(solution)/shard_map/ppermute | solution.py:27
  46.2 1.1 %shard_map.93.token.pu = bf16[320,768]{1,0:T(8,128)(2,1)S(1)} custom-call(bf16[128,1792]{1,0:T(8,128)(2,1)S(1)} %get-tuple-element.27.r0, bf16[128,1792]{1,0:T(8,128)(2,1)S(1)} %collective-permute-done.3.refs_0_.r1, bf16[128,1792]{1,0:T(8,128)(2,1)S(1)} %collective-permute-done.2.refs_0_.r2, bf16[128,1792]{1,0:T(8,128)(2,1)S(1)} %collective-permute-done.6.r3, ...), custom_call_target="tpu_custom_call" | custom-call | flops 880803840 | bytes 4194304 | tf_op jit(solution)/shard_map/pallas_call | solution.py:58
  47.3 4.6 %collective-permute-start.14 = (bf16[320,768]{1,0:T(8,128)(2,1)S(1)}, bf16[320,768]{1,0:T(8,128)(2,1)S(1)}, u32[]{:S(2)}, u32[]{:S(2)}) collective-permute-start(bf16[320,768]{1,0:T(8,128)(2,1)S(1)} %shard_map.93.token.pu), channel_id=1, source_target_pairs={{0,1},{1,0},{2,3},{3,2},{4,5},{5,4},{6,7},{7,6},{8,9},{9,8},{10,11... | collective-permute-start | bytes 1474568 | tf_op jit(solution)/shard_map/ppermute | solution.py:54
  51.9 1.1 %shard_map.94.pv = bf16[192,768]{1,0:T(8,128)(2,1)S(1)} custom-call(bf16[128,1792]{1,0:T(8,128)(2,1)S(1)} %get-tuple-element.27.r0, bf16[128,1792]{1,0:T(8,128)(2,1)S(1)} %collective-permute-done.3.refs_0_.r1, bf16[128,1792]{1,0:T(8,128)(2,1)S(1)} %collective-permute-done.2.refs_0_.r2, bf16[128,1792]{1,0:T(8,128)(2,1)S(1)} %collective-permute-done.6.r3, ...), custom_call_target="tpu_custom_call" | custom-call | flops 587202560 | bytes 4194304 | tf_op jit(solution)/shard_map/pallas_call | solution.py:58
  53.0 0.2 collective-permute-done.7.wa.ua
  53.2 3.2 %collective-permute-start.15 = (bf16[192,768]{1,0:T(8,128)(2,1)S(1)}, bf16[192,768]{1,0:T(8,128)(2,1)S(1)}, u32[]{:S(2)}, u32[]{:S(2)}) collective-permute-start(bf16[192,768]{1,0:T(8,128)(2,1)S(1)} %shard_map.94.pv), channel_id=1, source_target_pairs={{0,1},{1,0},{2,3},{3,2},{4,5},{5,4},{6,7},{7,6},{8,9},{9,8},{10,11... | collective-permute-start | bytes 884744 | tf_op jit(solution)/shard_map/ppermute | solution.py:54
  56.4 0.0 collective-permute-done.8.wb.ub
  56.4 0.5 shard_map.91.pu
  56.9 0.7 collective-permute-start.9
  57.6 0.0 collective-permute-done.15.qv
  57.6 0.0 collective-permute-done.14.qu
  57.6 1.4 %shard_map.95 = (f32[160,1792]{1,0:T(8,128)S(1)}, f32[160,1792]{1,0:T(8,128)S(1)}) custom-call(bf16[128,1792]{1,0:T(8,128)(2,1)S(1)} %get-tuple-element.27.r0, bf16[128,1792]{1,0:T(8,128)(2,1)S(1)} %collective-permute-done.3.refs_0_.r1, bf16[128,1792]{1,0:T(8,128)(2,1)S(1)} %collective-permute-done.2.refs_0_.r2, ...), custom_call_target="tpu_custom_call" | custom-call | flops 880803840 | bytes 8388608 | tf_op jit(solution)/shard_map/pallas_call | solution.py:58
  59.1 4.0 %collective-permute-done.12.va = bf16[128,1792]{1,0:T(8,128)(2,1)S(1)} collective-permute-done((bf16[128,1792]{1,0:T(8,128)(2,1)S(1)}, bf16[128,1792]{1,0:T(8,128)(2,1)S(1)}, u32[]{:S(2)}, u32[]{:S(2)}) %collective-permute-start.12) | collective-permute-done | bytes 458784 | tf_op jit(solution)/shard_map/ppermute | solution.py:27
  63.1 0.6 shard_map.96
  63.7 2.1 %collective-permute-start.17 = (bf16[192,256]{1,0:T(8,128)(2,1)S(1)}, bf16[192,256]{1,0:T(8,128)(2,1)S(1)}, u32[]{:S(2)}, u32[]{:S(2)}) collective-permute-start(bf16[192,256]{1,0:T(8,128)(2,1)S(1)} %get-tuple-element.38.pv), channel_id=1, source_target_pairs={{0,1},{1,0},{2,3},{3,2},{4,5},{5,4},{6,7},{7,6},{8,9},{9,8},{10,11... | collective-permute-start | bytes 294920 | tf_op jit(solution)/shard_map/ppermute | solution.py:54
  65.8 4.3 %collective-permute-start.16 = (bf16[40,1792]{1,0:T(8,128)(2,1)S(1)}, bf16[40,1792]{1,0:T(8,128)(2,1)S(1)}, u32[]{:S(2)}, u32[]{:S(2)}) collective-permute-start(bf16[40,1792]{1,0:T(8,128)(2,1)S(1)} %get-tuple-element.37), channel_id=1, source_target_pairs={{0,48},{2,50},{4,52},{6,54},{8,56},{10,58},{12,60},{14,62},{16,32}... | collective-permute-start | bytes 430088 | tf_op jit(solution)/shard_map/ppermute | solution.py:50
  70.0 2.1 %collective-permute-start.19 = (bf16[40,1792]{1,0:T(8,128)(2,1)S(1)}, bf16[40,1792]{1,0:T(8,128)(2,1)S(1)}, u32[]{:S(2)}, u32[]{:S(2)}) collective-permute-start(bf16[40,1792]{1,0:T(8,128)(2,1)S(1)} %get-tuple-element.41), channel_id=1, source_target_pairs={{0,56},{2,58},{4,60},{6,62},{8,32},{10,34},{12,36},{14,38},{16,40}... | collective-permute-start | bytes 430088 | tf_op jit(solution)/shard_map/ppermute | solution.py:50
  72.2 0.5 shard_map.98
  72.6 1.5 %collective-permute-start.18 = (bf16[40,1792]{1,0:T(8,128)(2,1)S(1)}, bf16[40,1792]{1,0:T(8,128)(2,1)S(1)}, u32[]{:S(2)}, u32[]{:S(2)}) collective-permute-start(bf16[40,1792]{1,0:T(8,128)(2,1)S(1)} %get-tuple-element.40), channel_id=1, source_target_pairs={{0,232},{2,234},{4,236},{6,238},{8,240},{10,242},{12,244},{14,246}... | collective-permute-start | bytes 430088 | tf_op jit(solution)/shard_map/ppermute | solution.py:50
  74.2 1.9 %collective-permute-start.20 = (bf16[40,1792]{1,0:T(8,128)(2,1)S(1)}, bf16[40,1792]{1,0:T(8,128)(2,1)S(1)}, u32[]{:S(2)}, u32[]{:S(2)}) collective-permute-start(bf16[40,1792]{1,0:T(8,128)(2,1)S(1)} %get-tuple-element.42), channel_id=1, source_target_pairs={{0,224},{2,226},{4,228},{6,230},{8,232},{10,234},{12,236},{14,238}... | collective-permute-start | bytes 430088 | tf_op jit(solution)/shard_map/ppermute | solution.py:50
  76.1 0.2 collective-permute-start.21
  76.3 2.8 %collective-permute-done.16.refs_0_ = bf16[40,1792]{1,0:T(8,128)(2,1)S(1)} collective-permute-done((bf16[40,1792]{1,0:T(8,128)(2,1)S(1)}, bf16[40,1792]{1,0:T(8,128)(2,1)S(1)}, u32[]{:S(2)}, u32[]{:S(2)}) %collective-permute-start.16) | collective-permute-done | bytes 143392 | tf_op jit(solution)/shard_map/ppermute | solution.py:50
  79.1 2.4 %collective-permute-start.22 = (bf16[40,1792]{1,0:T(8,128)(2,1)S(1)}, bf16[40,1792]{1,0:T(8,128)(2,1)S(1)}, u32[]{:S(2)}, u32[]{:S(2)}) collective-permute-start(bf16[40,1792]{1,0:T(8,128)(2,1)S(1)} %get-tuple-element.44), channel_id=1, source_target_pairs={{0,248},{2,250},{4,252},{6,254},{8,224},{10,226},{12,228},{14,230}... | collective-permute-start | bytes 430088 | tf_op jit(solution)/shard_map/ppermute | solution.py:50
  81.5 2.5 %collective-permute-start.23 = (bf16[40,1792]{1,0:T(8,128)(2,1)S(1)}, bf16[40,1792]{1,0:T(8,128)(2,1)S(1)}, u32[]{:S(2)}, u32[]{:S(2)}) collective-permute-start(bf16[40,1792]{1,0:T(8,128)(2,1)S(1)} %get-tuple-element.45), channel_id=1, source_target_pairs={{0,240},{2,242},{4,244},{6,246},{8,248},{10,250},{12,252},{14,254}... | collective-permute-start | bytes 430088 | tf_op jit(solution)/shard_map/ppermute | solution.py:50
  84.0 0.0 collective-permute-start.24
  84.0 0.2 shard_map.97.token.refs_0_
  84.2 0.3 shard_map.99.token.refs_0_
  84.5 0.2 shard_map.100.token.refs_0_
  84.8 0.2 shard_map.101.token.refs_0_
  85.0 0.3 shard_map.102.token.total_f
  85.3 0.3 shard_map.103.token.refs_0_
  85.6 3.4 %collective-permute-done.23.refs_1_ = bf16[40,1792]{1,0:T(8,128)(2,1)S(1)} collective-permute-done((bf16[40,1792]{1,0:T(8,128)(2,1)S(1)}, bf16[40,1792]{1,0:T(8,128)(2,1)S(1)}, u32[]{:S(2)}, u32[]{:S(2)}) %collective-permute-start.23) | collective-permute-done | bytes 143392 | tf_op jit(solution)/shard_map/ppermute | solution.py:50
  89.0 0.2 shard_map.104.total_b
  89.3 0.2 collective-permute-done.24.row
  89.4 1.0 %shard_map.105 = (bf16[128,1792]{1,0:T(8,128)(2,1)}, bf16[128,1792]{1,0:T(8,128)(2,1)}) custom-call(bf16[4,128,40]{2,1,0:T(8,128)(2,1)S(1)} %get-tuple-element.25.refs_1_.table, f32[128,1792]{1,0:T(8,128)S(1)} %shard_map.102.token.total_f, f32[128,1792]{1,0:T(8,128)S(1)} %shard_map.104.total_b, bf16[40,1792]{1,0:T(8,128)(2,1)S(1)} %collective-permute-done.24.row), custom_call_target="tpu_custom_call" | custom-call | flops 18350080 | bytes 2752512 | tf_op jit(solution)/shard_map/pallas_call | solution.py:58
  (20 shorter events, 0.0 us)
Async XLA Ops:
  0.6 19.4 %copy-start.1 = (bf16[1,1,256,1792]{3,2,1,0:T(8,128)(2,1)S(1)}, bf16[1,1,256,1792]{3,2,1,0:T(8,128)(2,1)}, u32[]{:S(2)}) copy-start(bf16[1,1,256,1792]{3,2,1,0:T(8,128)(2,1)} %param.13) | copy-start | bytes 2752516
  0.6 23.6 %collective-permute-start.4 = (bf16[1792,256]{1,0:T(8,128)(2,1)}, bf16[1792,256]{1,0:T(8,128)(2,1)S(1)}, u32[]{:S(2)}, u32[]{:S(2)}) collective-permute-start(bf16[1792,256]{1,0:T(8,128)(2,1)} %bitcast.10), channel_id=1, source_target_pairs={{0,2},{2,4},{4,6},{6,0},{8,10},{10,12},{12,14},{14,8},{16,18},{18,... | collective-permute-start | bytes 2752520 | tf_op jit(solution)/shard_map/ppermute | solution.py:27
  2.8 21.5 %collective-permute-start.5 = (bf16[1792,256]{1,0:T(8,128)(2,1)}, bf16[1792,256]{1,0:T(8,128)(2,1)S(1)}, u32[]{:S(2)}, u32[]{:S(2)}) collective-permute-start(bf16[1792,256]{1,0:T(8,128)(2,1)} %bitcast.11), channel_id=1, source_target_pairs={{0,6},{2,0},{4,2},{6,4},{8,14},{10,8},{12,10},{14,12},{16,22},{18,... | collective-permute-start | bytes 2752520 | tf_op jit(solution)/shard_map/ppermute | solution.py:27
  4.1 1.0 %copy-start.2 = (bf16[1,128,1792]{2,1,0:T(8,128)(2,1)S(1)}, bf16[1,128,1792]{2,1,0:T(8,128)(2,1)}, u32[]{:S(2)}) copy-start(bf16[1,128,1792]{2,1,0:T(8,128)(2,1)} %param.7) | copy-start | bytes 1376260
  5.1 1.0 %copy-start.3 = (bf16[1,1,128,1792]{3,2,1,0:T(8,128)(2,1)S(1)}, bf16[1,1,128,1792]{3,2,1,0:T(8,128)(2,1)}, u32[]{:S(2)}) copy-start(bf16[1,1,128,1792]{3,2,1,0:T(8,128)(2,1)} %param.10) | copy-start | bytes 1376260
  6.2 1.0 %copy-start.4 = (bf16[1,128,1792]{2,1,0:T(8,128)(2,1)S(1)}, bf16[1,128,1792]{2,1,0:T(8,128)(2,1)}, u32[]{:S(2)}) copy-start(bf16[1,128,1792]{2,1,0:T(8,128)(2,1)} %param.9) | copy-start | bytes 1376260
  7.2 0.7 copy-start.5
  7.8 0.7 copy-start.6
  10.1 13.1 %collective-permute-start.2 = (bf16[128,1792]{1,0:T(8,128)(2,1)S(1)}, bf16[128,1792]{1,0:T(8,128)(2,1)S(1)}, u32[]{:S(2)}, u32[]{:S(2)}) collective-permute-start(bf16[128,1792]{1,0:T(8,128)(2,1)S(1)} %get-tuple-element.29), channel_id=1, source_target_pairs={{0,16},{2,18},{4,20},{6,22},{8,24},{10,26},{12,28},{14,30},{16,0},... | collective-permute-start | bytes 1376264 | tf_op jit(solution)/shard_map/ppermute | solution.py:33
  13.2 6.8 %collective-permute-start = (s32[1,128]{1,0:T(1,128)S(1)}, s32[1,128]{1,0:T(1,128)S(1)}, u32[]{:S(2)}, u32[]{:S(2)}) collective-permute-start(s32[1,128]{1,0:T(1,128)S(1)} %bitcast.22), channel_id=1, source_target_pairs={{0,32},{32,64},{64,96},{96,128},{128,160},{160,192},{192,224},{224... | collective-permute-start | bytes 1544 | tf_op jit(solution)/shard_map/ppermute | solution.py:39
  14.9 5.2 %collective-permute-start.1 = (s32[1,128]{1,0:T(1,128)S(1)}, s32[1,128]{1,0:T(1,128)S(1)}, u32[]{:S(2)}, u32[]{:S(2)}) collective-permute-start(s32[1,128]{1,0:T(1,128)S(1)} %bitcast.24), channel_id=1, source_target_pairs={{0,224},{32,0},{64,32},{96,64},{128,96},{160,128},{192,160},{224,1... | collective-permute-start | bytes 1544 | tf_op jit(solution)/shard_map/ppermute | solution.py:39
  20.0 23.4 %collective-permute-start.10 = (bf16[256,1792]{1,0:T(8,128)(2,1)S(1)}, bf16[256,1792]{1,0:T(8,128)(2,1)S(1)}, u32[]{:S(2)}, u32[]{:S(2)}) collective-permute-start(bf16[256,1792]{1,0:T(8,128)(2,1)S(1)} %bitcast.14), channel_id=1, source_target_pairs={{0,2},{2,4},{4,6},{6,0},{8,10},{10,12},{12,14},{14,8},{16,18},{18,... | collective-permute-start | bytes 2752520 | tf_op jit(solution)/shard_map/ppermute | solution.py:27
  20.0 23.4 %collective-permute-start.11 = (bf16[256,1792]{1,0:T(8,128)(2,1)S(1)}, bf16[256,1792]{1,0:T(8,128)(2,1)S(1)}, u32[]{:S(2)}, u32[]{:S(2)}) collective-permute-start(bf16[256,1792]{1,0:T(8,128)(2,1)S(1)} %bitcast.15), channel_id=1, source_target_pairs={{0,6},{2,0},{4,2},{6,4},{8,14},{10,8},{12,10},{14,12},{16,22},{18,... | collective-permute-start | bytes 2752520 | tf_op jit(solution)/shard_map/ppermute | solution.py:27
  23.5 10.7 %collective-permute-start.3 = (bf16[128,1792]{1,0:T(8,128)(2,1)S(1)}, bf16[128,1792]{1,0:T(8,128)(2,1)S(1)}, u32[]{:S(2)}, u32[]{:S(2)}) collective-permute-start(bf16[128,1792]{1,0:T(8,128)(2,1)S(1)} %shard_map.88), channel_id=1, source_target_pairs={{0,8},{2,10},{4,12},{6,14},{8,16},{10,18},{12,20},{14,22},{16,24},... | collective-permute-start | bytes 1376264 | tf_op jit(solution)/shard_map/ppermute | solution.py:33
  34.4 11.8 %copy-start = (bf16[1,1,1792,256]{3,2,1,0:T(8,128)(2,1)S(1)}, bf16[1,1,1792,256]{3,2,1,0:T(8,128)(2,1)}, u32[]{:S(2)}) copy-start(bf16[1,1,1792,256]{3,2,1,0:T(8,128)(2,1)} %param.12) | copy-start | bytes 2752516
  34.4 11.8 %collective-permute-start.6 = (bf16[128,1792]{1,0:T(8,128)(2,1)S(1)}, bf16[128,1792]{1,0:T(8,128)(2,1)S(1)}, u32[]{:S(2)}, u32[]{:S(2)}) collective-permute-start(bf16[128,1792]{1,0:T(8,128)(2,1)S(1)} %shard_map.90), channel_id=1, source_target_pairs={{0,24},{2,26},{4,28},{6,30},{8,0},{10,2},{12,4},{14,6},{16,8},{18,... | collective-permute-start | bytes 1376264 | tf_op jit(solution)/shard_map/ppermute | solution.py:33
  35.9 17.3 %collective-permute-start.7 = (bf16[896,256]{1,0:T(8,128)(2,1)S(1)}, bf16[896,256]{1,0:T(8,128)(2,1)S(1)}, u32[]{:S(2)}, u32[]{:S(2)}) collective-permute-start(bf16[896,256]{1,0:T(8,128)(2,1)S(1)} %get-tuple-element.31.refs_1_), channel_id=1, source_target_pairs={{0,2},{2,4},{4,6},{6,0},{8,10},{10,12},{12,14},{14,8},{16,18},{18,... | collective-permute-start | bytes 1376264 | tf_op jit(solution)/shard_map/ppermute | solution.py:27
  35.9 20.5 %collective-permute-start.8 = (bf16[896,256]{1,0:T(8,128)(2,1)S(1)}, bf16[896,256]{1,0:T(8,128)(2,1)S(1)}, u32[]{:S(2)}, u32[]{:S(2)}) collective-permute-start(bf16[896,256]{1,0:T(8,128)(2,1)S(1)} %get-tuple-element.32), channel_id=1, source_target_pairs={{0,6},{2,0},{4,2},{6,4},{8,14},{10,8},{12,10},{14,12},{16,22},{18,... | collective-permute-start | bytes 1376264 | tf_op jit(solution)/shard_map/ppermute | solution.py:27
  43.5 19.6 %collective-permute-start.12 = (bf16[128,1792]{1,0:T(8,128)(2,1)S(1)}, bf16[128,1792]{1,0:T(8,128)(2,1)S(1)}, u32[]{:S(2)}, u32[]{:S(2)}) collective-permute-start(bf16[128,1792]{1,0:T(8,128)(2,1)S(1)} %get-tuple-element.33.token), channel_id=1, source_target_pairs={{0,2},{2,4},{4,6},{6,0},{8,10},{10,12},{12,14},{14,8},{16,18},{18,... | collective-permute-start | bytes 1376264 | tf_op jit(solution)/shard_map/ppermute | solution.py:27
  44.9 18.2 %collective-permute-start.13 = (bf16[128,1792]{1,0:T(8,128)(2,1)S(1)}, bf16[128,1792]{1,0:T(8,128)(2,1)S(1)}, u32[]{:S(2)}, u32[]{:S(2)}) collective-permute-start(bf16[128,1792]{1,0:T(8,128)(2,1)S(1)} %get-tuple-element.34), channel_id=1, source_target_pairs={{0,6},{2,0},{4,2},{6,4},{8,14},{10,8},{12,10},{14,12},{16,22},{18,... | collective-permute-start | bytes 1376264 | tf_op jit(solution)/shard_map/ppermute | solution.py:27
  47.3 10.3 %collective-permute-start.14 = (bf16[320,768]{1,0:T(8,128)(2,1)S(1)}, bf16[320,768]{1,0:T(8,128)(2,1)S(1)}, u32[]{:S(2)}, u32[]{:S(2)}) collective-permute-start(bf16[320,768]{1,0:T(8,128)(2,1)S(1)} %shard_map.93.token.pu), channel_id=1, source_target_pairs={{0,1},{1,0},{2,3},{3,2},{4,5},{5,4},{6,7},{7,6},{8,9},{9,8},{10,11... | collective-permute-start | bytes 1474568 | tf_op jit(solution)/shard_map/ppermute | solution.py:54
  53.2 4.4 %collective-permute-start.15 = (bf16[192,768]{1,0:T(8,128)(2,1)S(1)}, bf16[192,768]{1,0:T(8,128)(2,1)S(1)}, u32[]{:S(2)}, u32[]{:S(2)}) collective-permute-start(bf16[192,768]{1,0:T(8,128)(2,1)S(1)} %shard_map.94.pv), channel_id=1, source_target_pairs={{0,1},{1,0},{2,3},{3,2},{4,5},{5,4},{6,7},{7,6},{8,9},{9,8},{10,11... | collective-permute-start | bytes 884744 | tf_op jit(solution)/shard_map/ppermute | solution.py:54
  56.9 6.1 %collective-permute-start.9 = (bf16[320,256]{1,0:T(8,128)(2,1)S(1)}, bf16[320,256]{1,0:T(8,128)(2,1)S(1)}, u32[]{:S(2)}, u32[]{:S(2)}) collective-permute-start(bf16[320,256]{1,0:T(8,128)(2,1)S(1)} %shard_map.91.pu), channel_id=1, source_target_pairs={{0,1},{1,0},{2,3},{3,2},{4,5},{5,4},{6,7},{7,6},{8,9},{9,8},{10,11... | collective-permute-start | bytes 491528 | tf_op jit(solution)/shard_map/ppermute | solution.py:54
  63.7 8.5 %collective-permute-start.17 = (bf16[192,256]{1,0:T(8,128)(2,1)S(1)}, bf16[192,256]{1,0:T(8,128)(2,1)S(1)}, u32[]{:S(2)}, u32[]{:S(2)}) collective-permute-start(bf16[192,256]{1,0:T(8,128)(2,1)S(1)} %get-tuple-element.38.pv), channel_id=1, source_target_pairs={{0,1},{1,0},{2,3},{3,2},{4,5},{5,4},{6,7},{7,6},{8,9},{9,8},{10,11... | collective-permute-start | bytes 294920 | tf_op jit(solution)/shard_map/ppermute | solution.py:54
  65.8 13.4 %collective-permute-start.16 = (bf16[40,1792]{1,0:T(8,128)(2,1)S(1)}, bf16[40,1792]{1,0:T(8,128)(2,1)S(1)}, u32[]{:S(2)}, u32[]{:S(2)}) collective-permute-start(bf16[40,1792]{1,0:T(8,128)(2,1)S(1)} %get-tuple-element.37), channel_id=1, source_target_pairs={{0,48},{2,50},{4,52},{6,54},{8,56},{10,58},{12,60},{14,62},{16,32}... | collective-permute-start | bytes 430088 | tf_op jit(solution)/shard_map/ppermute | solution.py:50
  70.0 11.5 %collective-permute-start.19 = (bf16[40,1792]{1,0:T(8,128)(2,1)S(1)}, bf16[40,1792]{1,0:T(8,128)(2,1)S(1)}, u32[]{:S(2)}, u32[]{:S(2)}) collective-permute-start(bf16[40,1792]{1,0:T(8,128)(2,1)S(1)} %get-tuple-element.41), channel_id=1, source_target_pairs={{0,56},{2,58},{4,60},{6,62},{8,32},{10,34},{12,36},{14,38},{16,40}... | collective-permute-start | bytes 430088 | tf_op jit(solution)/shard_map/ppermute | solution.py:50
  72.6 11.3 %collective-permute-start.18 = (bf16[40,1792]{1,0:T(8,128)(2,1)S(1)}, bf16[40,1792]{1,0:T(8,128)(2,1)S(1)}, u32[]{:S(2)}, u32[]{:S(2)}) collective-permute-start(bf16[40,1792]{1,0:T(8,128)(2,1)S(1)} %get-tuple-element.40), channel_id=1, source_target_pairs={{0,232},{2,234},{4,236},{6,238},{8,240},{10,242},{12,244},{14,246}... | collective-permute-start | bytes 430088 | tf_op jit(solution)/shard_map/ppermute | solution.py:50
  74.2 10.6 %collective-permute-start.20 = (bf16[40,1792]{1,0:T(8,128)(2,1)S(1)}, bf16[40,1792]{1,0:T(8,128)(2,1)S(1)}, u32[]{:S(2)}, u32[]{:S(2)}) collective-permute-start(bf16[40,1792]{1,0:T(8,128)(2,1)S(1)} %get-tuple-element.42), channel_id=1, source_target_pairs={{0,224},{2,226},{4,228},{6,230},{8,232},{10,234},{12,236},{14,238}... | collective-permute-start | bytes 430088 | tf_op jit(solution)/shard_map/ppermute | solution.py:50
  76.1 8.9 %collective-permute-start.21 = (bf16[40,1792]{1,0:T(8,128)(2,1)S(1)}, bf16[40,1792]{1,0:T(8,128)(2,1)S(1)}, u32[]{:S(2)}, u32[]{:S(2)}) collective-permute-start(bf16[40,1792]{1,0:T(8,128)(2,1)S(1)} %get-tuple-element.43), channel_id=1, source_target_pairs={{0,40},{2,42},{4,44},{6,46},{8,48},{10,50},{12,52},{14,54},{16,56}... | collective-permute-start | bytes 430088 | tf_op jit(solution)/shard_map/ppermute | solution.py:50
  79.1 6.2 %collective-permute-start.22 = (bf16[40,1792]{1,0:T(8,128)(2,1)S(1)}, bf16[40,1792]{1,0:T(8,128)(2,1)S(1)}, u32[]{:S(2)}, u32[]{:S(2)}) collective-permute-start(bf16[40,1792]{1,0:T(8,128)(2,1)S(1)} %get-tuple-element.44), channel_id=1, source_target_pairs={{0,248},{2,250},{4,252},{6,254},{8,224},{10,226},{12,228},{14,230}... | collective-permute-start | bytes 430088 | tf_op jit(solution)/shard_map/ppermute | solution.py:50
  81.5 7.5 %collective-permute-start.23 = (bf16[40,1792]{1,0:T(8,128)(2,1)S(1)}, bf16[40,1792]{1,0:T(8,128)(2,1)S(1)}, u32[]{:S(2)}, u32[]{:S(2)}) collective-permute-start(bf16[40,1792]{1,0:T(8,128)(2,1)S(1)} %get-tuple-element.45), channel_id=1, source_target_pairs={{0,240},{2,242},{4,244},{6,246},{8,248},{10,250},{12,252},{14,254}... | collective-permute-start | bytes 430088 | tf_op jit(solution)/shard_map/ppermute | solution.py:50
  84.0 5.5 %collective-permute-start.24 = (bf16[40,1792]{1,0:T(8,128)(2,1)S(1)}, bf16[40,1792]{1,0:T(8,128)(2,1)S(1)}, u32[]{:S(2)}, u32[]{:S(2)}) collective-permute-start(bf16[40,1792]{1,0:T(8,128)(2,1)S(1)} %get-tuple-element.39.token), channel_id=1, source_target_pairs={{0,32},{2,34},{4,36},{6,38},{8,40},{10,42},{12,44},{14,46},{16,48}... | collective-permute-start | bytes 430088 | tf_op jit(solution)/shard_map/ppermute | solution.py:50

commit v6 on v5

--- a/solution.py
+++ b/solution.py
@@ -27,6 +27,16 @@
     return lax.ppermute(
         v, "expert", [(y * NX + x, y * NX + (x + d) % NX) for y in range(NY) for x in range(NX)]
     )
+
+
+def move_x_cores(v, d):
+    pairs = [
+        ((y * NX + x) * 2 + c, (y * NX + (x + d * (1 - 2 * c)) % NX) * 2 + c)
+        for y in range(NY)
+        for x in range(NX)
+        for c in range(2)
+    ]
+    return lax.ppermute(v, ("expert", "dp"), pairs)
 
 
 def move_y(v, d):
@@ -148,11 +158,29 @@
     out_b[...] = right[half:, :]
 
 
-def up_kernel(r0, r1, r2, r3, token, *refs):
-    *weights, out = refs
+def parts_cores_kernel(core_ref, one, two, out_a, out_b):
+    half = out_a.shape[0]
+    first = core_ref[0] == 0
+
+    @pl.when(first)
+    def _():
+        out_a[...] = one[:half, :]
+        out_b[...] = two[half:, :]
+
+    @pl.when(jnp.logical_not(first))
+    def _():
+        out_a[...] = two[:half, :]
+        out_b[...] = one[half:, :]
+
+
+def up_kernel(core_ref, r0, r1, r2, r3, token, own, one, two, out):
     rows = jnp.concatenate([r[0 : 2 * CAP, :] for r in (r0, r1, r2, r3)], axis=0)
-    for i, w in enumerate(weights):
-        out[:, i * 256 : (i + 1) * 256] = nn(rows, w[...]).astype(BF)
+    n = own.shape[1]
+    first = core_ref[0] == 0
+    a, b = nn(rows, one[...]), nn(rows, two[...])
+    out[:, :n] = nn(rows, own[...]).astype(BF)
+    out[:, n : 2 * n] = jnp.where(first, a, b).astype(BF)
+    out[:, 2 * n :] = jnp.where(first, b, a).astype(BF)
 
 
 def up_halves_kernel(r0, r1, r2, r3, wa, wb, out):
@@ -193,17 +221,24 @@
     return (g * (q * (1.0 + v * (1.0 - q)))).astype(BF)
 
 
-def mid_kernel(r0, r1, r2, r3, pu, qu, pv, qv, u0, u1, u2, v0, v1, v2, acc_f, acc_b):
+def mid_kernel(core_ref, r0, r1, r2, r3, pu, qu, pv, qv, u0, u1, u2, v0, v1, v2, acc_f, acc_b):
     su = added(pu[...], qu[...])
     act = activate(su)
     hid = grad_hidden(su, added(pv[...], qv[...]))
+    first = core_ref[0] == 0
+    left, right = hid[:, 256:512].astype(F32), hid[:, 512:].astype(F32)
+    hids = (
+        hid[:, :256],
+        jnp.where(first, left, right).astype(BF),
+        jnp.where(first, right, left).astype(BF),
+    )
     for c in columns(acc_f.shape[1]):
         rows = [r[:, c].astype(F32) for r in (r0, r1, r2, r3)]
         f = jnp.concatenate([r[:CAP] for r in rows], axis=0)
         b = jnp.concatenate([r[2 * CAP : 3 * CAP] for r in rows], axis=0)
         for i, (u, v) in enumerate(((u0, v0), (u1, v1), (u2, v2))):
             f += nn(act[:, i * 256 : (i + 1) * 256], v[:, c])
-            b += nt(hid[:, i * 256 : (i + 1) * 256], u[c, :])
+            b += nt(hids[i], u[c, :])
         acc_f[:, c] = f
         acc_b[:, c] = b
 
@@ -270,6 +305,7 @@
     ids_up = routes_up.reshape(1, n)
     ids_down = routes_down.reshape(1, n)
     y = (lax.axis_index("expert") // NX).reshape(1)
+    core = lax.axis_index("dp").reshape(1)
     mm = 2 * 320 * width * hp
 
     def parts(left, right, cost):
@@ -278,9 +314,19 @@
             parts_kernel, [half] * 2, cost, 4 * half.shape[0] * half.shape[1], [VM] * 2, left, right
         )
 
-    u_l, u_r = move_x(u_own, 1), move_x(u_own, -1)
+    u_1, u_2 = move_x_cores(u_own, 1), move_x_cores(u_own, -1)
     v_l, v_r = move_x(v_own, 1), move_x(v_own, -1)
-    to_r, to_l = parts(u_l, u_r, CU)
+    half_u = sds((width // 2, hp))
+    to_r, to_l = call(
+        parts_cores_kernel,
+        [half_u] * 2,
+        CU,
+        4 * width * hp,
+        [SM, VM, VM],
+        core,
+        u_1,
+        u_2,
+    )
     to_u = to_r
     u_a, u_b = move_x(to_r, 1), move_x(to_l, -1)
     to_r, to_l = parts(v_l, v_r, 0)
@@ -330,12 +376,13 @@
         sds((2 * CAP * NY, 3 * hp)),
         3 * mm,
         4 << 20,
-        [VM] * 4 + [ANY] + [VM] * 3,
+        [SM] + [VM] * 4 + [ANY] + [VM] * 3,
+        core,
         *rows,
         to_v,
         u_own,
-        u_l,
-        u_r,
+        u_1,
+        u_2,
     )
     qu = swap(pu)
     pv = call(
@@ -356,15 +403,16 @@
         [sds((NY * CAP, width), F32)] * 2,
         3 * mm,
         8 << 20,
-        [VM] * 14,
+        [SM] + [VM] * 14,
+        core,
         *rows,
         pu,
         qu,
         pv,
         qv,
         u_own,
-        u_l,
-        u_r,
+        u_1,
+        u_2,
         v_own,
         v_l,
         v_r,

time: 92.3 us -> 92.7 us (level)
  the two profiles are of different devices: /device:TPU:1 before, /device:TPU:8 now
where the time goes in v6:
time: 92.7 us; the launch traced here: 92.4 us
  starting transfers between devices  46.6 us (50%)
  waiting for transfers between devices  24.8 us (27%)
  Pallas kernels  15.2 us (16%)
  local copies, waits for them, and re-layouts  4.84 us (5%)
  between operations  1.01 us (1%)
    ppermute x8, starting transfers between devices, move_zy(): return lax.ppermute(v, ('section', 'expert'), pairs)  18.6 us
    pallas_call x20, Pallas kernels, call(): pl.pallas_call(kernel, out_shape=outs, scratch_shapes=scratch, in_specs=i...  15.2 us
    ppermute x6, starting transfers between devices, move_x(): lax.ppermute(v, 'expert', [(y * NX + x, y * NX + (x + d) % NX) for y in r...  10.6 us
    ppermute x6, waiting for transfers between devices, move_x(): lax.ppermute(v, 'expert', [(y * NX + x, y * NX + (x + d) % NX) for y in r...  9.62 us
    ppermute x3, waiting for transfers between devices, move_y(): lax.ppermute(v, 'expert', [(y * NX + x, (y + d) % NY * NX + x) for y in r...  7.79 us
    ppermute x3, starting transfers between devices, move_y(): lax.ppermute(v, 'expert', [(y * NX + x, (y + d) % NY * NX + x) for y in r...  6.24 us
    ppermute x2, starting transfers between devices, move_z(): return lax.ppermute(v, 'section', [(z, (z + d) % NZ) for z in range(NZ)])  5.86 us
    ppermute x8, waiting for transfers between devices, move_zy(): return lax.ppermute(v, ('section', 'expert'), pairs)  5.08 us
  transfers between devices with their start and end apart: 25, of which 10 were waited for; matrix products, arithmetic and copies ran while one was open for 0% of the time, Pallas kernels for 15%

profile of v6, /device:TPU:8, one launch (start us, length us, event | category | flops | bytes accessed | tf_op | source)
XLA Modules:
  0.0 92.4 jit_solution(8127209749443295414)
XLA Ops:
  0.6 1.6 %collective-permute-start.4 = (bf16[1792,256]{1,0:T(8,128)(2,1)}, bf16[1792,256]{1,0:T(8,128)(2,1)S(1)}, u32[]{:S(2)}, u32[]{:S(2)}) collective-permute-start(bf16[1792,256]{1,0:T(8,128)(2,1)} %bitcast.11), channel_id=1, source_target_pairs={{0,2},{1,7},{2,4},{3,1},{4,6},{5,3},{6,0},{7,5},{8,10},{9,15},{10,... | collective-permute-start | bytes 2752520 | tf_op jit(solution)/shard_map/ppermute | solution.py:39
  2.2 1.7 %collective-permute-start.5 = (bf16[1792,256]{1,0:T(8,128)(2,1)}, bf16[1792,256]{1,0:T(8,128)(2,1)}, u32[]{:S(2)}, u32[]{:S(2)}) collective-permute-start(bf16[1792,256]{1,0:T(8,128)(2,1)} %bitcast.12), channel_id=1, source_target_pairs={{0,6},{1,3},{2,0},{3,5},{4,2},{5,7},{6,4},{7,1},{8,14},{9,11},{10,... | collective-permute-start | bytes 2752520 | tf_op jit(solution)/shard_map/ppermute | solution.py:39
  4.0 1.0 %copy-done.2 = bf16[1,128,1792]{2,1,0:T(8,128)(2,1)S(1)} copy-done((bf16[1,128,1792]{2,1,0:T(8,128)(2,1)S(1)}, bf16[1,128,1792]{2,1,0:T(8,128)(2,1)}, u32[]{:S(2)}) %copy-start.2) | copy-done | bytes 458776
  5.0 1.0 %copy-done.3 = bf16[1,1,128,1792]{3,2,1,0:T(8,128)(2,1)S(1)} copy-done((bf16[1,1,128,1792]{3,2,1,0:T(8,128)(2,1)S(1)}, bf16[1,1,128,1792]{3,2,1,0:T(8,128)(2,1)}, u32[]{:S(2)}) %copy-start.3) | copy-done | bytes 458776
  6.0 1.0 %copy-done.4 = bf16[1,128,1792]{2,1,0:T(8,128)(2,1)S(1)} copy-done((bf16[1,128,1792]{2,1,0:T(8,128)(2,1)S(1)}, bf16[1,128,1792]{2,1,0:T(8,128)(2,1)}, u32[]{:S(2)}) %copy-start.4) | copy-done | bytes 458776
  7.0 2.4 %shard_map.87 = (bf16[128,1792]{1,0:T(8,128)(2,1)S(1)}, bf16[128,1792]{1,0:T(8,128)(2,1)S(1)}, bf16[128,1792]{1,0:T(8,128)(2,1)}, bf16[128,1792]{1,0:T(8,128)(2,1)S(1)}) custom-call(s32[1]{0:T(128)} %bitcast.y_ref, s32[1,128]{1,0:T(1,128)} %bitcast.1.refs_0_, s32[1,128]{1,0:T(1,128)} %bitcast.2.refs_1_, bf16[128,1792]{1,0:T(8,128)(2,1)S(1)} %bitcast.19, ...), custom_call_target="tpu_custom_call" | custom-call | flops 220200960 | bytes 3211264 | tf_op jit(solution)/shard_map/pallas_call | solution.py:68
  9.4 0.0 copy-start.5
  9.4 0.8 copy-done.5
  10.2 2.3 %collective-permute-start.2 = (bf16[128,1792]{1,0:T(8,128)(2,1)}, bf16[128,1792]{1,0:T(8,128)(2,1)S(1)}, u32[]{:S(2)}, u32[]{:S(2)}) collective-permute-start(bf16[128,1792]{1,0:T(8,128)(2,1)} %get-tuple-element.29), channel_id=1, source_target_pairs={{0,16},{2,18},{4,20},{6,22},{8,24},{10,26},{12,28},{14,30},{16,0},... | collective-permute-start | bytes 1376264 | tf_op jit(solution)/shard_map/ppermute | solution.py:43
  12.5 1.9 %collective-permute-start = (s32[1,128]{1,0:T(1,128)}, s32[1,128]{1,0:T(1,128)S(1)}, u32[]{:S(2)}, u32[]{:S(2)}) collective-permute-start(s32[1,128]{1,0:T(1,128)} %bitcast.1.refs_0_), channel_id=1, source_target_pairs={{0,32},{32,64},{64,96},{96,128},{128,160},{160,192},{192,224},{224... | collective-permute-start | bytes 1544 | tf_op jit(solution)/shard_map/ppermute | solution.py:49
  14.4 3.9 %collective-permute-start.1 = (s32[1,128]{1,0:T(1,128)}, s32[1,128]{1,0:T(1,128)S(1)}, u32[]{:S(2)}, u32[]{:S(2)}) collective-permute-start(s32[1,128]{1,0:T(1,128)} %bitcast.2.refs_1_), channel_id=1, source_target_pairs={{0,224},{32,0},{64,32},{96,64},{128,96},{160,128},{192,160},{224,1... | collective-permute-start | bytes 1544 | tf_op jit(solution)/shard_map/ppermute | solution.py:49
  18.3 1.6 %collective-permute-done.ids_f = s32[1,128]{1,0:T(1,128)S(1)} collective-permute-done((s32[1,128]{1,0:T(1,128)}, s32[1,128]{1,0:T(1,128)S(1)}, u32[]{:S(2)}, u32[]{:S(2)}) %collective-permute-start) | collective-permute-done | bytes 544 | tf_op jit(solution)/shard_map/ppermute | solution.py:49
  20.0 0.3 collective-permute-start.10
  20.2 0.0 collective-permute-done.1.ids_b
  20.2 3.0 %collective-permute-start.11 = (bf16[256,1792]{1,0:T(8,128)(2,1)S(1)}, bf16[256,1792]{1,0:T(8,128)(2,1)S(1)}, u32[]{:S(2)}, u32[]{:S(2)}) collective-permute-start(bf16[256,1792]{1,0:T(8,128)(2,1)S(1)} %bitcast.16), channel_id=1, source_target_pairs={{0,6},{2,0},{4,2},{6,4},{8,14},{10,8},{12,10},{14,12},{16,22},{18,... | collective-permute-start | bytes 2752520 | tf_op jit(solution)/shard_map/ppermute | solution.py:27
  23.2 0.5 shard_map.86
  23.7 0.0 collective-permute-done.2.refs_0_.r2
  23.7 0.0 copy-start.6
  23.7 1.0 %copy-done.6 = bf16[128,1792]{1,0:T(8,128)(2,1)S(1)} copy-done((bf16[128,1792]{1,0:T(8,128)(2,1)S(1)}, bf16[128,1792]{1,0:T(8,128)(2,1)}, u32[]{:S(2)}) %copy-start.6) | copy-done | bytes 458776
  24.7 0.3 shard_map.88
  25.0 1.3 %collective-permute-start.3 = (bf16[128,1792]{1,0:T(8,128)(2,1)S(1)}, bf16[128,1792]{1,0:T(8,128)(2,1)S(1)}, u32[]{:S(2)}, u32[]{:S(2)}) collective-permute-start(bf16[128,1792]{1,0:T(8,128)(2,1)S(1)} %shard_map.88), channel_id=1, source_target_pairs={{0,8},{2,10},{4,12},{6,14},{8,16},{10,18},{12,20},{14,22},{16,24},... | collective-permute-start | bytes 1376264 | tf_op jit(solution)/shard_map/ppermute | solution.py:43
  26.3 1.2 %shard_map.89 = (bf16[896,256]{1,0:T(8,128)(2,1)S(1)}, bf16[896,256]{1,0:T(8,128)(2,1)S(1)}) custom-call(s32[1]{0:T(128)} %bitcast.6.core_ref, bf16[1792,256]{1,0:T(8,128)(2,1)S(1)} %collective-permute-done.4.one.u1, bf16[1792,256]{1,0:T(8,128)(2,1)} %collective-permute-done.5.two.u2), custom_call_target="tpu_custom_call" | custom-call | flops 8000000000 | bytes 1835008 | tf_op jit(solution)/shard_map/pallas_call | solution.py:68
  27.6 7.8 %collective-permute-done.3.refs_0_.r1 = bf16[128,1792]{1,0:T(8,128)(2,1)S(1)} collective-permute-done((bf16[128,1792]{1,0:T(8,128)(2,1)S(1)}, bf16[128,1792]{1,0:T(8,128)(2,1)S(1)}, u32[]{:S(2)}, u32[]{:S(2)}) %collective-permute-start.3) | collective-permute-done | bytes 458784 | tf_op jit(solution)/shard_map/ppermute | solution.py:43
  35.4 0.3 shard_map.90
  35.7 0.0 copy-start
  35.7 2.6 %collective-permute-start.6 = (bf16[128,1792]{1,0:T(8,128)(2,1)S(1)}, bf16[128,1792]{1,0:T(8,128)(2,1)S(1)}, u32[]{:S(2)}, u32[]{:S(2)}) collective-permute-start(bf16[128,1792]{1,0:T(8,128)(2,1)S(1)} %shard_map.90), channel_id=1, source_target_pairs={{0,24},{2,26},{4,28},{6,30},{8,0},{10,2},{12,4},{14,6},{16,8},{18,... | collective-permute-start | bytes 1376264 | tf_op jit(solution)/shard_map/ppermute | solution.py:43
  38.3 3.6 %collective-permute-start.8 = (bf16[896,256]{1,0:T(8,128)(2,1)S(1)}, bf16[896,256]{1,0:T(8,128)(2,1)S(1)}, u32[]{:S(2)}, u32[]{:S(2)}) collective-permute-start(bf16[896,256]{1,0:T(8,128)(2,1)S(1)} %get-tuple-element.32), channel_id=1, source_target_pairs={{0,6},{2,0},{4,2},{6,4},{8,14},{10,8},{12,10},{14,12},{16,22},{18,... | collective-permute-start | bytes 1376264 | tf_op jit(solution)/shard_map/ppermute | solution.py:27
  41.9 2.6 %collective-permute-done.10.left.refs_1_.v1 = bf16[256,1792]{1,0:T(8,128)(2,1)S(1)} collective-permute-done((bf16[256,1792]{1,0:T(8,128)(2,1)S(1)}, bf16[256,1792]{1,0:T(8,128)(2,1)S(1)}, u32[]{:S(2)}, u32[]{:S(2)}) %collective-permute-start.10) | collective-permute-done | bytes 917536 | tf_op jit(solution)/shard_map/ppermute | solution.py:27
  44.5 0.3 collective-permute-done.11.right.refs_2_.v2
  44.8 0.1 shard_map.92
  44.8 0.7 collective-permute-start.12
  45.5 3.1 %collective-permute-start.13 = (bf16[128,1792]{1,0:T(8,128)(2,1)S(1)}, bf16[128,1792]{1,0:T(8,128)(2,1)S(1)}, u32[]{:S(2)}, u32[]{:S(2)}) collective-permute-start(bf16[128,1792]{1,0:T(8,128)(2,1)S(1)} %get-tuple-element.34), channel_id=1, source_target_pairs={{0,6},{2,0},{4,2},{6,4},{8,14},{10,8},{12,10},{14,12},{16,22},{18,... | collective-permute-start | bytes 1376264 | tf_op jit(solution)/shard_map/ppermute | solution.py:27
  48.6 2.2 %shard_map.93.token.pu = bf16[320,768]{1,0:T(8,128)(2,1)S(1)} custom-call(s32[1]{0:T(128)} %bitcast.6.core_ref, bf16[128,1792]{1,0:T(8,128)(2,1)S(1)} %get-tuple-element.27.r0, bf16[128,1792]{1,0:T(8,128)(2,1)S(1)} %collective-permute-done.3.refs_0_.r1, bf16[128,1792]{1,0:T(8,128)(2,1)S(1)} %collective-permute-done.2.refs_0_.r2, ...), custom_call_target="tpu_custom_call" | custom-call | flops 880803840 | bytes 4194304 | tf_op jit(solution)/shard_map/pallas_call | solution.py:68
  50.8 0.3 collective-permute-start.14
  51.1 1.1 %shard_map.94.pv = bf16[192,768]{1,0:T(8,128)(2,1)S(1)} custom-call(bf16[128,1792]{1,0:T(8,128)(2,1)S(1)} %get-tuple-element.27.r0, bf16[128,1792]{1,0:T(8,128)(2,1)S(1)} %collective-permute-done.3.refs_0_.r1, bf16[128,1792]{1,0:T(8,128)(2,1)S(1)} %collective-permute-done.2.refs_0_.r2, bf16[128,1792]{1,0:T(8,128)(2,1)S(1)} %collective-permute-done.6.r3, ...), custom_call_target="tpu_custom_call" | custom-call | flops 587202560 | bytes 4194304 | tf_op jit(solution)/shard_map/pallas_call | solution.py:68
  52.2 2.1 %collective-permute-done.7.wa.ua = bf16[896,256]{1,0:T(8,128)(2,1)S(1)} collective-permute-done((bf16[896,256]{1,0:T(8,128)(2,1)S(1)}, bf16[896,256]{1,0:T(8,128)(2,1)S(1)}, u32[]{:S(2)}, u32[]{:S(2)}) %collective-permute-start.7) | collective-permute-done | bytes 458784 | tf_op jit(solution)/shard_map/ppermute | solution.py:27
  54.3 1.2 %collective-permute-start.15 = (bf16[192,768]{1,0:T(8,128)(2,1)S(1)}, bf16[192,768]{1,0:T(8,128)(2,1)S(1)}, u32[]{:S(2)}, u32[]{:S(2)}) collective-permute-start(bf16[192,768]{1,0:T(8,128)(2,1)S(1)} %shard_map.94.pv), channel_id=1, source_target_pairs={{0,1},{1,0},{2,3},{3,2},{4,5},{5,4},{6,7},{7,6},{8,9},{9,8},{10,11... | collective-permute-start | bytes 884744 | tf_op jit(solution)/shard_map/ppermute | solution.py:64
  55.5 0.5 shard_map.91.pu
  56.0 0.1 collective-permute-start.9
  56.1 0.6 collective-permute-done.15.qv
  56.7 2.8 %shard_map.95 = (f32[160,1792]{1,0:T(8,128)S(1)}, f32[160,1792]{1,0:T(8,128)S(1)}) custom-call(s32[1]{0:T(128)} %bitcast.6.core_ref, bf16[128,1792]{1,0:T(8,128)(2,1)S(1)} %get-tuple-element.27.r0, bf16[128,1792]{1,0:T(8,128)(2,1)S(1)} %collective-permute-done.3.refs_0_.r1, bf16[128,1792]{1,0:T(8,128)(2,1)S(1)} %collective-permute-done.2.refs_0_.r2, ...), custom_call_target="tpu_custom_call" | custom-call | flops 880803840 | bytes 8388608 | tf_op jit(solution)/shard_map/pallas_call | solution.py:68
  59.5 4.6 %collective-permute-done.12.va = bf16[128,1792]{1,0:T(8,128)(2,1)S(1)} collective-permute-done((bf16[128,1792]{1,0:T(8,128)(2,1)S(1)}, bf16[128,1792]{1,0:T(8,128)(2,1)S(1)}, u32[]{:S(2)}, u32[]{:S(2)}) %collective-permute-start.12) | collective-permute-done | bytes 458784 | tf_op jit(solution)/shard_map/ppermute | solution.py:27
  64.1 0.6 shard_map.96
  64.8 0.5 collective-permute-start.17
  65.2 3.6 %collective-permute-start.16 = (bf16[40,1792]{1,0:T(8,128)(2,1)S(1)}, bf16[40,1792]{1,0:T(8,128)(2,1)S(1)}, u32[]{:S(2)}, u32[]{:S(2)}) collective-permute-start(bf16[40,1792]{1,0:T(8,128)(2,1)S(1)} %get-tuple-element.37), channel_id=1, source_target_pairs={{0,48},{2,50},{4,52},{6,54},{8,56},{10,58},{12,60},{14,62},{16,32}... | collective-permute-start | bytes 430088 | tf_op jit(solution)/shard_map/ppermute | solution.py:60
  68.9 2.7 %collective-permute-start.19 = (bf16[40,1792]{1,0:T(8,128)(2,1)S(1)}, bf16[40,1792]{1,0:T(8,128)(2,1)S(1)}, u32[]{:S(2)}, u32[]{:S(2)}) collective-permute-start(bf16[40,1792]{1,0:T(8,128)(2,1)S(1)} %get-tuple-element.41), channel_id=1, source_target_pairs={{0,56},{2,58},{4,60},{6,62},{8,32},{10,34},{12,36},{14,38},{16,40}... | collective-permute-start | bytes 430088 | tf_op jit(solution)/shard_map/ppermute | solution.py:60
  71.6 0.5 shard_map.98
  72.1 1.6 %collective-permute-start.18 = (bf16[40,1792]{1,0:T(8,128)(2,1)S(1)}, bf16[40,1792]{1,0:T(8,128)(2,1)S(1)}, u32[]{:S(2)}, u32[]{:S(2)}) collective-permute-start(bf16[40,1792]{1,0:T(8,128)(2,1)S(1)} %get-tuple-element.40), channel_id=1, source_target_pairs={{0,232},{2,234},{4,236},{6,238},{8,240},{10,242},{12,244},{14,246}... | collective-permute-start | bytes 430088 | tf_op jit(solution)/shard_map/ppermute | solution.py:60
  73.6 1.0 %collective-permute-start.20 = (bf16[40,1792]{1,0:T(8,128)(2,1)S(1)}, bf16[40,1792]{1,0:T(8,128)(2,1)S(1)}, u32[]{:S(2)}, u32[]{:S(2)}) collective-permute-start(bf16[40,1792]{1,0:T(8,128)(2,1)S(1)} %get-tuple-element.42), channel_id=1, source_target_pairs={{0,224},{2,226},{4,228},{6,230},{8,232},{10,234},{12,236},{14,238}... | collective-permute-start | bytes 430088 | tf_op jit(solution)/shard_map/ppermute | solution.py:60
  74.6 1.7 %collective-permute-start.21 = (bf16[40,1792]{1,0:T(8,128)(2,1)S(1)}, bf16[40,1792]{1,0:T(8,128)(2,1)S(1)}, u32[]{:S(2)}, u32[]{:S(2)}) collective-permute-start(bf16[40,1792]{1,0:T(8,128)(2,1)S(1)} %get-tuple-element.43), channel_id=1, source_target_pairs={{0,40},{2,42},{4,44},{6,46},{8,48},{10,50},{12,52},{14,54},{16,56}... | collective-permute-start | bytes 430088 | tf_op jit(solution)/shard_map/ppermute | solution.py:60
  76.3 1.7 %collective-permute-done.16.refs_0_ = bf16[40,1792]{1,0:T(8,128)(2,1)S(1)} collective-permute-done((bf16[40,1792]{1,0:T(8,128)(2,1)S(1)}, bf16[40,1792]{1,0:T(8,128)(2,1)S(1)}, u32[]{:S(2)}, u32[]{:S(2)}) %collective-permute-start.16) | collective-permute-done | bytes 143392 | tf_op jit(solution)/shard_map/ppermute | solution.py:60
  78.1 2.2 %collective-permute-start.22 = (bf16[40,1792]{1,0:T(8,128)(2,1)S(1)}, bf16[40,1792]{1,0:T(8,128)(2,1)S(1)}, u32[]{:S(2)}, u32[]{:S(2)}) collective-permute-start(bf16[40,1792]{1,0:T(8,128)(2,1)S(1)} %get-tuple-element.44), channel_id=1, source_target_pairs={{0,248},{2,250},{4,252},{6,254},{8,224},{10,226},{12,228},{14,230}... | collective-permute-start | bytes 430088 | tf_op jit(solution)/shard_map/ppermute | solution.py:60
  80.3 4.5 %collective-permute-start.23 = (bf16[40,1792]{1,0:T(8,128)(2,1)S(1)}, bf16[40,1792]{1,0:T(8,128)(2,1)S(1)}, u32[]{:S(2)}, u32[]{:S(2)}) collective-permute-start(bf16[40,1792]{1,0:T(8,128)(2,1)S(1)} %get-tuple-element.45), channel_id=1, source_target_pairs={{0,240},{2,242},{4,244},{6,246},{8,248},{10,250},{12,252},{14,254}... | collective-permute-start | bytes 430088 | tf_op jit(solution)/shard_map/ppermute | solution.py:60
  84.9 1.1 %collective-permute-start.24 = (bf16[40,1792]{1,0:T(8,128)(2,1)S(1)}, bf16[40,1792]{1,0:T(8,128)(2,1)S(1)}, u32[]{:S(2)}, u32[]{:S(2)}) collective-permute-start(bf16[40,1792]{1,0:T(8,128)(2,1)S(1)} %get-tuple-element.39.token), channel_id=1, source_target_pairs={{0,32},{2,34},{4,36},{6,38},{8,40},{10,42},{12,44},{14,46},{16,48}... | collective-permute-start | bytes 430088 | tf_op jit(solution)/shard_map/ppermute | solution.py:60
  86.0 0.2 shard_map.97.token.refs_0_
  86.3 0.2 shard_map.99.token.refs_0_
  86.5 0.2 shard_map.100.token.refs_0_
  86.8 0.3 shard_map.101.token.refs_0_
  87.0 0.2 shard_map.102.token.total_f
  87.3 0.3 shard_map.103.token.refs_0_
  87.6 1.6 %collective-permute-done.23.refs_1_ = bf16[40,1792]{1,0:T(8,128)(2,1)S(1)} collective-permute-done((bf16[40,1792]{1,0:T(8,128)(2,1)S(1)}, bf16[40,1792]{1,0:T(8,128)(2,1)S(1)}, u32[]{:S(2)}, u32[]{:S(2)}) %collective-permute-start.23) | collective-permute-done | bytes 143392 | tf_op jit(solution)/shard_map/ppermute | solution.py:60
  89.2 0.2 shard_map.104.total_b
  89.4 1.7 %collective-permute-done.24.row = bf16[40,1792]{1,0:T(8,128)(2,1)S(1)} collective-permute-done((bf16[40,1792]{1,0:T(8,128)(2,1)S(1)}, bf16[40,1792]{1,0:T(8,128)(2,1)S(1)}, u32[]{:S(2)}, u32[]{:S(2)}) %collective-permute-start.24) | collective-permute-done | bytes 143392 | tf_op jit(solution)/shard_map/ppermute | solution.py:60
  91.2 1.0 %shard_map.105 = (bf16[128,1792]{1,0:T(8,128)(2,1)}, bf16[128,1792]{1,0:T(8,128)(2,1)}) custom-call(bf16[4,128,40]{2,1,0:T(8,128)(2,1)S(1)} %get-tuple-element.25.refs_1_.table, f32[128,1792]{1,0:T(8,128)S(1)} %shard_map.102.token.total_f, f32[128,1792]{1,0:T(8,128)S(1)} %shard_map.104.total_b, bf16[40,1792]{1,0:T(8,128)(2,1)S(1)} %collective-permute-done.24.row), custom_call_target="tpu_custom_call" | custom-call | flops 18350080 | bytes 2752512 | tf_op jit(solution)/shard_map/pallas_call | solution.py:68
  (20 shorter events, 0.0 us)
Async XLA Ops:
  0.6 19.3 %copy-start.1 = (bf16[1,1,256,1792]{3,2,1,0:T(8,128)(2,1)S(1)}, bf16[1,1,256,1792]{3,2,1,0:T(8,128)(2,1)}, u32[]{:S(2)}) copy-start(bf16[1,1,256,1792]{3,2,1,0:T(8,128)(2,1)} %param.13) | copy-start | bytes 2752516
  0.6 25.7 %collective-permute-start.4 = (bf16[1792,256]{1,0:T(8,128)(2,1)}, bf16[1792,256]{1,0:T(8,128)(2,1)S(1)}, u32[]{:S(2)}, u32[]{:S(2)}) collective-permute-start(bf16[1792,256]{1,0:T(8,128)(2,1)} %bitcast.11), channel_id=1, source_target_pairs={{0,2},{1,7},{2,4},{3,1},{4,6},{5,3},{6,0},{7,5},{8,10},{9,15},{10,... | collective-permute-start | bytes 2752520 | tf_op jit(solution)/shard_map/ppermute | solution.py:39
  2.2 24.1 %collective-permute-start.5 = (bf16[1792,256]{1,0:T(8,128)(2,1)}, bf16[1792,256]{1,0:T(8,128)(2,1)}, u32[]{:S(2)}, u32[]{:S(2)}) collective-permute-start(bf16[1792,256]{1,0:T(8,128)(2,1)} %bitcast.12), channel_id=1, source_target_pairs={{0,6},{1,3},{2,0},{3,5},{4,2},{5,7},{6,4},{7,1},{8,14},{9,11},{10,... | collective-permute-start | bytes 2752520 | tf_op jit(solution)/shard_map/ppermute | solution.py:39
  4.0 1.0 %copy-start.2 = (bf16[1,128,1792]{2,1,0:T(8,128)(2,1)S(1)}, bf16[1,128,1792]{2,1,0:T(8,128)(2,1)}, u32[]{:S(2)}) copy-start(bf16[1,128,1792]{2,1,0:T(8,128)(2,1)} %param.7) | copy-start | bytes 1376260
  5.0 1.0 %copy-start.3 = (bf16[1,1,128,1792]{3,2,1,0:T(8,128)(2,1)S(1)}, bf16[1,1,128,1792]{3,2,1,0:T(8,128)(2,1)}, u32[]{:S(2)}) copy-start(bf16[1,1,128,1792]{3,2,1,0:T(8,128)(2,1)} %param.10) | copy-start | bytes 1376260
  6.0 1.0 %copy-start.4 = (bf16[1,128,1792]{2,1,0:T(8,128)(2,1)S(1)}, bf16[1,128,1792]{2,1,0:T(8,128)(2,1)}, u32[]{:S(2)}) copy-start(bf16[1,128,1792]{2,1,0:T(8,128)(2,1)} %param.9) | copy-start | bytes 1376260
  9.4 0.8 copy-start.5
  10.2 13.5 %collective-permute-start.2 = (bf16[128,1792]{1,0:T(8,128)(2,1)}, bf16[128,1792]{1,0:T(8,128)(2,1)S(1)}, u32[]{:S(2)}, u32[]{:S(2)}) collective-permute-start(bf16[128,1792]{1,0:T(8,128)(2,1)} %get-tuple-element.29), channel_id=1, source_target_pairs={{0,16},{2,18},{4,20},{6,22},{8,24},{10,26},{12,28},{14,30},{16,0},... | collective-permute-start | bytes 1376264 | tf_op jit(solution)/shard_map/ppermute | solution.py:43
  12.5 7.5 %collective-permute-start = (s32[1,128]{1,0:T(1,128)}, s32[1,128]{1,0:T(1,128)S(1)}, u32[]{:S(2)}, u32[]{:S(2)}) collective-permute-start(s32[1,128]{1,0:T(1,128)} %bitcast.1.refs_0_), channel_id=1, source_target_pairs={{0,32},{32,64},{64,96},{96,128},{128,160},{160,192},{192,224},{224... | collective-permute-start | bytes 1544 | tf_op jit(solution)/shard_map/ppermute | solution.py:49
  14.4 5.9 %collective-permute-start.1 = (s32[1,128]{1,0:T(1,128)}, s32[1,128]{1,0:T(1,128)S(1)}, u32[]{:S(2)}, u32[]{:S(2)}) collective-permute-start(s32[1,128]{1,0:T(1,128)} %bitcast.2.refs_1_), channel_id=1, source_target_pairs={{0,224},{32,0},{64,32},{96,64},{128,96},{160,128},{192,160},{224,1... | collective-permute-start | bytes 1544 | tf_op jit(solution)/shard_map/ppermute | solution.py:49
  20.0 24.5 %collective-permute-start.10 = (bf16[256,1792]{1,0:T(8,128)(2,1)S(1)}, bf16[256,1792]{1,0:T(8,128)(2,1)S(1)}, u32[]{:S(2)}, u32[]{:S(2)}) collective-permute-start(bf16[256,1792]{1,0:T(8,128)(2,1)S(1)} %bitcast.15), channel_id=1, source_target_pairs={{0,2},{2,4},{4,6},{6,0},{8,10},{10,12},{12,14},{14,8},{16,18},{18,... | collective-permute-start | bytes 2752520 | tf_op jit(solution)/shard_map/ppermute | solution.py:27
  20.2 24.5 %collective-permute-start.11 = (bf16[256,1792]{1,0:T(8,128)(2,1)S(1)}, bf16[256,1792]{1,0:T(8,128)(2,1)S(1)}, u32[]{:S(2)}, u32[]{:S(2)}) collective-permute-start(bf16[256,1792]{1,0:T(8,128)(2,1)S(1)} %bitcast.16), channel_id=1, source_target_pairs={{0,6},{2,0},{4,2},{6,4},{8,14},{10,8},{12,10},{14,12},{16,22},{18,... | collective-permute-start | bytes 2752520 | tf_op jit(solution)/shard_map/ppermute | solution.py:27
  23.7 1.0 %copy-start.6 = (bf16[128,1792]{1,0:T(8,128)(2,1)S(1)}, bf16[128,1792]{1,0:T(8,128)(2,1)}, u32[]{:S(2)}) copy-start(bf16[128,1792]{1,0:T(8,128)(2,1)} %copy-done.5) | copy-start | bytes 1376260
  25.0 10.4 %collective-permute-start.3 = (bf16[128,1792]{1,0:T(8,128)(2,1)S(1)}, bf16[128,1792]{1,0:T(8,128)(2,1)S(1)}, u32[]{:S(2)}, u32[]{:S(2)}) collective-permute-start(bf16[128,1792]{1,0:T(8,128)(2,1)S(1)} %shard_map.88), channel_id=1, source_target_pairs={{0,8},{2,10},{4,12},{6,14},{8,16},{10,18},{12,20},{14,22},{16,24},... | collective-permute-start | bytes 1376264 | tf_op jit(solution)/shard_map/ppermute | solution.py:43
  35.7 12.9 %copy-start = (bf16[1,1,1792,256]{3,2,1,0:T(8,128)(2,1)S(1)}, bf16[1,1,1792,256]{3,2,1,0:T(8,128)(2,1)}, u32[]{:S(2)}) copy-start(bf16[1,1,1792,256]{3,2,1,0:T(8,128)(2,1)} %param.12) | copy-start | bytes 2752516
  35.7 12.9 %collective-permute-start.6 = (bf16[128,1792]{1,0:T(8,128)(2,1)S(1)}, bf16[128,1792]{1,0:T(8,128)(2,1)S(1)}, u32[]{:S(2)}, u32[]{:S(2)}) collective-permute-start(bf16[128,1792]{1,0:T(8,128)(2,1)S(1)} %shard_map.90), channel_id=1, source_target_pairs={{0,24},{2,26},{4,28},{6,30},{8,0},{10,2},{12,4},{14,6},{16,8},{18,... | collective-permute-start | bytes 1376264 | tf_op jit(solution)/shard_map/ppermute | solution.py:43
  38.3 16.0 %collective-permute-start.7 = (bf16[896,256]{1,0:T(8,128)(2,1)S(1)}, bf16[896,256]{1,0:T(8,128)(2,1)S(1)}, u32[]{:S(2)}, u32[]{:S(2)}) collective-permute-start(bf16[896,256]{1,0:T(8,128)(2,1)S(1)} %get-tuple-element.31.refs_1_), channel_id=1, source_target_pairs={{0,2},{2,4},{4,6},{6,0},{8,10},{10,12},{12,14},{14,8},{16,18},{18,... | collective-permute-start | bytes 1376264 | tf_op jit(solution)/shard_map/ppermute | solution.py:27
  38.3 17.2 %collective-permute-start.8 = (bf16[896,256]{1,0:T(8,128)(2,1)S(1)}, bf16[896,256]{1,0:T(8,128)(2,1)S(1)}, u32[]{:S(2)}, u32[]{:S(2)}) collective-permute-start(bf16[896,256]{1,0:T(8,128)(2,1)S(1)} %get-tuple-element.32), channel_id=1, source_target_pairs={{0,6},{2,0},{4,2},{6,4},{8,14},{10,8},{12,10},{14,12},{16,22},{18,... | collective-permute-start | bytes 1376264 | tf_op jit(solution)/shard_map/ppermute | solution.py:27
  44.8 19.3 %collective-permute-start.12 = (bf16[128,1792]{1,0:T(8,128)(2,1)S(1)}, bf16[128,1792]{1,0:T(8,128)(2,1)S(1)}, u32[]{:S(2)}, u32[]{:S(2)}) collective-permute-start(bf16[128,1792]{1,0:T(8,128)(2,1)S(1)} %get-tuple-element.33.token), channel_id=1, source_target_pairs={{0,2},{2,4},{4,6},{6,0},{8,10},{10,12},{12,14},{14,8},{16,18},{18,... | collective-permute-start | bytes 1376264 | tf_op jit(solution)/shard_map/ppermute | solution.py:27
  45.5 18.6 %collective-permute-start.13 = (bf16[128,1792]{1,0:T(8,128)(2,1)S(1)}, bf16[128,1792]{1,0:T(8,128)(2,1)S(1)}, u32[]{:S(2)}, u32[]{:S(2)}) collective-permute-start(bf16[128,1792]{1,0:T(8,128)(2,1)S(1)} %get-tuple-element.34), channel_id=1, source_target_pairs={{0,6},{2,0},{4,2},{6,4},{8,14},{10,8},{12,10},{14,12},{16,22},{18,... | collective-permute-start | bytes 1376264 | tf_op jit(solution)/shard_map/ppermute | solution.py:27
  50.8 5.9 %collective-permute-start.14 = (bf16[320,768]{1,0:T(8,128)(2,1)S(1)}, bf16[320,768]{1,0:T(8,128)(2,1)S(1)}, u32[]{:S(2)}, u32[]{:S(2)}) collective-permute-start(bf16[320,768]{1,0:T(8,128)(2,1)S(1)} %shard_map.93.token.pu), channel_id=1, source_target_pairs={{0,1},{1,0},{2,3},{3,2},{4,5},{5,4},{6,7},{7,6},{8,9},{9,8},{10,11... | collective-permute-start | bytes 1474568 | tf_op jit(solution)/shard_map/ppermute | solution.py:64
  54.3 2.4 %collective-permute-start.15 = (bf16[192,768]{1,0:T(8,128)(2,1)S(1)}, bf16[192,768]{1,0:T(8,128)(2,1)S(1)}, u32[]{:S(2)}, u32[]{:S(2)}) collective-permute-start(bf16[192,768]{1,0:T(8,128)(2,1)S(1)} %shard_map.94.pv), channel_id=1, source_target_pairs={{0,1},{1,0},{2,3},{3,2},{4,5},{5,4},{6,7},{7,6},{8,9},{9,8},{10,11... | collective-permute-start | bytes 884744 | tf_op jit(solution)/shard_map/ppermute | solution.py:64
  56.0 8.1 %collective-permute-start.9 = (bf16[320,256]{1,0:T(8,128)(2,1)S(1)}, bf16[320,256]{1,0:T(8,128)(2,1)S(1)}, u32[]{:S(2)}, u32[]{:S(2)}) collective-permute-start(bf16[320,256]{1,0:T(8,128)(2,1)S(1)} %shard_map.91.pu), channel_id=1, source_target_pairs={{0,1},{1,0},{2,3},{3,2},{4,5},{5,4},{6,7},{7,6},{8,9},{9,8},{10,11... | collective-permute-start | bytes 491528 | tf_op jit(solution)/shard_map/ppermute | solution.py:64
  64.8 6.8 %collective-permute-start.17 = (bf16[192,256]{1,0:T(8,128)(2,1)S(1)}, bf16[192,256]{1,0:T(8,128)(2,1)S(1)}, u32[]{:S(2)}, u32[]{:S(2)}) collective-permute-start(bf16[192,256]{1,0:T(8,128)(2,1)S(1)} %get-tuple-element.38.pv), channel_id=1, source_target_pairs={{0,1},{1,0},{2,3},{3,2},{4,5},{5,4},{6,7},{7,6},{8,9},{9,8},{10,11... | collective-permute-start | bytes 294920 | tf_op jit(solution)/shard_map/ppermute | solution.py:64
  65.2 12.9 %collective-permute-start.16 = (bf16[40,1792]{1,0:T(8,128)(2,1)S(1)}, bf16[40,1792]{1,0:T(8,128)(2,1)S(1)}, u32[]{:S(2)}, u32[]{:S(2)}) collective-permute-start(bf16[40,1792]{1,0:T(8,128)(2,1)S(1)} %get-tuple-element.37), channel_id=1, source_target_pairs={{0,48},{2,50},{4,52},{6,54},{8,56},{10,58},{12,60},{14,62},{16,32}... | collective-permute-start | bytes 430088 | tf_op jit(solution)/shard_map/ppermute | solution.py:60
  68.9 11.4 %collective-permute-start.19 = (bf16[40,1792]{1,0:T(8,128)(2,1)S(1)}, bf16[40,1792]{1,0:T(8,128)(2,1)S(1)}, u32[]{:S(2)}, u32[]{:S(2)}) collective-permute-start(bf16[40,1792]{1,0:T(8,128)(2,1)S(1)} %get-tuple-element.41), channel_id=1, source_target_pairs={{0,56},{2,58},{4,60},{6,62},{8,32},{10,34},{12,36},{14,38},{16,40}... | collective-permute-start | bytes 430088 | tf_op jit(solution)/shard_map/ppermute | solution.py:60
  72.1 12.8 %collective-permute-start.18 = (bf16[40,1792]{1,0:T(8,128)(2,1)S(1)}, bf16[40,1792]{1,0:T(8,128)(2,1)S(1)}, u32[]{:S(2)}, u32[]{:S(2)}) collective-permute-start(bf16[40,1792]{1,0:T(8,128)(2,1)S(1)} %get-tuple-element.40), channel_id=1, source_target_pairs={{0,232},{2,234},{4,236},{6,238},{8,240},{10,242},{12,244},{14,246}... | collective-permute-start | bytes 430088 | tf_op jit(solution)/shard_map/ppermute | solution.py:60
  73.6 13.2 %collective-permute-start.20 = (bf16[40,1792]{1,0:T(8,128)(2,1)S(1)}, bf16[40,1792]{1,0:T(8,128)(2,1)S(1)}, u32[]{:S(2)}, u32[]{:S(2)}) collective-permute-start(bf16[40,1792]{1,0:T(8,128)(2,1)S(1)} %get-tuple-element.42), channel_id=1, source_target_pairs={{0,224},{2,226},{4,228},{6,230},{8,232},{10,234},{12,236},{14,238}... | collective-permute-start | bytes 430088 | tf_op jit(solution)/shard_map/ppermute | solution.py:60
  74.6 12.4 %collective-permute-start.21 = (bf16[40,1792]{1,0:T(8,128)(2,1)S(1)}, bf16[40,1792]{1,0:T(8,128)(2,1)S(1)}, u32[]{:S(2)}, u32[]{:S(2)}) collective-permute-start(bf16[40,1792]{1,0:T(8,128)(2,1)S(1)} %get-tuple-element.43), channel_id=1, source_target_pairs={{0,40},{2,42},{4,44},{6,46},{8,48},{10,50},{12,52},{14,54},{16,56}... | collective-permute-start | bytes 430088 | tf_op jit(solution)/shard_map/ppermute | solution.py:60
  78.1 9.2 %collective-permute-start.22 = (bf16[40,1792]{1,0:T(8,128)(2,1)S(1)}, bf16[40,1792]{1,0:T(8,128)(2,1)S(1)}, u32[]{:S(2)}, u32[]{:S(2)}) collective-permute-start(bf16[40,1792]{1,0:T(8,128)(2,1)S(1)} %get-tuple-element.44), channel_id=1, source_target_pairs={{0,248},{2,250},{4,252},{6,254},{8,224},{10,226},{12,228},{14,230}... | collective-permute-start | bytes 430088 | tf_op jit(solution)/shard_map/ppermute | solution.py:60
  80.3 8.8 %collective-permute-start.23 = (bf16[40,1792]{1,0:T(8,128)(2,1)S(1)}, bf16[40,1792]{1,0:T(8,128)(2,1)S(1)}, u32[]{:S(2)}, u32[]{:S(2)}) collective-permute-start(bf16[40,1792]{1,0:T(8,128)(2,1)S(1)} %get-tuple-element.45), channel_id=1, source_target_pairs={{0,240},{2,242},{4,244},{6,246},{8,248},{10,250},{12,252},{14,254}... | collective-permute-start | bytes 430088 | tf_op jit(solution)/shard_map/ppermute | solution.py:60
  84.9 6.3 %collective-permute-start.24 = (bf16[40,1792]{1,0:T(8,128)(2,1)S(1)}, bf16[40,1792]{1,0:T(8,128)(2,1)S(1)}, u32[]{:S(2)}, u32[]{:S(2)}) collective-permute-start(bf16[40,1792]{1,0:T(8,128)(2,1)S(1)} %get-tuple-element.39.token), channel_id=1, source_target_pairs={{0,32},{2,34},{4,36},{6,38},{8,40},{10,42},{12,44},{14,46},{16,48}... | collective-permute-start | bytes 430088 | tf_op jit(solution)/shard_map/ppermute | solution.py:60

commit v7 on v5

--- a/solution.py
+++ b/solution.py
@@ -435,14 +435,14 @@
             out_specs=[ANY, ANY],
         )
 
-    sum_f = combine(table_f, got_f, (2,), None, table_b)
-    sum_b = combine(table_b, got_b, (3,), None, sum_f)
-    sum_f = combine(table_f, got_f, (1,), sum_f, sum_b)
+    sum_f = combine(table_f, got_f, (3,), None, table_b)
+    sum_b = combine(table_b, got_b, (1,), None, sum_f)
+    sum_f = combine(table_f, got_f, (0,), sum_f, sum_b)
     sum_b = combine(table_b, got_b, (0,), sum_b, sum_f)
-    sum_f = combine(table_f, got_f, (3,), sum_f, sum_b)
-    sum_b = combine(table_b, got_b, (1,), sum_b, sum_f)
-    sum_b = combine(table_b, got_b, (2,), sum_b, sum_b)
-    out_f, out_b = finish(sum_f, sum_b, 0, 0)
+    sum_f = combine(table_f, got_f, (2,), sum_f, sum_b)
+    sum_f = combine(table_f, got_f, (1,), sum_f, sum_f)
+    sum_b = combine(table_b, got_b, (3,), sum_b, sum_f)
+    out_f, out_b = finish(sum_f, sum_b, 1, 2)
     return (out_f[None], out_b[None])
 
 

time: 92.3 us -> 92.3 us (level); the launches traced: 90.6 us -> 91.8 us
  starting transfers between devices: 48 us -> 49.2 us
    ppermute x8, starting transfers between devices: 14.9 us -> 16.2 us  [move_zy(): return lax.ppermute(v, ('section', 'expert'), pairs)]
  transfers between devices with their start and end apart: 25 -> 25, of which waited for: 8 -> 9; matrix products, arithmetic and copies ran while one was open for 0% -> 0% of each run, Pallas kernels for 10% -> 10%
where the time goes in v7:
time: 92.3 us; the launch traced here: 91.8 us
  starting transfers between devices  49.2 us (53%)
  waiting for transfers between devices  26.6 us (29%)
  Pallas kernels  10.7 us (12%)
  local copies, waits for them, and re-layouts  4.37 us (5%)
  between operations  0.97 us (1%)
    ppermute x8, starting transfers between devices, move_zy(): return lax.ppermute(v, ('section', 'expert'), pairs)  16.2 us
    ppermute x8, starting transfers between devices, move_x(): lax.ppermute(v, 'expert', [(y * NX + x, y * NX + (x + d) % NX) for y in r...  11.6 us
    pallas_call x20, Pallas kernels, call(): pl.pallas_call(kernel, out_shape=outs, scratch_shapes=scratch, in_specs=i...  10.7 us
    ppermute x4, starting transfers between devices, swap(): return lax.ppermute(v, 'dp', [(0, 1), (1, 0)])  10.6 us
    ppermute x3, waiting for transfers between devices, move_y(): lax.ppermute(v, 'expert', [(y * NX + x, (y + d) % NY * NX + x) for y in r...  9.85 us
    ppermute x8, waiting for transfers between devices, move_x(): lax.ppermute(v, 'expert', [(y * NX + x, y * NX + (x + d) % NX) for y in r...  9.08 us
    ppermute x8, waiting for transfers between devices, move_zy(): return lax.ppermute(v, ('section', 'expert'), pairs)  6.42 us
    ppermute x2, starting transfers between devices, move_z(): return lax.ppermute(v, 'section', [(z, (z + d) % NZ) for z in range(NZ)])  5.58 us
  transfers between devices with their start and end apart: 25, of which 9 were waited for; matrix products, arithmetic and copies ran while one was open for 0% of the time, Pallas kernels for 10%

profile of v7, /device:TPU:1, one launch (start us, length us, event | category | flops | bytes accessed | tf_op | source)
XLA Modules:
  0.0 91.8 jit_solution(9027003671781444569)
XLA Ops:
  0.6 2.1 %collective-permute-start.4 = (bf16[1792,256]{1,0:T(8,128)(2,1)}, bf16[1792,256]{1,0:T(8,128)(2,1)S(1)}, u32[]{:S(2)}, u32[]{:S(2)}) collective-permute-start(bf16[1792,256]{1,0:T(8,128)(2,1)} %bitcast.10), channel_id=1, source_target_pairs={{0,2},{2,4},{4,6},{6,0},{8,10},{10,12},{12,14},{14,8},{16,18},{18,... | collective-permute-start | bytes 2752520 | tf_op jit(solution)/shard_map/ppermute | solution.py:27
  2.8 1.4 %collective-permute-start.5 = (bf16[1792,256]{1,0:T(8,128)(2,1)}, bf16[1792,256]{1,0:T(8,128)(2,1)S(1)}, u32[]{:S(2)}, u32[]{:S(2)}) collective-permute-start(bf16[1792,256]{1,0:T(8,128)(2,1)} %bitcast.11), channel_id=1, source_target_pairs={{0,6},{2,0},{4,2},{6,4},{8,14},{10,8},{12,10},{14,12},{16,22},{18,... | collective-permute-start | bytes 2752520 | tf_op jit(solution)/shard_map/ppermute | solution.py:27
  4.1 1.0 %copy-done.2 = bf16[1,128,1792]{2,1,0:T(8,128)(2,1)S(1)} copy-done((bf16[1,128,1792]{2,1,0:T(8,128)(2,1)S(1)}, bf16[1,128,1792]{2,1,0:T(8,128)(2,1)}, u32[]{:S(2)}) %copy-start.2) | copy-done | bytes 458776
  5.1 1.0 %copy-done.3 = bf16[1,1,128,1792]{3,2,1,0:T(8,128)(2,1)S(1)} copy-done((bf16[1,1,128,1792]{3,2,1,0:T(8,128)(2,1)S(1)}, bf16[1,1,128,1792]{3,2,1,0:T(8,128)(2,1)}, u32[]{:S(2)}) %copy-start.3) | copy-done | bytes 458776
  6.2 1.0 %copy-done.4 = bf16[1,128,1792]{2,1,0:T(8,128)(2,1)S(1)} copy-done((bf16[1,128,1792]{2,1,0:T(8,128)(2,1)S(1)}, bf16[1,128,1792]{2,1,0:T(8,128)(2,1)}, u32[]{:S(2)}) %copy-start.4) | copy-done | bytes 458776
  7.2 0.7 copy-done.5
  7.8 0.7 copy-done.6
  8.5 1.6 %shard_map.87 = (bf16[128,1792]{1,0:T(8,128)(2,1)S(1)}, bf16[128,1792]{1,0:T(8,128)(2,1)S(1)}, bf16[128,1792]{1,0:T(8,128)(2,1)S(1)}, bf16[128,1792]{1,0:T(8,128)(2,1)S(1)}) custom-call(s32[1]{0:T(128)} %bitcast.y_ref, s32[1,128]{1,0:T(1,128)S(1)} %bitcast.21, s32[1,128]{1,0:T(1,128)S(1)} %bitcast.23, bf16[128,1792]{1,0:T(8,128)(2,1)S(1)} %bitcast.18, ...), custom_call_target="tpu_custom_call" | custom-call | flops 220200960 | bytes 3211264 | tf_op jit(solution)/shard_map/pallas_call | solution.py:58
  10.1 3.1 %collective-permute-start.2 = (bf16[128,1792]{1,0:T(8,128)(2,1)S(1)}, bf16[128,1792]{1,0:T(8,128)(2,1)S(1)}, u32[]{:S(2)}, u32[]{:S(2)}) collective-permute-start(bf16[128,1792]{1,0:T(8,128)(2,1)S(1)} %get-tuple-element.29), channel_id=1, source_target_pairs={{0,16},{2,18},{4,20},{6,22},{8,24},{10,26},{12,28},{14,30},{16,0},... | collective-permute-start | bytes 1376264 | tf_op jit(solution)/shard_map/ppermute | solution.py:33
  13.2 1.6 %collective-permute-start = (s32[1,128]{1,0:T(1,128)S(1)}, s32[1,128]{1,0:T(1,128)S(1)}, u32[]{:S(2)}, u32[]{:S(2)}) collective-permute-start(s32[1,128]{1,0:T(1,128)S(1)} %bitcast.22), channel_id=1, source_target_pairs={{0,32},{32,64},{64,96},{96,128},{128,160},{160,192},{192,224},{224... | collective-permute-start | bytes 1544 | tf_op jit(solution)/shard_map/ppermute | solution.py:39
  14.9 3.9 %collective-permute-start.1 = (s32[1,128]{1,0:T(1,128)S(1)}, s32[1,128]{1,0:T(1,128)S(1)}, u32[]{:S(2)}, u32[]{:S(2)}) collective-permute-start(s32[1,128]{1,0:T(1,128)S(1)} %bitcast.24), channel_id=1, source_target_pairs={{0,224},{32,0},{64,32},{96,64},{128,96},{160,128},{192,160},{224,1... | collective-permute-start | bytes 1544 | tf_op jit(solution)/shard_map/ppermute | solution.py:39
  18.8 1.2 %collective-permute-done.ids_f = s32[1,128]{1,0:T(1,128)S(1)} collective-permute-done((s32[1,128]{1,0:T(1,128)S(1)}, s32[1,128]{1,0:T(1,128)S(1)}, u32[]{:S(2)}, u32[]{:S(2)}) %collective-permute-start) | collective-permute-done | bytes 544 | tf_op jit(solution)/shard_map/ppermute | solution.py:39
  20.0 0.0 collective-permute-start.10
  20.0 0.0 collective-permute-done.1.ids_b
  20.0 2.7 %collective-permute-start.11 = (bf16[256,1792]{1,0:T(8,128)(2,1)S(1)}, bf16[256,1792]{1,0:T(8,128)(2,1)S(1)}, u32[]{:S(2)}, u32[]{:S(2)}) collective-permute-start(bf16[256,1792]{1,0:T(8,128)(2,1)S(1)} %bitcast.15), channel_id=1, source_target_pairs={{0,6},{2,0},{4,2},{6,4},{8,14},{10,8},{12,10},{14,12},{16,22},{18,... | collective-permute-start | bytes 2752520 | tf_op jit(solution)/shard_map/ppermute | solution.py:27
  22.7 0.5 shard_map.86
  23.2 0.3 shard_map.88
  23.5 0.7 collective-permute-start.3
  24.2 0.0 collective-permute-done.4.left.refs_1_.u1
  24.2 0.1 shard_map.89
  24.3 9.8 %collective-permute-done.3.refs_0_.r1 = bf16[128,1792]{1,0:T(8,128)(2,1)S(1)} collective-permute-done((bf16[128,1792]{1,0:T(8,128)(2,1)S(1)}, bf16[128,1792]{1,0:T(8,128)(2,1)S(1)}, u32[]{:S(2)}, u32[]{:S(2)}) %collective-permute-start.3) | collective-permute-done | bytes 458784 | tf_op jit(solution)/shard_map/ppermute | solution.py:33
  34.2 0.3 shard_map.90
  34.4 0.0 copy-start
  34.4 1.5 %collective-permute-start.6 = (bf16[128,1792]{1,0:T(8,128)(2,1)S(1)}, bf16[128,1792]{1,0:T(8,128)(2,1)S(1)}, u32[]{:S(2)}, u32[]{:S(2)}) collective-permute-start(bf16[128,1792]{1,0:T(8,128)(2,1)S(1)} %shard_map.90), channel_id=1, source_target_pairs={{0,24},{2,26},{4,28},{6,30},{8,0},{10,2},{12,4},{14,6},{16,8},{18,... | collective-permute-start | bytes 1376264 | tf_op jit(solution)/shard_map/ppermute | solution.py:33
  35.9 0.0 collective-permute-start.7
  35.9 2.7 %collective-permute-start.8 = (bf16[896,256]{1,0:T(8,128)(2,1)S(1)}, bf16[896,256]{1,0:T(8,128)(2,1)S(1)}, u32[]{:S(2)}, u32[]{:S(2)}) collective-permute-start(bf16[896,256]{1,0:T(8,128)(2,1)S(1)} %get-tuple-element.32), channel_id=1, source_target_pairs={{0,6},{2,0},{4,2},{6,4},{8,14},{10,8},{12,10},{14,12},{16,22},{18,... | collective-permute-start | bytes 1376264 | tf_op jit(solution)/shard_map/ppermute | solution.py:27
  38.6 4.8 %collective-permute-done.10.left.refs_1_.v1 = bf16[256,1792]{1,0:T(8,128)(2,1)S(1)} collective-permute-done((bf16[256,1792]{1,0:T(8,128)(2,1)S(1)}, bf16[256,1792]{1,0:T(8,128)(2,1)S(1)}, u32[]{:S(2)}, u32[]{:S(2)}) %collective-permute-start.10) | collective-permute-done | bytes 917536 | tf_op jit(solution)/shard_map/ppermute | solution.py:27
  43.4 0.1 shard_map.92
  43.5 1.4 %collective-permute-start.12 = (bf16[128,1792]{1,0:T(8,128)(2,1)S(1)}, bf16[128,1792]{1,0:T(8,128)(2,1)S(1)}, u32[]{:S(2)}, u32[]{:S(2)}) collective-permute-start(bf16[128,1792]{1,0:T(8,128)(2,1)S(1)} %get-tuple-element.33.token), channel_id=1, source_target_pairs={{0,2},{2,4},{4,6},{6,0},{8,10},{10,12},{12,14},{14,8},{16,18},{18,... | collective-permute-start | bytes 1376264 | tf_op jit(solution)/shard_map/ppermute | solution.py:27
  44.9 1.3 %collective-permute-start.13 = (bf16[128,1792]{1,0:T(8,128)(2,1)S(1)}, bf16[128,1792]{1,0:T(8,128)(2,1)S(1)}, u32[]{:S(2)}, u32[]{:S(2)}) collective-permute-start(bf16[128,1792]{1,0:T(8,128)(2,1)S(1)} %get-tuple-element.34), channel_id=1, source_target_pairs={{0,6},{2,0},{4,2},{6,4},{8,14},{10,8},{12,10},{14,12},{16,22},{18,... | collective-permute-start | bytes 1376264 | tf_op jit(solution)/shard_map/ppermute | solution.py:27
  46.2 1.1 %shard_map.93.token.pu = bf16[320,768]{1,0:T(8,128)(2,1)S(1)} custom-call(bf16[128,1792]{1,0:T(8,128)(2,1)S(1)} %get-tuple-element.27.r0, bf16[128,1792]{1,0:T(8,128)(2,1)S(1)} %collective-permute-done.3.refs_0_.r1, bf16[128,1792]{1,0:T(8,128)(2,1)S(1)} %collective-permute-done.2.refs_0_.r2, bf16[128,1792]{1,0:T(8,128)(2,1)S(1)} %collective-permute-done.6.r3, ...), custom_call_target="tpu_custom_call" | custom-call | flops 880803840 | bytes 4194304 | tf_op jit(solution)/shard_map/pallas_call | solution.py:58
  47.3 4.6 %collective-permute-start.14 = (bf16[320,768]{1,0:T(8,128)(2,1)S(1)}, bf16[320,768]{1,0:T(8,128)(2,1)S(1)}, u32[]{:S(2)}, u32[]{:S(2)}) collective-permute-start(bf16[320,768]{1,0:T(8,128)(2,1)S(1)} %shard_map.93.token.pu), channel_id=1, source_target_pairs={{0,1},{1,0},{2,3},{3,2},{4,5},{5,4},{6,7},{7,6},{8,9},{9,8},{10,11... | collective-permute-start | bytes 1474568 | tf_op jit(solution)/shard_map/ppermute | solution.py:54
  51.9 1.1 %shard_map.94.pv = bf16[192,768]{1,0:T(8,128)(2,1)S(1)} custom-call(bf16[128,1792]{1,0:T(8,128)(2,1)S(1)} %get-tuple-element.27.r0, bf16[128,1792]{1,0:T(8,128)(2,1)S(1)} %collective-permute-done.3.refs_0_.r1, bf16[128,1792]{1,0:T(8,128)(2,1)S(1)} %collective-permute-done.2.refs_0_.r2, bf16[128,1792]{1,0:T(8,128)(2,1)S(1)} %collective-permute-done.6.r3, ...), custom_call_target="tpu_custom_call" | custom-call | flops 587202560 | bytes 4194304 | tf_op jit(solution)/shard_map/pallas_call | solution.py:58
  53.0 0.2 collective-permute-done.7.wa.ua
  53.2 3.2 %collective-permute-start.15 = (bf16[192,768]{1,0:T(8,128)(2,1)S(1)}, bf16[192,768]{1,0:T(8,128)(2,1)S(1)}, u32[]{:S(2)}, u32[]{:S(2)}) collective-permute-start(bf16[192,768]{1,0:T(8,128)(2,1)S(1)} %shard_map.94.pv), channel_id=1, source_target_pairs={{0,1},{1,0},{2,3},{3,2},{4,5},{5,4},{6,7},{7,6},{8,9},{9,8},{10,11... | collective-permute-start | bytes 884744 | tf_op jit(solution)/shard_map/ppermute | solution.py:54
  56.4 0.5 shard_map.91.pu
  56.9 0.7 collective-permute-start.9
  57.6 0.0 collective-permute-done.15.qv
  57.6 1.4 %shard_map.95 = (f32[160,1792]{1,0:T(8,128)S(1)}, f32[160,1792]{1,0:T(8,128)S(1)}) custom-call(bf16[128,1792]{1,0:T(8,128)(2,1)S(1)} %get-tuple-element.27.r0, bf16[128,1792]{1,0:T(8,128)(2,1)S(1)} %collective-permute-done.3.refs_0_.r1, bf16[128,1792]{1,0:T(8,128)(2,1)S(1)} %collective-permute-done.2.refs_0_.r2, ...), custom_call_target="tpu_custom_call" | custom-call | flops 880803840 | bytes 8388608 | tf_op jit(solution)/shard_map/pallas_call | solution.py:58
  59.1 4.0 %collective-permute-done.12.va = bf16[128,1792]{1,0:T(8,128)(2,1)S(1)} collective-permute-done((bf16[128,1792]{1,0:T(8,128)(2,1)S(1)}, bf16[128,1792]{1,0:T(8,128)(2,1)S(1)}, u32[]{:S(2)}, u32[]{:S(2)}) %collective-permute-start.12) | collective-permute-done | bytes 458784 | tf_op jit(solution)/shard_map/ppermute | solution.py:27
  63.1 0.6 shard_map.96
  63.7 2.1 %collective-permute-start.17 = (bf16[192,256]{1,0:T(8,128)(2,1)S(1)}, bf16[192,256]{1,0:T(8,128)(2,1)S(1)}, u32[]{:S(2)}, u32[]{:S(2)}) collective-permute-start(bf16[192,256]{1,0:T(8,128)(2,1)S(1)} %get-tuple-element.38.pv), channel_id=1, source_target_pairs={{0,1},{1,0},{2,3},{3,2},{4,5},{5,4},{6,7},{7,6},{8,9},{9,8},{10,11... | collective-permute-start | bytes 294920 | tf_op jit(solution)/shard_map/ppermute | solution.py:54
  65.8 2.7 %collective-permute-start.16 = (bf16[40,1792]{1,0:T(8,128)(2,1)S(1)}, bf16[40,1792]{1,0:T(8,128)(2,1)S(1)}, u32[]{:S(2)}, u32[]{:S(2)}) collective-permute-start(bf16[40,1792]{1,0:T(8,128)(2,1)S(1)} %get-tuple-element.37), channel_id=1, source_target_pairs={{0,40},{2,42},{4,44},{6,46},{8,48},{10,50},{12,52},{14,54},{16,56}... | collective-permute-start | bytes 430088 | tf_op jit(solution)/shard_map/ppermute | solution.py:50
  68.4 1.6 %collective-permute-start.19 = (bf16[40,1792]{1,0:T(8,128)(2,1)S(1)}, bf16[40,1792]{1,0:T(8,128)(2,1)S(1)}, u32[]{:S(2)}, u32[]{:S(2)}) collective-permute-start(bf16[40,1792]{1,0:T(8,128)(2,1)S(1)} %get-tuple-element.39.token), channel_id=1, source_target_pairs={{0,32},{2,34},{4,36},{6,38},{8,40},{10,42},{12,44},{14,46},{16,48}... | collective-permute-start | bytes 430088 | tf_op jit(solution)/shard_map/ppermute | solution.py:50
  70.1 0.5 shard_map.98
  70.5 4.7 %collective-permute-start.18 = (bf16[40,1792]{1,0:T(8,128)(2,1)S(1)}, bf16[40,1792]{1,0:T(8,128)(2,1)S(1)}, u32[]{:S(2)}, u32[]{:S(2)}) collective-permute-start(bf16[40,1792]{1,0:T(8,128)(2,1)S(1)} %get-tuple-element.40), channel_id=1, source_target_pairs={{0,248},{2,250},{4,252},{6,254},{8,224},{10,226},{12,228},{14,230}... | collective-permute-start | bytes 430088 | tf_op jit(solution)/shard_map/ppermute | solution.py:50
  75.3 0.7 collective-permute-start.20
  76.0 0.8 collective-permute-start.21
  76.8 1.0 %collective-permute-done.16.refs_0_ = bf16[40,1792]{1,0:T(8,128)(2,1)S(1)} collective-permute-done((bf16[40,1792]{1,0:T(8,128)(2,1)S(1)}, bf16[40,1792]{1,0:T(8,128)(2,1)S(1)}, u32[]{:S(2)}, u32[]{:S(2)}) %collective-permute-start.16) | collective-permute-done | bytes 143392 | tf_op jit(solution)/shard_map/ppermute | solution.py:50
  77.8 0.6 collective-permute-start.22
  78.4 0.0 collective-permute-done.19.refs_1_
  78.4 3.3 %collective-permute-start.23 = (bf16[40,1792]{1,0:T(8,128)(2,1)S(1)}, bf16[40,1792]{1,0:T(8,128)(2,1)S(1)}, u32[]{:S(2)}, u32[]{:S(2)}) collective-permute-start(bf16[40,1792]{1,0:T(8,128)(2,1)S(1)} %get-tuple-element.44), channel_id=1, source_target_pairs={{0,232},{2,234},{4,236},{6,238},{8,240},{10,242},{12,244},{14,246}... | collective-permute-start | bytes 430088 | tf_op jit(solution)/shard_map/ppermute | solution.py:50
  81.8 1.7 %collective-permute-start.24 = (bf16[40,1792]{1,0:T(8,128)(2,1)S(1)}, bf16[40,1792]{1,0:T(8,128)(2,1)S(1)}, u32[]{:S(2)}, u32[]{:S(2)}) collective-permute-start(bf16[40,1792]{1,0:T(8,128)(2,1)S(1)} %get-tuple-element.45), channel_id=1, source_target_pairs={{0,240},{2,242},{4,244},{6,246},{8,248},{10,250},{12,252},{14,254}... | collective-permute-start | bytes 430088 | tf_op jit(solution)/shard_map/ppermute | solution.py:50
  83.5 0.2 shard_map.97.token.refs_0_
  83.7 0.2 shard_map.99.token.refs_0_
  84.0 0.3 shard_map.100.token.refs_0_
  84.2 0.2 shard_map.101.token.refs_0_
  84.5 0.3 shard_map.102.token.refs_0_
  84.8 1.0 %collective-permute-done.22.refs_1_ = bf16[40,1792]{1,0:T(8,128)(2,1)S(1)} collective-permute-done((bf16[40,1792]{1,0:T(8,128)(2,1)S(1)}, bf16[40,1792]{1,0:T(8,128)(2,1)S(1)}, u32[]{:S(2)}, u32[]{:S(2)}) %collective-permute-start.22) | collective-permute-done | bytes 143392 | tf_op jit(solution)/shard_map/ppermute | solution.py:50
  85.7 0.2 shard_map.103.token.total_f
  86.0 0.1 collective-permute-done.23.refs_1_
  86.1 0.2 shard_map.104.total_b
  86.3 4.3 %collective-permute-done.24.row = bf16[40,1792]{1,0:T(8,128)(2,1)S(1)} collective-permute-done((bf16[40,1792]{1,0:T(8,128)(2,1)S(1)}, bf16[40,1792]{1,0:T(8,128)(2,1)S(1)}, u32[]{:S(2)}, u32[]{:S(2)}) %collective-permute-start.24) | collective-permute-done | bytes 143392 | tf_op jit(solution)/shard_map/ppermute | solution.py:50
  90.6 1.0 %shard_map.105 = (bf16[128,1792]{1,0:T(8,128)(2,1)}, bf16[128,1792]{1,0:T(8,128)(2,1)}) custom-call(bf16[4,128,40]{2,1,0:T(8,128)(2,1)S(1)} %get-tuple-element.25.token.table, f32[128,1792]{1,0:T(8,128)S(1)} %shard_map.103.token.total_f, f32[128,1792]{1,0:T(8,128)S(1)} %shard_map.104.total_b, bf16[40,1792]{1,0:T(8,128)(2,1)S(1)} %collective-permute-done.24.row), custom_call_target="tpu_custom_call" | custom-call | flops 18350080 | bytes 2752512 | tf_op jit(solution)/shard_map/pallas_call | solution.py:58
  (20 shorter events, 0.0 us)
Async XLA Ops:
  0.6 19.4 %copy-start.1 = (bf16[1,1,256,1792]{3,2,1,0:T(8,128)(2,1)S(1)}, bf16[1,1,256,1792]{3,2,1,0:T(8,128)(2,1)}, u32[]{:S(2)}) copy-start(bf16[1,1,256,1792]{3,2,1,0:T(8,128)(2,1)} %param.13) | copy-start | bytes 2752516
  0.6 23.6 %collective-permute-start.4 = (bf16[1792,256]{1,0:T(8,128)(2,1)}, bf16[1792,256]{1,0:T(8,128)(2,1)S(1)}, u32[]{:S(2)}, u32[]{:S(2)}) collective-permute-start(bf16[1792,256]{1,0:T(8,128)(2,1)} %bitcast.10), channel_id=1, source_target_pairs={{0,2},{2,4},{4,6},{6,0},{8,10},{10,12},{12,14},{14,8},{16,18},{18,... | collective-permute-start | bytes 2752520 | tf_op jit(solution)/shard_map/ppermute | solution.py:27
  2.8 21.5 %collective-permute-start.5 = (bf16[1792,256]{1,0:T(8,128)(2,1)}, bf16[1792,256]{1,0:T(8,128)(2,1)S(1)}, u32[]{:S(2)}, u32[]{:S(2)}) collective-permute-start(bf16[1792,256]{1,0:T(8,128)(2,1)} %bitcast.11), channel_id=1, source_target_pairs={{0,6},{2,0},{4,2},{6,4},{8,14},{10,8},{12,10},{14,12},{16,22},{18,... | collective-permute-start | bytes 2752520 | tf_op jit(solution)/shard_map/ppermute | solution.py:27
  4.1 1.0 %copy-start.2 = (bf16[1,128,1792]{2,1,0:T(8,128)(2,1)S(1)}, bf16[1,128,1792]{2,1,0:T(8,128)(2,1)}, u32[]{:S(2)}) copy-start(bf16[1,128,1792]{2,1,0:T(8,128)(2,1)} %param.7) | copy-start | bytes 1376260
  5.1 1.0 %copy-start.3 = (bf16[1,1,128,1792]{3,2,1,0:T(8,128)(2,1)S(1)}, bf16[1,1,128,1792]{3,2,1,0:T(8,128)(2,1)}, u32[]{:S(2)}) copy-start(bf16[1,1,128,1792]{3,2,1,0:T(8,128)(2,1)} %param.10) | copy-start | bytes 1376260
  6.2 1.0 %copy-start.4 = (bf16[1,128,1792]{2,1,0:T(8,128)(2,1)S(1)}, bf16[1,128,1792]{2,1,0:T(8,128)(2,1)}, u32[]{:S(2)}) copy-start(bf16[1,128,1792]{2,1,0:T(8,128)(2,1)} %param.9) | copy-start | bytes 1376260
  7.2 0.7 copy-start.5
  7.8 0.7 copy-start.6
  10.1 13.1 %collective-permute-start.2 = (bf16[128,1792]{1,0:T(8,128)(2,1)S(1)}, bf16[128,1792]{1,0:T(8,128)(2,1)S(1)}, u32[]{:S(2)}, u32[]{:S(2)}) collective-permute-start(bf16[128,1792]{1,0:T(8,128)(2,1)S(1)} %get-tuple-element.29), channel_id=1, source_target_pairs={{0,16},{2,18},{4,20},{6,22},{8,24},{10,26},{12,28},{14,30},{16,0},... | collective-permute-start | bytes 1376264 | tf_op jit(solution)/shard_map/ppermute | solution.py:33
  13.2 6.8 %collective-permute-start = (s32[1,128]{1,0:T(1,128)S(1)}, s32[1,128]{1,0:T(1,128)S(1)}, u32[]{:S(2)}, u32[]{:S(2)}) collective-permute-start(s32[1,128]{1,0:T(1,128)S(1)} %bitcast.22), channel_id=1, source_target_pairs={{0,32},{32,64},{64,96},{96,128},{128,160},{160,192},{192,224},{224... | collective-permute-start | bytes 1544 | tf_op jit(solution)/shard_map/ppermute | solution.py:39
  14.9 5.2 %collective-permute-start.1 = (s32[1,128]{1,0:T(1,128)S(1)}, s32[1,128]{1,0:T(1,128)S(1)}, u32[]{:S(2)}, u32[]{:S(2)}) collective-permute-start(s32[1,128]{1,0:T(1,128)S(1)} %bitcast.24), channel_id=1, source_target_pairs={{0,224},{32,0},{64,32},{96,64},{128,96},{160,128},{192,160},{224,1... | collective-permute-start | bytes 1544 | tf_op jit(solution)/shard_map/ppermute | solution.py:39
  20.0 23.4 %collective-permute-start.10 = (bf16[256,1792]{1,0:T(8,128)(2,1)S(1)}, bf16[256,1792]{1,0:T(8,128)(2,1)S(1)}, u32[]{:S(2)}, u32[]{:S(2)}) collective-permute-start(bf16[256,1792]{1,0:T(8,128)(2,1)S(1)} %bitcast.14), channel_id=1, source_target_pairs={{0,2},{2,4},{4,6},{6,0},{8,10},{10,12},{12,14},{14,8},{16,18},{18,... | collective-permute-start | bytes 2752520 | tf_op jit(solution)/shard_map/ppermute | solution.py:27
  20.0 23.4 %collective-permute-start.11 = (bf16[256,1792]{1,0:T(8,128)(2,1)S(1)}, bf16[256,1792]{1,0:T(8,128)(2,1)S(1)}, u32[]{:S(2)}, u32[]{:S(2)}) collective-permute-start(bf16[256,1792]{1,0:T(8,128)(2,1)S(1)} %bitcast.15), channel_id=1, source_target_pairs={{0,6},{2,0},{4,2},{6,4},{8,14},{10,8},{12,10},{14,12},{16,22},{18,... | collective-permute-start | bytes 2752520 | tf_op jit(solution)/shard_map/ppermute | solution.py:27
  23.5 10.7 %collective-permute-start.3 = (bf16[128,1792]{1,0:T(8,128)(2,1)S(1)}, bf16[128,1792]{1,0:T(8,128)(2,1)S(1)}, u32[]{:S(2)}, u32[]{:S(2)}) collective-permute-start(bf16[128,1792]{1,0:T(8,128)(2,1)S(1)} %shard_map.88), channel_id=1, source_target_pairs={{0,8},{2,10},{4,12},{6,14},{8,16},{10,18},{12,20},{14,22},{16,24},... | collective-permute-start | bytes 1376264 | tf_op jit(solution)/shard_map/ppermute | solution.py:33
  34.4 11.8 %copy-start = (bf16[1,1,1792,256]{3,2,1,0:T(8,128)(2,1)S(1)}, bf16[1,1,1792,256]{3,2,1,0:T(8,128)(2,1)}, u32[]{:S(2)}) copy-start(bf16[1,1,1792,256]{3,2,1,0:T(8,128)(2,1)} %param.12) | copy-start | bytes 2752516
  34.4 11.8 %collective-permute-start.6 = (bf16[128,1792]{1,0:T(8,128)(2,1)S(1)}, bf16[128,1792]{1,0:T(8,128)(2,1)S(1)}, u32[]{:S(2)}, u32[]{:S(2)}) collective-permute-start(bf16[128,1792]{1,0:T(8,128)(2,1)S(1)} %shard_map.90), channel_id=1, source_target_pairs={{0,24},{2,26},{4,28},{6,30},{8,0},{10,2},{12,4},{14,6},{16,8},{18,... | collective-permute-start | bytes 1376264 | tf_op jit(solution)/shard_map/ppermute | solution.py:33
  35.9 17.3 %collective-permute-start.7 = (bf16[896,256]{1,0:T(8,128)(2,1)S(1)}, bf16[896,256]{1,0:T(8,128)(2,1)S(1)}, u32[]{:S(2)}, u32[]{:S(2)}) collective-permute-start(bf16[896,256]{1,0:T(8,128)(2,1)S(1)} %get-tuple-element.31.refs_1_), channel_id=1, source_target_pairs={{0,2},{2,4},{4,6},{6,0},{8,10},{10,12},{12,14},{14,8},{16,18},{18,... | collective-permute-start | bytes 1376264 | tf_op jit(solution)/shard_map/ppermute | solution.py:27
  35.9 20.5 %collective-permute-start.8 = (bf16[896,256]{1,0:T(8,128)(2,1)S(1)}, bf16[896,256]{1,0:T(8,128)(2,1)S(1)}, u32[]{:S(2)}, u32[]{:S(2)}) collective-permute-start(bf16[896,256]{1,0:T(8,128)(2,1)S(1)} %get-tuple-element.32), channel_id=1, source_target_pairs={{0,6},{2,0},{4,2},{6,4},{8,14},{10,8},{12,10},{14,12},{16,22},{18,... | collective-permute-start | bytes 1376264 | tf_op jit(solution)/shard_map/ppermute | solution.py:27
  43.5 19.6 %collective-permute-start.12 = (bf16[128,1792]{1,0:T(8,128)(2,1)S(1)}, bf16[128,1792]{1,0:T(8,128)(2,1)S(1)}, u32[]{:S(2)}, u32[]{:S(2)}) collective-permute-start(bf16[128,1792]{1,0:T(8,128)(2,1)S(1)} %get-tuple-element.33.token), channel_id=1, source_target_pairs={{0,2},{2,4},{4,6},{6,0},{8,10},{10,12},{12,14},{14,8},{16,18},{18,... | collective-permute-start | bytes 1376264 | tf_op jit(solution)/shard_map/ppermute | solution.py:27
  44.9 18.2 %collective-permute-start.13 = (bf16[128,1792]{1,0:T(8,128)(2,1)S(1)}, bf16[128,1792]{1,0:T(8,128)(2,1)S(1)}, u32[]{:S(2)}, u32[]{:S(2)}) collective-permute-start(bf16[128,1792]{1,0:T(8,128)(2,1)S(1)} %get-tuple-element.34), channel_id=1, source_target_pairs={{0,6},{2,0},{4,2},{6,4},{8,14},{10,8},{12,10},{14,12},{16,22},{18,... | collective-permute-start | bytes 1376264 | tf_op jit(solution)/shard_map/ppermute | solution.py:27
  47.3 10.3 %collective-permute-start.14 = (bf16[320,768]{1,0:T(8,128)(2,1)S(1)}, bf16[320,768]{1,0:T(8,128)(2,1)S(1)}, u32[]{:S(2)}, u32[]{:S(2)}) collective-permute-start(bf16[320,768]{1,0:T(8,128)(2,1)S(1)} %shard_map.93.token.pu), channel_id=1, source_target_pairs={{0,1},{1,0},{2,3},{3,2},{4,5},{5,4},{6,7},{7,6},{8,9},{9,8},{10,11... | collective-permute-start | bytes 1474568 | tf_op jit(solution)/shard_map/ppermute | solution.py:54
  53.2 4.4 %collective-permute-start.15 = (bf16[192,768]{1,0:T(8,128)(2,1)S(1)}, bf16[192,768]{1,0:T(8,128)(2,1)S(1)}, u32[]{:S(2)}, u32[]{:S(2)}) collective-permute-start(bf16[192,768]{1,0:T(8,128)(2,1)S(1)} %shard_map.94.pv), channel_id=1, source_target_pairs={{0,1},{1,0},{2,3},{3,2},{4,5},{5,4},{6,7},{7,6},{8,9},{9,8},{10,11... | collective-permute-start | bytes 884744 | tf_op jit(solution)/shard_map/ppermute | solution.py:54
  56.9 6.1 %collective-permute-start.9 = (bf16[320,256]{1,0:T(8,128)(2,1)S(1)}, bf16[320,256]{1,0:T(8,128)(2,1)S(1)}, u32[]{:S(2)}, u32[]{:S(2)}) collective-permute-start(bf16[320,256]{1,0:T(8,128)(2,1)S(1)} %shard_map.91.pu), channel_id=1, source_target_pairs={{0,1},{1,0},{2,3},{3,2},{4,5},{5,4},{6,7},{7,6},{8,9},{9,8},{10,11... | collective-permute-start | bytes 491528 | tf_op jit(solution)/shard_map/ppermute | solution.py:54
  63.7 6.4 %collective-permute-start.17 = (bf16[192,256]{1,0:T(8,128)(2,1)S(1)}, bf16[192,256]{1,0:T(8,128)(2,1)S(1)}, u32[]{:S(2)}, u32[]{:S(2)}) collective-permute-start(bf16[192,256]{1,0:T(8,128)(2,1)S(1)} %get-tuple-element.38.pv), channel_id=1, source_target_pairs={{0,1},{1,0},{2,3},{3,2},{4,5},{5,4},{6,7},{7,6},{8,9},{9,8},{10,11... | collective-permute-start | bytes 294920 | tf_op jit(solution)/shard_map/ppermute | solution.py:54
  65.8 12.1 %collective-permute-start.16 = (bf16[40,1792]{1,0:T(8,128)(2,1)S(1)}, bf16[40,1792]{1,0:T(8,128)(2,1)S(1)}, u32[]{:S(2)}, u32[]{:S(2)}) collective-permute-start(bf16[40,1792]{1,0:T(8,128)(2,1)S(1)} %get-tuple-element.37), channel_id=1, source_target_pairs={{0,40},{2,42},{4,44},{6,46},{8,48},{10,50},{12,52},{14,54},{16,56}... | collective-permute-start | bytes 430088 | tf_op jit(solution)/shard_map/ppermute | solution.py:50
  68.4 10.0 %collective-permute-start.19 = (bf16[40,1792]{1,0:T(8,128)(2,1)S(1)}, bf16[40,1792]{1,0:T(8,128)(2,1)S(1)}, u32[]{:S(2)}, u32[]{:S(2)}) collective-permute-start(bf16[40,1792]{1,0:T(8,128)(2,1)S(1)} %get-tuple-element.39.token), channel_id=1, source_target_pairs={{0,32},{2,34},{4,36},{6,38},{8,40},{10,42},{12,44},{14,46},{16,48}... | collective-permute-start | bytes 430088 | tf_op jit(solution)/shard_map/ppermute | solution.py:50
  70.5 11.2 %collective-permute-start.18 = (bf16[40,1792]{1,0:T(8,128)(2,1)S(1)}, bf16[40,1792]{1,0:T(8,128)(2,1)S(1)}, u32[]{:S(2)}, u32[]{:S(2)}) collective-permute-start(bf16[40,1792]{1,0:T(8,128)(2,1)S(1)} %get-tuple-element.40), channel_id=1, source_target_pairs={{0,248},{2,250},{4,252},{6,254},{8,224},{10,226},{12,228},{14,230}... | collective-permute-start | bytes 430088 | tf_op jit(solution)/shard_map/ppermute | solution.py:50
  75.3 9.0 %collective-permute-start.20 = (bf16[40,1792]{1,0:T(8,128)(2,1)S(1)}, bf16[40,1792]{1,0:T(8,128)(2,1)S(1)}, u32[]{:S(2)}, u32[]{:S(2)}) collective-permute-start(bf16[40,1792]{1,0:T(8,128)(2,1)S(1)} %get-tuple-element.41), channel_id=1, source_target_pairs={{0,224},{2,226},{4,228},{6,230},{8,232},{10,234},{12,236},{14,238}... | collective-permute-start | bytes 430088 | tf_op jit(solution)/shard_map/ppermute | solution.py:50
  76.0 8.5 %collective-permute-start.21 = (bf16[40,1792]{1,0:T(8,128)(2,1)S(1)}, bf16[40,1792]{1,0:T(8,128)(2,1)S(1)}, u32[]{:S(2)}, u32[]{:S(2)}) collective-permute-start(bf16[40,1792]{1,0:T(8,128)(2,1)S(1)} %get-tuple-element.42), channel_id=1, source_target_pairs={{0,48},{2,50},{4,52},{6,54},{8,56},{10,58},{12,60},{14,62},{16,32}... | collective-permute-start | bytes 430088 | tf_op jit(solution)/shard_map/ppermute | solution.py:50
  77.8 7.9 %collective-permute-start.22 = (bf16[40,1792]{1,0:T(8,128)(2,1)S(1)}, bf16[40,1792]{1,0:T(8,128)(2,1)S(1)}, u32[]{:S(2)}, u32[]{:S(2)}) collective-permute-start(bf16[40,1792]{1,0:T(8,128)(2,1)S(1)} %get-tuple-element.43), channel_id=1, source_target_pairs={{0,56},{2,58},{4,60},{6,62},{8,32},{10,34},{12,36},{14,38},{16,40}... | collective-permute-start | bytes 430088 | tf_op jit(solution)/shard_map/ppermute | solution.py:50
  78.4 7.6 %collective-permute-start.23 = (bf16[40,1792]{1,0:T(8,128)(2,1)S(1)}, bf16[40,1792]{1,0:T(8,128)(2,1)S(1)}, u32[]{:S(2)}, u32[]{:S(2)}) collective-permute-start(bf16[40,1792]{1,0:T(8,128)(2,1)S(1)} %get-tuple-element.44), channel_id=1, source_target_pairs={{0,232},{2,234},{4,236},{6,238},{8,240},{10,242},{12,244},{14,246}... | collective-permute-start | bytes 430088 | tf_op jit(solution)/shard_map/ppermute | solution.py:50
  81.8 8.9 %collective-permute-start.24 = (bf16[40,1792]{1,0:T(8,128)(2,1)S(1)}, bf16[40,1792]{1,0:T(8,128)(2,1)S(1)}, u32[]{:S(2)}, u32[]{:S(2)}) collective-permute-start(bf16[40,1792]{1,0:T(8,128)(2,1)S(1)} %get-tuple-element.45), channel_id=1, source_target_pairs={{0,240},{2,242},{4,244},{6,246},{8,248},{10,250},{12,252},{14,254}... | collective-permute-start | bytes 430088 | tf_op jit(solution)/shard_map/ppermute | solution.py:50
